TPU v7x, 32 devices: a whole 2x2x4 slice. The times are simulated.
32 devices in a mesh: row: 8 (over z, y), col: 4 (over x, core).
Axes of the slice: x: 2, y: 2, z: 4, core: 2. Of those that a mesh axis runs over, the one named last changes fastest.
Arguments:
- left_blocks: float32 [8, 8, 4, 4096], P('row', 'col'), may hold values from -0.75 to 0.75
- right_blocks: float32 [8, 4, 20, 4096], P('row', 'col'), may hold values from -6 to 6
- left_slots: int32 [8, 4, 4, 2, 24], P('row', 'col'), may hold values from 0 to 3
- right_slots: int32 [8, 4, 4, 2, 24], P('row', 'col'), may hold values from 0 to 19
- sink_slots: int32 [8, 4, 4, 2, 24], P('row', 'col'), may hold values from 0 to 11
- live_counts: int32 [8, 4, 4, 2], P('row', 'col'), may hold values from 3 to 24, as said below
Outputs:
- product_blocks: float32 [8, 4, 12, 4096], P('row', 'col')
Inputs may be any that keep to these rules, and one draw needn't show every extreme that they name: `live_counts`: entries of a list at positions from its live count on are not read; at least one list in every draw is full.
All inputs are finite; a program needn't handle non-finite values.
Results may differ from a plain program's by a relative error of at most 0.0003.
Values sent between devices are 32-bit elements; how exact they have to be, the bound alone decides.
No kernel may reach another device: no remote copies, remote signals or barrier semaphores. Data moves between devices by JAX's collectives and lax.ppermute only.
A program may use at most 64 MiB of HBM per device.

v0:
```python
import jax
import jax.numpy as jnp
from jax import lax
from jax.sharding import PartitionSpec as P

TILE_SIDE = 64
SINK_SLOTS = 12
PRODUCTS = 24
SECTIONS = 4


def shifted_2(shard, axis, by):
    devices = lax.axis_size(axis)
    return lax.ppermute(shard, axis, [(i, (i + by) % devices) for i in range(devices)])


def partner_2(value, axis, apart):
    mask = 2**apart
    pairs = [(source, source ^ mask) for source in range(lax.axis_size(axis))]
    return lax.ppermute(value, axis, pairs)


def block_terms(running, left_panel, right_panel, left_index, right_index, sink_index, live_count):
    is_live = (jnp.arange(PRODUCTS) < live_count).astype(jnp.float32)
    left_tiles = jnp.take(left_panel, left_index, axis=0).reshape(PRODUCTS, TILE_SIDE, TILE_SIDE)
    right_tiles = jnp.take(right_panel, right_index, axis=0).reshape(PRODUCTS, TILE_SIDE, TILE_SIDE)
    products = jnp.einsum("pik,pkj->pij", left_tiles, right_tiles, precision=lax.Precision.HIGHEST)
    products = products.reshape(PRODUCTS, TILE_SIDE * TILE_SIDE)
    sink_table = (jnp.arange(SINK_SLOTS)[:, None] == sink_index[None, :]).astype(
        jnp.float32
    ) * is_live[None, :]
    return running + jnp.dot(
        sink_table, products, precision=lax.Precision.HIGHEST, preferred_element_type=jnp.float32
    )


def order_pair(own_panel, partner, parity):
    first_half = jnp.where(parity == 0, own_panel, partner)
    second_half = jnp.where(parity == 0, partner, own_panel)
    return jnp.stack([first_half, second_half])


def per_device(left_blocks, right_blocks, left_slots, right_slots, sink_slots, live_counts):
    col_count = lax.axis_size("col")
    col_bits = col_count.bit_length() - 1
    half_row = lax.axis_index("row") // 2
    parity = lax.axis_index("row") % 2
    column = lax.axis_index("col")
    left_lists = left_slots[0, 0]
    right_lists = right_slots[0, 0]
    sink_lists = sink_slots[0, 0]
    count_lists = live_counts[0, 0]
    own_panel = right_blocks[0, 0]
    for bit_no in range(col_bits):
        shifted = shifted_2(own_panel, "row", -(2 << bit_no))
        own_panel = jnp.where(column // (1 << bit_no) % 2 == 1, shifted, own_panel)
    right_pairs = []
    for section_no in range(SECTIONS):
        partner = partner_2(own_panel, "row", 0)
        right_pairs.append(order_pair(own_panel, partner, parity))
        if section_no + 1 < SECTIONS:
            own_panel = shifted_2(own_panel, "row", -2)
    running = jnp.zeros((SINK_SLOTS, TILE_SIDE * TILE_SIDE), jnp.float32)
    left_pair = left_blocks[0]
    for bit_no in range(col_bits):
        shifted = shifted_2(left_pair, "col", -(1 << bit_no))
        left_pair = jnp.where(half_row // (1 << bit_no) % 2 == 1, shifted, left_pair)
    for section_no in range(SECTIONS):
        for half_no in range(2):
            running = block_terms(
                running,
                left_pair[half_no],
                right_pairs[section_no][half_no],
                left_lists[section_no, half_no],
                right_lists[section_no, half_no],
                sink_lists[section_no, half_no],
                count_lists[section_no, half_no],
            )
        if section_no + 1 < SECTIONS:
            left_pair = shifted_2(left_pair, "col", -1)
    return running[None, None]


def solution(mesh):
    return jax.shard_map(
        per_device,
        mesh=mesh,
        in_specs=(
            P("row", "col", None, None),
            P("row", "col", None, None),
            P("row", "col", None, None, None),
            P("row", "col", None, None, None),
            P("row", "col", None, None, None),
            P("row", "col", None, None),
        ),
        out_specs=P("row", "col", None, None),
        check_vma=False,
    )
```

profile of v0, /device:TPU:0, one launch (start us, length us, event | category | flops | bytes accessed | tf_op | source)
XLA Modules:
  0.0 150.5 jit_solution(3275519678079688870)
XLA Ops:
  0.0 2.4 %collective-permute-start = (f32[2,4,4096]{2,1,0:T(4,128)}, f32[2,4,4096]{2,1,0:T(4,128)S(1)}, u32[]{:S(2)}, u32[]{:S(2)}) collective-permute-start(f32[2,4,4096]{2,1,0:T(4,128)} %bitcast.164), channel_id=1, source_target_pairs={{0,3},{1,0},{2,1},{3,2},{4,7},{5,4},{6,5},{7,6},{8,11},{9,8},{10,9... | collective-permute-start | bytes 393224 | tf_op jit(solution)/shard_map/ppermute | solution.py:14
  2.4 1.2 copy.12
  3.6 3.7 %collective-permute-start.2 = (f32[20,4096]{1,0:T(8,128)S(1)}, f32[20,4096]{1,0:T(8,128)S(1)}, u32[]{:S(2)}, u32[]{:S(2)}) collective-permute-start(f32[20,4096]{1,0:T(8,128)S(1)} %bitcast.163), channel_id=1, source_target_pairs={{0,24},{4,28},{8,0},{12,4},{16,8},{20,12},{24,16},{28,20},{1,25},{... | collective-permute-start | bytes 983048 | tf_op jit(solution)/shard_map/ppermute | solution.py:14
  9.9 1.2 compare_convert_fusion.7
  15.8 1.2 compare_convert_fusion.3
  17.1 1.3 compare_convert_fusion.2
  21.9 2.7 %collective-permute-done.1 = f32[2,4,4096]{2,1,0:T(4,128)S(1)} collective-permute-done((f32[2,4,4096]{2,1,0:T(4,128)S(1)}, f32[2,4,4096]{2,1,0:T(4,128)S(1)}, u32[]{:S(2)}, u32[]{:S(2)}) %collective-permute-start.1) | collective-permute-done | bytes 131104 | tf_op jit(solution)/shard_map/ppermute | solution.py:14
  26.4 1.2 reshape.130
  33.0 1.2 reshape.139
  35.7 1.3 reshape.142
  37.2 2.2 %collective-permute-start.11 = (f32[2,4,4096]{2,1,0:T(4,128)S(1)}, f32[2,4,4096]{2,1,0:T(4,128)S(1)}, u32[]{:S(2)}, u32[]{:S(2)}) collective-permute-start(f32[2,4,4096]{2,1,0:T(4,128)S(1)} %collective-permute-done.8), channel_id=1, source_target_pairs={{0,3},{1,0},{2,1},{3,2},{4,7},{5,4},{6,5},{7,6},{8,11},{9,8},{10,9... | collective-permute-start | bytes 393224 | tf_op jit(solution)/shard_map/ppermute | solution.py:14
  39.4 8.2 %collective-permute-done.3 = f32[20,4096]{1,0:T(8,128)S(1)} collective-permute-done((f32[20,4096]{1,0:T(8,128)S(1)}, f32[20,4096]{1,0:T(8,128)S(1)}, u32[]{:S(2)}, u32[]{:S(2)}) %collective-permute-start.3) | collective-permute-done | bytes 327712 | tf_op jit(solution)/shard_map/ppermute | solution.py:14
  48.4 1.5 %collective-permute-start.4 = (f32[20,4096]{1,0:T(8,128)}, f32[20,4096]{1,0:T(8,128)S(1)}, u32[]{:S(2)}, u32[]{:S(2)}) collective-permute-start(f32[20,4096]{1,0:T(8,128)} %broadcast_select_fusion.17), channel_id=1, source_target_pairs={{0,4},{4,0},{8,12},{12,8},{16,20},{20,16},{24,28},{28,24},{1,5},{5... | collective-permute-start | bytes 983048 | tf_op jit(solution)/shard_map/ppermute | solution.py:20
  49.9 2.6 %collective-permute-start.6 = (f32[20,4096]{1,0:T(8,128)}, f32[20,4096]{1,0:T(8,128)}, u32[]{:S(2)}, u32[]{:S(2)}) collective-permute-start(f32[20,4096]{1,0:T(8,128)} %broadcast_select_fusion.17), channel_id=1, source_target_pairs={{0,24},{4,28},{8,0},{12,4},{16,8},{20,12},{24,16},{28,20},{1,25},{... | collective-permute-start | bytes 983048 | tf_op jit(solution)/shard_map/ppermute | solution.py:14
  54.6 5.1 %collective-permute-done.4 = f32[20,4096]{1,0:T(8,128)S(1)} collective-permute-done((f32[20,4096]{1,0:T(8,128)}, f32[20,4096]{1,0:T(8,128)S(1)}, u32[]{:S(2)}, u32[]{:S(2)}) %collective-permute-start.4) | collective-permute-done | bytes 327712 | tf_op jit(solution)/shard_map/ppermute | solution.py:20
  60.7 1.5 %gather_fusion.3 = f32[24,4096]{1,0:T(8,128)} fusion(f32[20,4096]{1,0:T(8,128)S(1)} %get-tuple-element.45, s32[1024]{0:T(1024)} %pad_clamp_fusion.12), kind=kCustom, calls=%fused_computation.9.clone | custom fusion | bytes 786528 | tf_op jit(solution)/shard_map/jit(_take)/gather | solution.py:26
  62.2 1.7 %gather_fusion.1 = f32[24,4096]{1,0:T(8,128)} fusion(f32[20,4096]{1,0:T(8,128)S(1)} %get-tuple-element.46, s32[1024]{0:T(1024)} %pad_clamp_fusion.14), kind=kCustom, calls=%fused_computation.1.clone | custom fusion | bytes 786528 | tf_op jit(solution)/shard_map/jit(_take)/gather | solution.py:26
  64.6 1.9 %broadcast_select_fusion.12 = (f32[24,4096]{1,0:T(8,128)}, f32[24,4096]{1,0:T(8,128)S(1)}) fusion(f32[24,4096]{1,0:T(8,128)S(1)} %copy-done.8, pred[24]{0:T(512)(128)(4,1)S(1)} %copy-done.34, f32[24,4096]{1,0:T(8,128)} %gather_fusion.1, pred[24]{0:T(512)(128)(4,1)S(1)} %copy-done.35), kind=kLoop, calls=%fused_computation.37 | loop fusion | flops 196608 | bytes 1572912 | tf_op jit(solution)/shard_map/jit(_take)/select_n | solution.py:26
  66.4 1.2 reshape.131
  67.7 2.9 %fusion.43 = f32[24,64,64]{2,1,0:T(8,128)} fusion(f32[24,64,64]{2,1,0:T(8,128)S(1)} %copy-done.4, f32[24,64,64]{2,1,0:T(8,128)} %reshape.131), kind=kOutput, calls=%fused_computation.191 | convolution fusion | flops 75497472 | bytes 1179648 | tf_op jit(solution)/shard_map/pik,pkj->pij/dot_general | solution.py:27
  70.6 1.4 reshape.132
  72.0 2.3 %reshape.134 = f32[24,64,64]{2,1,0:T(8,128)} reshape(f32[24,4096]{1,0:T(8,128)} %get-tuple-element.113) | data formatting | bytes 786432 | tf_op jit(solution)/shard_map/reshape | solution.py:26
  74.3 2.9 %fusion.44 = f32[24,64,64]{2,1,0:T(8,128)} fusion(f32[24,64,64]{2,1,0:T(8,128)S(1)} %copy-done.3, f32[24,64,64]{2,1,0:T(8,128)} %reshape.134), kind=kOutput, calls=%fused_computation.192 | convolution fusion | flops 75497472 | bytes 1179648 | tf_op jit(solution)/shard_map/pik,pkj->pij/dot_general | solution.py:27
  77.2 1.6 %collective-permute-start.7 = (f32[20,4096]{1,0:T(8,128)}, f32[20,4096]{1,0:T(8,128)}, u32[]{:S(2)}, u32[]{:S(2)}) collective-permute-start(f32[20,4096]{1,0:T(8,128)} %collective-permute-done.6), channel_id=1, source_target_pairs={{0,4},{4,0},{8,12},{12,8},{16,20},{20,16},{24,28},{28,24},{1,5},{5... | collective-permute-start | bytes 983048 | tf_op jit(solution)/shard_map/ppermute | solution.py:20
  79.2 1.4 reshape.135
  80.6 2.2 %collective-permute-start.9 = (f32[20,4096]{1,0:T(8,128)}, f32[20,4096]{1,0:T(8,128)}, u32[]{:S(2)}, u32[]{:S(2)}) collective-permute-start(f32[20,4096]{1,0:T(8,128)} %collective-permute-done.6), channel_id=1, source_target_pairs={{0,24},{4,28},{8,0},{12,4},{16,8},{20,12},{24,16},{28,20},{1,25},{... | collective-permute-start | bytes 983048 | tf_op jit(solution)/shard_map/ppermute | solution.py:14
  83.9 4.0 %collective-permute-done.7 = f32[20,4096]{1,0:T(8,128)} collective-permute-done((f32[20,4096]{1,0:T(8,128)}, f32[20,4096]{1,0:T(8,128)}, u32[]{:S(2)}, u32[]{:S(2)}) %collective-permute-start.7) | collective-permute-done | bytes 327712 | tf_op jit(solution)/shard_map/ppermute | solution.py:20
  89.1 1.5 %gather_fusion.7 = f32[24,4096]{1,0:T(8,128)} fusion(f32[20,4096]{1,0:T(8,128)S(1)} %get-tuple-element.43, s32[1024]{0:T(1024)} %pad_clamp_fusion.8), kind=kCustom, calls=%fused_computation.11.clone | custom fusion | bytes 786528 | tf_op jit(solution)/shard_map/jit(_take)/gather | solution.py:26
  90.6 1.4 gather_fusion.5
  92.7 1.9 %broadcast_select_fusion.8 = (f32[24,4096]{1,0:T(8,128)}, f32[24,4096]{1,0:T(8,128)S(1)}) fusion(f32[24,4096]{1,0:T(8,128)S(1)} %copy-done.9, pred[24]{0:T(512)(128)(4,1)S(1)} %copy-done.30, f32[24,4096]{1,0:T(8,128)} %gather_fusion.5, pred[24]{0:T(512)(128)(4,1)S(1)} %copy-done.31), kind=kLoop, calls=%fused_computation.33 | loop fusion | flops 196608 | bytes 1572912 | tf_op jit(solution)/shard_map/jit(_take)/select_n | solution.py:26
  95.8 2.9 %fusion.45 = f32[24,64,64]{2,1,0:T(8,128)} fusion(f32[24,64,64]{2,1,0:T(8,128)S(1)} %copy-done.2, f32[24,64,64]{2,1,0:T(8,128)} %reshape.137), kind=kOutput, calls=%fused_computation.193 | convolution fusion | flops 75497472 | bytes 1179648 | tf_op jit(solution)/shard_map/pik,pkj->pij/dot_general | solution.py:27
  98.7 1.4 reshape.138
  100.1 2.3 %reshape.140 = f32[24,64,64]{2,1,0:T(8,128)} reshape(f32[24,4096]{1,0:T(8,128)} %get-tuple-element.111) | data formatting | bytes 786432 | tf_op jit(solution)/shard_map/reshape | solution.py:26
  102.4 3.0 %fusion.46 = f32[24,64,64]{2,1,0:T(8,128)} fusion(f32[24,64,64]{2,1,0:T(8,128)S(1)} %copy-done.1, f32[24,64,64]{2,1,0:T(8,128)} %reshape.140), kind=kOutput, calls=%fused_computation.194 | convolution fusion | flops 75497472 | bytes 1179648 | tf_op jit(solution)/shard_map/pik,pkj->pij/dot_general | solution.py:27
  105.4 1.5 %collective-permute-start.10 = (f32[20,4096]{1,0:T(8,128)}, f32[20,4096]{1,0:T(8,128)}, u32[]{:S(2)}, u32[]{:S(2)}) collective-permute-start(f32[20,4096]{1,0:T(8,128)} %collective-permute-done.9), channel_id=1, source_target_pairs={{0,4},{4,0},{8,12},{12,8},{16,20},{20,16},{24,28},{28,24},{1,5},{5... | collective-permute-start | bytes 983048 | tf_op jit(solution)/shard_map/ppermute | solution.py:20
  108.3 1.4 collective-permute-start.12
  109.6 2.0 %convolution_add_fusion.4 = f32[12,4096]{1,0:T(8,128)} fusion(f32[12,4096]{1,0:T(8,128)} %convolution_add_fusion.5, f32[24,4096]{1,0:T(8,128)S(1)} %reshape.141, f32[24]{0:T(128)S(1)} %copy-done.40, s32[24]{0:T(128)S(1)} %copy-done.28), kind=kOutput, calls=%fused_computation.21 | convolution fusion | flops 14205504 | bytes 786624 | tf_op jit(solution)/shard_map/dot_general | solution.py:32
  111.7 3.4 %collective-permute-done.10 = f32[20,4096]{1,0:T(8,128)} collective-permute-done((f32[20,4096]{1,0:T(8,128)}, f32[20,4096]{1,0:T(8,128)}, u32[]{:S(2)}, u32[]{:S(2)}) %collective-permute-start.10) | collective-permute-done | bytes 327712 | tf_op jit(solution)/shard_map/ppermute | solution.py:20
  116.3 1.4 gather_fusion.11
  117.7 1.4 gather_fusion.9
  119.8 1.9 %broadcast_select_fusion.4 = (f32[24,4096]{1,0:T(8,128)}, f32[24,4096]{1,0:T(8,128)S(1)}) fusion(f32[24,4096]{1,0:T(8,128)S(1)} %copy-done.10, pred[24]{0:T(512)(128)(4,1)S(1)} %copy-done.26, f32[24,4096]{1,0:T(8,128)} %gather_fusion.9, pred[24]{0:T(512)(128)(4,1)S(1)} %copy-done.27), kind=kLoop, calls=%fused_computation.29 | loop fusion | flops 196608 | bytes 1572912 | tf_op jit(solution)/shard_map/jit(_take)/select_n | solution.py:26
  121.7 1.2 reshape.143
  122.9 3.0 %fusion.47 = f32[24,64,64]{2,1,0:T(8,128)} fusion(f32[24,64,64]{2,1,0:T(8,128)S(1)} %copy-done, f32[24,64,64]{2,1,0:T(8,128)} %reshape.143), kind=kOutput, calls=%fused_computation.195 | convolution fusion | flops 75497472 | bytes 1179648 | tf_op jit(solution)/shard_map/pik,pkj->pij/dot_general | solution.py:27
  125.9 1.5 reshape.144
  127.3 1.3 reshape.146
  128.6 2.1 %fusion.48 = f32[24,64,64]{2,1,0:T(8,128)S(1)} fusion(f32[24,64,64]{2,1,0:T(8,128)S(1)} %reshape.145, f32[24,64,64]{2,1,0:T(8,128)} %reshape.146), kind=kOutput, calls=%fused_computation.196 | convolution fusion | flops 75497472 | bytes 1179648 | tf_op jit(solution)/shard_map/pik,pkj->pij/dot_general | solution.py:27
  130.7 1.6 %collective-permute-start.13 = (f32[20,4096]{1,0:T(8,128)}, f32[20,4096]{1,0:T(8,128)}, u32[]{:S(2)}, u32[]{:S(2)}) collective-permute-start(f32[20,4096]{1,0:T(8,128)} %collective-permute-done.12), channel_id=1, source_target_pairs={{0,4},{4,0},{8,12},{12,8},{16,20},{20,16},{24,28},{28,24},{1,5},{5... | collective-permute-start | bytes 983048 | tf_op jit(solution)/shard_map/ppermute | solution.py:20
  134.7 4.9 %collective-permute-done.13 = f32[20,4096]{1,0:T(8,128)} collective-permute-done((f32[20,4096]{1,0:T(8,128)}, f32[20,4096]{1,0:T(8,128)}, u32[]{:S(2)}, u32[]{:S(2)}) %collective-permute-start.13) | collective-permute-done | bytes 327712 | tf_op jit(solution)/shard_map/ppermute | solution.py:20
  (174 shorter events, 45.1 us)
Async XLA Ops:
  0.0 19.5 %collective-permute-start = (f32[2,4,4096]{2,1,0:T(4,128)}, f32[2,4,4096]{2,1,0:T(4,128)S(1)}, u32[]{:S(2)}, u32[]{:S(2)}) collective-permute-start(f32[2,4,4096]{2,1,0:T(4,128)} %bitcast.164), channel_id=1, source_target_pairs={{0,3},{1,0},{2,1},{3,2},{4,7},{5,4},{6,5},{7,6},{8,11},{9,8},{10,9... | collective-permute-start | bytes 393224 | tf_op jit(solution)/shard_map/ppermute | solution.py:14
  2.4 4.9 %copy-start.17 = (s32[1,1,4,2,24]{4,3,2,1,0:T(2,128)S(1)}, s32[1,1,4,2,24]{4,3,2,1,0:T(2,128)}, u32[]{:S(2)}) copy-start(s32[1,1,4,2,24]{4,3,2,1,0:T(2,128)} %param.12) | copy-start | bytes 2308
  2.4 4.9 %copy-start.18 = (s32[1,1,4,2,24]{4,3,2,1,0:T(2,128)S(1)}, s32[1,1,4,2,24]{4,3,2,1,0:T(2,128)}, u32[]{:S(2)}) copy-start(s32[1,1,4,2,24]{4,3,2,1,0:T(2,128)} %param.13) | copy-start | bytes 2308
  2.4 6.8 %copy-start.16 = (s32[1,1,4,2]{2,3,1,0:T(2,128)S(1)}, s32[1,1,4,2]{2,3,1,0:T(2,128)}, u32[]{:S(2)}) copy-start(s32[1,1,4,2]{2,3,1,0:T(2,128)} %param.15) | copy-start | bytes 100
  2.4 8.7 %copy-start.19 = (s32[1,1,4,2,24]{4,3,2,1,0:T(2,128)S(1)}, s32[1,1,4,2,24]{4,3,2,1,0:T(2,128)}, u32[]{:S(2)}) copy-start(s32[1,1,4,2,24]{4,3,2,1,0:T(2,128)} %param.14) | copy-start | bytes 2308
  3.6 15.9 %copy-start.15 = (f32[1,2,4,4096]{3,2,1,0:T(4,128)S(1)}, f32[1,2,4,4096]{3,2,1,0:T(4,128)}, u32[]{:S(2)}) copy-start(f32[1,2,4,4096]{3,2,1,0:T(4,128)} %param.10) | copy-start | bytes 393220
  3.6 25.2 %collective-permute-start.2 = (f32[20,4096]{1,0:T(8,128)S(1)}, f32[20,4096]{1,0:T(8,128)S(1)}, u32[]{:S(2)}, u32[]{:S(2)}) collective-permute-start(f32[20,4096]{1,0:T(8,128)S(1)} %bitcast.163), channel_id=1, source_target_pairs={{0,24},{4,28},{8,0},{12,4},{16,8},{20,12},{24,16},{28,20},{1,25},{... | collective-permute-start | bytes 983048 | tf_op jit(solution)/shard_map/ppermute | solution.py:14
  19.6 5.0 %collective-permute-start.1 = (f32[2,4,4096]{2,1,0:T(4,128)S(1)}, f32[2,4,4096]{2,1,0:T(4,128)S(1)}, u32[]{:S(2)}, u32[]{:S(2)}) collective-permute-start(f32[2,4,4096]{2,1,0:T(4,128)S(1)} %broadcast_select_fusion.26), channel_id=1, source_target_pairs={{0,2},{1,3},{2,0},{3,1},{4,6},{5,7},{6,4},{7,5},{8,10},{9,11},{10,... | collective-permute-start | bytes 393224 | tf_op jit(solution)/shard_map/ppermute | solution.py:14
  24.6 4.5 %collective-permute-start.5 = (f32[2,4,4096]{2,1,0:T(4,128)S(1)}, f32[2,4,4096]{2,1,0:T(4,128)S(1)}, u32[]{:S(2)}, u32[]{:S(2)}) collective-permute-start(f32[2,4,4096]{2,1,0:T(4,128)S(1)} %bitcast.162), channel_id=1, source_target_pairs={{0,3},{1,0},{2,1},{3,2},{4,7},{5,4},{6,5},{7,6},{8,11},{9,8},{10,9... | collective-permute-start | bytes 393224 | tf_op jit(solution)/shard_map/ppermute | solution.py:14
  27.6 1.2 copy-start.11
  29.0 18.5 %collective-permute-start.3 = (f32[20,4096]{1,0:T(8,128)S(1)}, f32[20,4096]{1,0:T(8,128)S(1)}, u32[]{:S(2)}, u32[]{:S(2)}) collective-permute-start(f32[20,4096]{1,0:T(8,128)S(1)} %broadcast_select_fusion.16), channel_id=1, source_target_pairs={{0,16},{4,20},{8,24},{12,28},{16,0},{20,4},{24,8},{28,12},{1,17},{... | collective-permute-start | bytes 983048 | tf_op jit(solution)/shard_map/ppermute | solution.py:14
  30.5 3.7 %collective-permute-start.8 = (f32[2,4,4096]{2,1,0:T(4,128)S(1)}, f32[2,4,4096]{2,1,0:T(4,128)S(1)}, u32[]{:S(2)}, u32[]{:S(2)}) collective-permute-start(f32[2,4,4096]{2,1,0:T(4,128)S(1)} %collective-permute-done.5), channel_id=1, source_target_pairs={{0,3},{1,0},{2,1},{3,2},{4,7},{5,4},{6,5},{7,6},{8,11},{9,8},{10,9... | collective-permute-start | bytes 393224 | tf_op jit(solution)/shard_map/ppermute | solution.py:14
  37.2 15.2 %collective-permute-start.11 = (f32[2,4,4096]{2,1,0:T(4,128)S(1)}, f32[2,4,4096]{2,1,0:T(4,128)S(1)}, u32[]{:S(2)}, u32[]{:S(2)}) collective-permute-start(f32[2,4,4096]{2,1,0:T(4,128)S(1)} %collective-permute-done.8), channel_id=1, source_target_pairs={{0,3},{1,0},{2,1},{3,2},{4,7},{5,4},{6,5},{7,6},{8,11},{9,8},{10,9... | collective-permute-start | bytes 393224 | tf_op jit(solution)/shard_map/ppermute | solution.py:14
  48.4 11.3 %collective-permute-start.4 = (f32[20,4096]{1,0:T(8,128)}, f32[20,4096]{1,0:T(8,128)S(1)}, u32[]{:S(2)}, u32[]{:S(2)}) collective-permute-start(f32[20,4096]{1,0:T(8,128)} %broadcast_select_fusion.17), channel_id=1, source_target_pairs={{0,4},{4,0},{8,12},{12,8},{16,20},{20,16},{24,28},{28,24},{1,5},{5... | collective-permute-start | bytes 983048 | tf_op jit(solution)/shard_map/ppermute | solution.py:20
  49.9 27.3 %collective-permute-start.6 = (f32[20,4096]{1,0:T(8,128)}, f32[20,4096]{1,0:T(8,128)}, u32[]{:S(2)}, u32[]{:S(2)}) collective-permute-start(f32[20,4096]{1,0:T(8,128)} %broadcast_select_fusion.17), channel_id=1, source_target_pairs={{0,24},{4,28},{8,0},{12,4},{16,8},{20,12},{24,16},{28,20},{1,25},{... | collective-permute-start | bytes 983048 | tf_op jit(solution)/shard_map/ppermute | solution.py:14
  62.2 1.7 %copy-start.8 = (f32[24,4096]{1,0:T(8,128)S(1)}, f32[24,4096]{1,0:T(8,128)}, u32[]{:S(2)}) copy-start(f32[24,4096]{1,0:T(8,128)} %gather_fusion.3) | copy-start | bytes 1179652
  63.9 0.7 copy-start.35
  66.4 1.2 copy-start.4
  72.0 2.3 %copy-start.3 = (f32[24,64,64]{2,1,0:T(8,128)S(1)}, f32[24,64,64]{2,1,0:T(8,128)}, u32[]{:S(2)}) copy-start(f32[24,64,64]{2,1,0:T(8,128)} %reshape.133) | copy-start | bytes 1179652
  77.2 1.6 %copy-start.33 = (s32[24]{0:T(128)S(1)}, s32[24]{0:T(128)}, u32[]{:S(2)}) copy-start(s32[24]{0:T(128)} %get-tuple-element.62) | copy-start | bytes 292
  77.2 1.6 %copy-start.42 = (f32[24]{0:T(128)S(1)}, f32[24]{0:T(128)}, u32[]{:S(2)}) copy-start(f32[24]{0:T(128)} %compare_convert_fusion.7) | copy-start | bytes 292
  77.2 10.7 %collective-permute-start.7 = (f32[20,4096]{1,0:T(8,128)}, f32[20,4096]{1,0:T(8,128)}, u32[]{:S(2)}, u32[]{:S(2)}) collective-permute-start(f32[20,4096]{1,0:T(8,128)} %collective-permute-done.6), channel_id=1, source_target_pairs={{0,4},{4,0},{8,12},{12,8},{16,20},{20,16},{24,28},{28,24},{1,5},{5... | collective-permute-start | bytes 983048 | tf_op jit(solution)/shard_map/ppermute | solution.py:20
  80.6 2.2 %copy-start.32 = (s32[24]{0:T(128)S(1)}, s32[24]{0:T(128)}, u32[]{:S(2)}) copy-start(s32[24]{0:T(128)} %get-tuple-element.61) | copy-start | bytes 292
  80.6 2.2 %copy-start.43 = (f32[24]{0:T(128)S(1)}, f32[24]{0:T(128)}, u32[]{:S(2)}) copy-start(f32[24]{0:T(128)} %compare_convert_fusion.6) | copy-start | bytes 292
  80.6 24.8 %collective-permute-start.9 = (f32[20,4096]{1,0:T(8,128)}, f32[20,4096]{1,0:T(8,128)}, u32[]{:S(2)}, u32[]{:S(2)}) collective-permute-start(f32[20,4096]{1,0:T(8,128)} %collective-permute-done.6), channel_id=1, source_target_pairs={{0,24},{4,28},{8,0},{12,4},{16,8},{20,12},{24,16},{28,20},{1,25},{... | collective-permute-start | bytes 983048 | tf_op jit(solution)/shard_map/ppermute | solution.py:14
  90.6 1.4 copy-start.9
  94.6 1.2 copy-start.2
  100.1 2.3 %copy-start.1 = (f32[24,64,64]{2,1,0:T(8,128)S(1)}, f32[24,64,64]{2,1,0:T(8,128)}, u32[]{:S(2)}) copy-start(f32[24,64,64]{2,1,0:T(8,128)} %reshape.139) | copy-start | bytes 1179652
  102.4 4.5 %copy-start.12 = (f32[12,4096]{1,0:T(8,128)S(1)}, f32[12,4096]{1,0:T(8,128)}, u32[]{:S(2)}) copy-start(f32[12,4096]{1,0:T(8,128)} %convolution_add_fusion.6) | copy-start | bytes 589828
  102.4 4.5 %copy-start.29 = (s32[24]{0:T(128)S(1)}, s32[24]{0:T(128)}, u32[]{:S(2)}) copy-start(s32[24]{0:T(128)} %get-tuple-element.60) | copy-start | bytes 292
  102.4 4.5 %copy-start.41 = (f32[24]{0:T(128)S(1)}, f32[24]{0:T(128)}, u32[]{:S(2)}) copy-start(f32[24]{0:T(128)} %compare_convert_fusion.5) | copy-start | bytes 292
  105.4 2.6 %copy-start.5 = (f32[24,64,64]{2,1,0:T(8,128)S(1)}, f32[24,64,64]{2,1,0:T(8,128)}, u32[]{:S(2)}) copy-start(f32[24,64,64]{2,1,0:T(8,128)} %fusion.46) | copy-start | bytes 1179652
  105.4 9.7 %collective-permute-start.10 = (f32[20,4096]{1,0:T(8,128)}, f32[20,4096]{1,0:T(8,128)}, u32[]{:S(2)}, u32[]{:S(2)}) collective-permute-start(f32[20,4096]{1,0:T(8,128)} %collective-permute-done.9), channel_id=1, source_target_pairs={{0,4},{4,0},{8,12},{12,8},{16,20},{20,16},{24,28},{28,24},{1,5},{5... | collective-permute-start | bytes 983048 | tf_op jit(solution)/shard_map/ppermute | solution.py:20
  108.2 1.4 copy-start.28
  108.2 1.4 copy-start.40
  108.3 22.4 %collective-permute-start.12 = (f32[20,4096]{1,0:T(8,128)}, f32[20,4096]{1,0:T(8,128)}, u32[]{:S(2)}, u32[]{:S(2)}) collective-permute-start(f32[20,4096]{1,0:T(8,128)} %collective-permute-done.9), channel_id=1, source_target_pairs={{0,24},{4,28},{8,0},{12,4},{16,8},{20,12},{24,16},{28,20},{1,25},{... | collective-permute-start | bytes 983048 | tf_op jit(solution)/shard_map/ppermute | solution.py:14
  117.7 1.4 copy-start.10
  119.1 0.7 copy-start.27
  121.7 1.2 copy-start
  125.8 1.5 copy-start.6
  128.6 3.7 %copy-start.13 = (f32[12,4096]{1,0:T(8,128)S(1)}, f32[12,4096]{1,0:T(8,128)}, u32[]{:S(2)}) copy-start(f32[12,4096]{1,0:T(8,128)} %convolution_add_fusion.4) | copy-start | bytes 589828
  130.7 1.6 %copy-start.25 = (s32[24]{0:T(128)S(1)}, s32[24]{0:T(128)}, u32[]{:S(2)}) copy-start(s32[24]{0:T(128)} %get-tuple-element.58) | copy-start | bytes 292
  130.7 1.6 %copy-start.38 = (f32[24]{0:T(128)S(1)}, f32[24]{0:T(128)}, u32[]{:S(2)}) copy-start(f32[24]{0:T(128)} %compare_convert_fusion.3) | copy-start | bytes 292
  130.7 8.9 %collective-permute-start.13 = (f32[20,4096]{1,0:T(8,128)}, f32[20,4096]{1,0:T(8,128)}, u32[]{:S(2)}, u32[]{:S(2)}) collective-permute-start(f32[20,4096]{1,0:T(8,128)} %collective-permute-done.12), channel_id=1, source_target_pairs={{0,4},{4,0},{8,12},{12,8},{16,20},{20,16},{24,28},{28,24},{1,5},{5... | collective-permute-start | bytes 983048 | tf_op jit(solution)/shard_map/ppermute | solution.py:20
  142.2 0.7 copy-start.22
  145.0 1.0 copy-start.7
  147.3 1.0 copy-start.14
  147.6 0.7 copy-start.36
  (10 other events, 6.3 us)
where the time goes:
time: 152 us; the launch traced here: 151 us
  local copies, waits for them, and re-layouts  48.6 us (32%)
  waiting for transfers between devices  28.3 us (19%)
  matrix products  25.2 us (17%)
  other arithmetic  25.1 us (17%)
  starting transfers between devices  22.8 us (15%)
    dot_general x8, matrix products, block_terms(): jnp.einsum('pik,pkj->pij', left_tiles, right_tiles, precision=lax.Precisi...  18.6 us
    ppermute x4, waiting for transfers between devices, partner_2(): return lax.ppermute(value, axis, pairs)  17.4 us
    ppermute x10, starting transfers between devices, shifted_2(): lax.ppermute(shard, axis, [(i, (i + by) % devices) for i in range(devices)])  16.6 us
    ppermute x10, waiting for transfers between devices, shifted_2(): lax.ppermute(shard, axis, [(i, (i + by) % devices) for i in range(devices)])  10.9 us
    gather x8, local copies, waits for them, and re-layouts, block_terms(): jnp.take(right_panel, right_index, axis=0)  10.5 us
    reshape x8, local copies, waits for them, and re-layouts, block_terms(): jnp.take(right_panel, right_index, axis=0)  10.1 us
    convert_element_type x8, other arithmetic, block_terms(): is_live = (jnp.arange(PRODUCTS) < live_count).astype(jnp.float32)  9.46 us
    reshape x8, local copies, waits for them, and re-layouts, block_terms(): jnp.take(left_panel, left_index, axis=0)  7.01 us
  transfers between devices with their start and end apart: 14, of which 6 were waited for; matrix products, arithmetic and copies ran while one was open for 57% of the time, Pallas kernels for 0%

commit v1 on v0

v1 whole, which is shorter than its diff:
```python
import functools

import jax
import jax.numpy as jnp
from jax import lax
from jax.experimental import pallas as pl
from jax.experimental.pallas import tpu as pltpu
from jax.sharding import PartitionSpec as P

TILE_SIDE = 64
LEFT_SLOTS = 4
RIGHT_SLOTS = 20
SINK_SLOTS = 12
PRODUCTS = 24
SECTIONS = 4
HALF = TILE_SIDE // 2
LANES = 2 * TILE_SIDE
AXES = ("row", "col")
MIB = 1 << 20


def in_low_half(shape):
    return lax.broadcasted_iota(jnp.int32, shape, 1) % LANES < TILE_SIDE


def spread_table():
    shape = (2 * LANES, 8 * TILE_SIDE)
    source = lax.broadcasted_iota(jnp.int32, shape, 0)
    target = lax.broadcasted_iota(jnp.int32, shape, 1)
    place = target % TILE_SIDE
    part = target // TILE_SIDE % 2
    odd_row = target // (4 * TILE_SIDE)
    inner = 2 * (place % HALF) + place // HALF
    return (source == part * LANES + odd_row * TILE_SIDE + inner).astype(jnp.bfloat16)


def spread_left(blocks, table):
    high = blocks.astype(jnp.bfloat16)
    low = (blocks - high.astype(jnp.float32)).astype(jnp.bfloat16)
    both = jnp.concatenate([high, low], axis=1)
    wide = jnp.dot(both, table, preferred_element_type=jnp.float32).astype(jnp.bfloat16)
    return jnp.concatenate([wide[:, : 4 * TILE_SIDE], wide[:, 4 * TILE_SIDE :]], axis=0)


def slots_in_order(panel_ref, half):
    return jnp.concatenate(
        [panel_ref[half, pl.ds(slot, HALF, stride=LEFT_SLOTS), :] for slot in range(LEFT_SLOTS)], axis=0
    )


def right_pair(first, second):
    low_half = in_low_half((HALF, LANES))
    first_turned = pltpu.roll(first, TILE_SIDE, 1)
    second_turned = pltpu.roll(second, TILE_SIDE, 1)
    even = jnp.where(low_half, first, second_turned)
    odd = jnp.where(low_half, first_turned, second)
    rows = jnp.concatenate([even, odd], axis=0)
    high = rows.astype(jnp.bfloat16)
    low = (rows - high.astype(jnp.float32)).astype(jnp.bfloat16)
    return jnp.concatenate([high, high, low, low], axis=0)


def all_products(lefts, right_ref, product_refs):
    rows = LEFT_SLOTS * HALF
    left = lefts[0] if len(lefts) == 1 else jnp.concatenate(lefts, axis=0)
    low_half = in_low_half((HALF, LANES))
    for slot in range(0, RIGHT_SLOTS, 4):
        weights = jnp.concatenate(
            [right_pair(right_ref[slot + n], right_ref[slot + n + 1]) for n in (0, 2)], axis=1
        )
        result = jnp.dot(left, weights, preferred_element_type=jnp.float32)
        for t, product_ref in enumerate(product_refs):
            for l in range(LEFT_SLOTS):
                for n in (0, 2):
                    start = t * 2 * rows + l * HALF
                    even = result[start : start + HALF, n * TILE_SIDE : (n + 2) * TILE_SIDE]
                    odd = result[start + rows : start + rows + HALF, n * TILE_SIDE : (n + 2) * TILE_SIDE]
                    place = l * RIGHT_SLOTS + slot + n
                    product_ref[place] = jnp.where(low_half, even, pltpu.roll(odd, TILE_SIDE, 1))
                    product_ref[place + 1] = jnp.where(low_half, pltpu.roll(even, TILE_SIDE, 1), odd)


def add_listed(total_ref, product_ref, lists, section, half):
    left_ref, right_ref, sink_ref, count_ref = lists
    live = count_ref[section, half]
    for p in range(PRODUCTS):
        place = left_ref[section, half, p] * RIGHT_SLOTS + right_ref[section, half, p]
        sink = jnp.where(p < live, sink_ref[section, half, p], SINK_SLOTS)
        total_ref[sink] += product_ref[place]


def group_kernel(
    meta, near_l, near_r, near_s, near_n, far_l, far_r, far_s, far_n,
    own, q1, q2, r1, r2, r3, right_own, right_y, right_z,
    near_out, far_out, near_left_d, far_left_d,
    lefts, near_total, far_total, near_products, far_products,
):
    table = spread_table()
    inside = meta[0] == 1
    for half in range(2):
        def pick(a, b, half=half):
            return jnp.where(inside, slots_in_order(a, half), slots_in_order(b, half))
        lefts[0, 0, half] = spread_left(pick(own, q1), table)
        lefts[0, 1, half] = spread_left(pick(q2, r1), table)
        lefts[1, 0, half] = spread_left(pick(q1, r2), table)
        lefts[1, 1, half] = spread_left(pick(r1, r3), table)
    near_total[...] = jnp.zeros_like(near_total)
    far_total[...] = jnp.zeros_like(far_total)
    near_lists = (near_l, near_r, near_s, near_n)
    far_lists = (far_l, far_r, far_s, far_n)
    half = meta[1]
    for right, level, in_half in ((right_own, 0, half), (right_y, 0, 1 - half), (right_z, 1, half)):
        which = meta[2 + level]
        all_products(
            [lefts[0, which, in_half], lefts[1, which, in_half]], right, [near_products, far_products]
        )
        add_listed(far_total, far_products, far_lists, meta[6 + level], in_half)
        add_listed(near_total, near_products, near_lists, meta[4 + level], in_half)
    near_out[...] = near_total[:SINK_SLOTS]
    far_out[...] = far_total[:SINK_SLOTS]
    near_left_d[...] = lefts[0, meta[3], 1 - half]
    far_left_d[...] = lefts[1, meta[3], 1 - half]


def last_kernel(meta, l, r, s, n, left, right, before, out, total, products, *, far):
    total[:SINK_SLOTS] = before[...]
    all_products([left[...]], right, [products])
    add_listed(total, products, (l, r, s, n), meta[7 if far else 5], 1 - meta[1])
    out[...] = total[:SINK_SLOTS]


def pair_kernel(meta, l, r, s, n, left, right_0, right_1, before, out, total, products):
    table = spread_table()
    total[:SINK_SLOTS] = before[...]
    for half, right in ((0, right_0), (1, right_1)):
        all_products([spread_left(slots_in_order(left, half), table)], right, [products])
        add_listed(total, products, (l, r, s, n), meta[0], half)
    out[...] = total[:SINK_SLOTS]


SMEM = pl.BlockSpec(memory_space=pltpu.SMEM)
VMEM = pl.BlockSpec(memory_space=pltpu.VMEM)
SUMS = (SINK_SLOTS, HALF, LANES)
TOTAL = pltpu.VMEM((SINK_SLOTS + 1, HALF, LANES), jnp.float32)
PRODUCT_TABLE = pltpu.VMEM((LEFT_SLOTS * RIGHT_SLOTS, HALF, LANES), jnp.float32)
SPREAD = (2 * LEFT_SLOTS * HALF, 4 * TILE_SIDE)


def call(kernel, n_smem, n_vmem, outs, scratch, flops, name):
    return pl.pallas_call(
        kernel,
        out_shape=outs,
        in_specs=[SMEM] * n_smem + [VMEM] * n_vmem,
        out_specs=jax.tree.map(lambda _: VMEM, outs),
        scratch_shapes=scratch,
        compiler_params=pltpu.CompilerParams(vmem_limit_bytes=24 * MIB),
        cost_estimate=pl.CostEstimate(flops=flops, bytes_accessed=4 * MIB, transcendentals=0),
        name=name,
    )


def sums():
    return jax.ShapeDtypeStruct(SUMS, jnp.float32)


def spread_shape():
    return jax.ShapeDtypeStruct(SPREAD, jnp.bfloat16)


def left_view(panels):
    halves = panels.shape[0]
    return panels.reshape(halves, LEFT_SLOTS, HALF, LANES).transpose(0, 2, 1, 3).reshape(halves, -1, LANES)


def grouped(left, right, lists):
    cols = lax.axis_size("col")

    def device(pair, parity, col):
        return (2 * pair + parity) * cols + col

    def send(value, to):
        where = [
            (device(pair, parity, col), device(*to(pair, parity, col)))
            for pair in range(cols)
            for parity in range(2)
            for col in range(cols)
        ]
        return lax.ppermute(value, AXES, where)

    row, col = lax.axis_index("row"), lax.axis_index("col")
    pair, parity = row // 2, row % 2
    core = col % 2
    inside = (col // 2 == pair // 2).astype(jnp.int32)
    level_0 = (pair % 2 != core).astype(jnp.int32)
    far_pair = pair ^ 2
    meta = jnp.stack(
        [
            inside,
            parity,
            level_0,
            1 - level_0,
            (pair - pair - col) % cols,
            ((pair ^ 1) - pair - col) % cols,
            (pair - far_pair - col) % cols,
            ((pair ^ 1) - far_pair - col) % cols,
        ]
    ).astype(jnp.int32)

    def left_home(pair, parity, col):
        return (pair, parity, col ^ 2) if col // 2 == pair // 2 else (pair ^ 2, parity, col)

    q1 = send(left, left_home)
    right_y = send(right, lambda pair, parity, col: (pair, 1 - parity, col))
    right_z = send(right, lambda pair, parity, col: (pair ^ 1, parity, col))
    right_d = send(right, lambda pair, parity, col: (pair ^ 1, 1 - parity, col))
    q2 = send(left, lambda pair, parity, col: (pair, parity, col ^ 1))
    left_list, right_list, sink_list, counts = lists
    packed = jnp.concatenate([left_list, right_list, sink_list, counts[..., None]], axis=-1)
    packed = send(packed, lambda pair, parity, col: (pair ^ 2, parity, col))
    far_lists = tuple(packed[..., n * PRODUCTS : (n + 1) * PRODUCTS] for n in range(3)) + (packed[..., -1],)
    r1 = send(q1, lambda pair, parity, col: (pair, parity, col ^ 1))
    r2 = send(q1, lambda pair, parity, col: (pair, parity, col ^ 2))
    r3 = send(q1, lambda pair, parity, col: (pair, parity, col ^ 3))

    near, far, near_left, far_left = call(
        group_kernel, 9, 9,
        (sums(), sums(), spread_shape(), spread_shape()),
        [pltpu.VMEM((2, 2, 2) + SPREAD, jnp.bfloat16), TOTAL, TOTAL, PRODUCT_TABLE, PRODUCT_TABLE],
        3 * 10**9, "three_panels",
    )(meta, *lists, *far_lists, left, q1, q2, r1, r2, r3, right, right_y, right_z)
    far = call(
        functools.partial(last_kernel, far=True), 5, 3, sums(), [TOTAL, PRODUCT_TABLE], 10**9, "far_panel"
    )(meta, *far_lists, far_left, right_d, far)
    received = send(far, lambda pair, parity, col: (pair ^ 2, parity, col))
    near = call(
        functools.partial(last_kernel, far=False), 5, 3, sums(), [TOTAL, PRODUCT_TABLE], 10**9, "near_panel"
    )(meta, *lists, near_left, right_d, near)
    return near + received


def shifted(shard, axis, by):
    devices = lax.axis_size(axis)
    return lax.ppermute(shard, axis, [(i, (i + by) % devices) for i in range(devices)])


def windowed(left, right, lists):
    cols = lax.axis_size("col")
    half_row, parity = lax.axis_index("row") // 2, lax.axis_index("row") % 2
    column = lax.axis_index("col")
    bits = cols.bit_length() - 1
    for bit in range(bits):
        right = jnp.where(column // (1 << bit) % 2 == 1, shifted(right, "row", -(2 << bit)), right)
        left = jnp.where(half_row // (1 << bit) % 2 == 1, shifted(left, "col", -(1 << bit)), left)
    total = jnp.zeros(SUMS, jnp.float32)
    for section in range(SECTIONS):
        swap = [(i, i ^ 1) for i in range(lax.axis_size("row"))]
        partner = lax.ppermute(right, "row", swap)
        total = call(pair_kernel, 5, 4, sums(), [TOTAL, PRODUCT_TABLE], 2 * 10**9, "panel_pair")(
            jnp.full((1,), section, jnp.int32), *lists, left,
            jnp.where(parity == 0, right, partner), jnp.where(parity == 0, partner, right), total,
        )
        if section + 1 < SECTIONS:
            right = shifted(right, "row", -2)
            left = shifted(left, "col", -1)
    return total


def per_device(left_blocks, right_blocks, left_slots, right_slots, sink_slots, live_counts):
    left = left_view(left_blocks[0])
    right = right_blocks.reshape(RIGHT_SLOTS, HALF, LANES)
    lists = (left_slots[0, 0], right_slots[0, 0], sink_slots[0, 0], live_counts[0, 0])
    plan = grouped if lax.axis_size("col") == SECTIONS == 4 else windowed
    return plan(left, right, lists).reshape(1, 1, SINK_SLOTS, TILE_SIDE * TILE_SIDE)


def solution(mesh):
    return jax.shard_map(
        per_device,
        mesh=mesh,
        in_specs=(
            P("row", "col", None, None),
            P("row", "col", None, None),
            P("row", "col", None, None, None),
            P("row", "col", None, None, None),
            P("row", "col", None, None, None),
            P("row", "col", None, None),
        ),
        out_specs=P("row", "col", None, None),
        check_vma=False,
    )
```

time: 152 us -> 52.8 us (0.35)
  local copies, waits for them, and re-layouts: 48.6 us -> 2.21 us
  matrix products: 25.2 us -> 0 us
  other arithmetic: 25.1 us -> 0.79 us
  starting transfers between devices: 22.8 us -> 10.9 us
  Pallas kernels: 0 us -> 9.09 us
    dot_general x16 -> x0, matrix products: 25.2 us -> none  [the longest x8 18.6 us: block_terms(): jnp.einsum('pik,pkj->pij', left_tiles, right_tiles, precision=lax.Precisi...]
    reshape x24 -> x0, local copies, waits for them, and re-layouts: 23.9 us -> none  [the longest x8 10.1 us: block_terms(): jnp.take(right_panel, right_index, axis=0)]
    gather x16 -> x0, local copies, waits for them, and re-layouts: 15.8 us -> none  [the longest x8 10.5 us: block_terms(): jnp.take(right_panel, right_index, axis=0)]
    select_n x16 -> x0, other arithmetic: 12.6 us -> none  [the longest x4 6.48 us: block_terms(): jnp.take(right_panel, right_index, axis=0)]
    ppermute x14 -> x10, starting transfers between devices: 22.8 us -> 10.9 us  [send(): return lax.ppermute(value, AXES, where)]
    convert_element_type x8 -> x0, other arithmetic: 9.46 us -> none  [block_terms(): is_live = (jnp.arange(PRODUCTS) < live_count).astype(jnp.float32)]
    pallas_call x0 -> x3, Pallas kernels: none -> 9.09 us  [the longest x1 5.92 us: grouped(): call(group_kernel, 9, 9, (sums(), sums(), spread_shape(), spread_shape())...]
    unnamed x89 -> x12, local copies, waits for them, and re-layouts: 6.64 us -> 1.59 us
  transfers between devices with their start and end apart: 14 -> 10, of which waited for: 6 -> 5; matrix products, arithmetic and copies ran while one was open for 57% -> 1% of each run, Pallas kernels for 0% -> 14%
where the time goes in v1:
time: 52.8 us; the launch traced here: 52.6 us
  waiting for transfers between devices  29.6 us (56%)
  starting transfers between devices  10.9 us (21%)
  Pallas kernels  9.09 us (17%)
  local copies, waits for them, and re-layouts  2.21 us (4%)
  other arithmetic  0.79 us (1%)
    ppermute x10, waiting for transfers between devices, send(): return lax.ppermute(value, AXES, where)  29.6 us
    ppermute x10, starting transfers between devices, send(): return lax.ppermute(value, AXES, where)  10.9 us
    pallas_call x1, Pallas kernels, grouped(): call(group_kernel, 9, 9, (sums(), sums(), spread_shape(), spread_shape())...  5.92 us
    pallas_call x1, Pallas kernels, grouped(): call(functools.partial(last_kernel, far=True), 5, 3, sums(), [TOTAL, PROD...  1.6 us
    unnamed x12, local copies, waits for them, and re-layouts  1.59 us
    pallas_call x1, Pallas kernels, grouped(): call(functools.partial(last_kernel, far=False), 5, 3, sums(), [TOTAL, PRO...  1.56 us
  transfers between devices with their start and end apart: 10, of which 5 were waited for; matrix products, arithmetic and copies ran while one was open for 1% of the time, Pallas kernels for 14%

profile of v1, /device:TPU:0, one launch (start us, length us, event | category | flops | bytes accessed | tf_op | source)
XLA Modules:
  0.0 52.6 jit_solution(1871358275351544117)
XLA Ops:
  0.0 2.9 %collective-permute-start.1 = (f32[2,128,128]{2,1,0:T(8,128)}, f32[2,128,128]{2,1,0:T(8,128)S(1)}, u32[]{:S(2)}, u32[]{:S(2)}) collective-permute-start(f32[2,128,128]{2,1,0:T(8,128)} %bitcast.34), channel_id=1, source_target_pairs={{0,2},{1,3},{2,18},{3,19},{4,6},{5,7},{6,22},{7,23},{8,10},{9,11},... | collective-permute-start | bytes 393224 | tf_op jit(solution)/shard_map/ppermute | solution.py:188
  2.9 0.0 collective-permute-start.2
  2.9 7.6 %collective-permute-done.1.q1 = f32[2,128,128]{2,1,0:T(8,128)S(1)} collective-permute-done((f32[2,128,128]{2,1,0:T(8,128)}, f32[2,128,128]{2,1,0:T(8,128)S(1)}, u32[]{:S(2)}, u32[]{:S(2)}) %collective-permute-start.1) | collective-permute-done | bytes 131104 | tf_op jit(solution)/shard_map/ppermute | solution.py:188
  10.6 0.0 collective-permute-start.3
  10.6 0.0 copy-start.5
  10.6 1.6 %collective-permute-start.6 = (f32[20,32,128]{2,1,0:T(8,128)}, f32[20,32,128]{2,1,0:T(8,128)S(1)}, u32[]{:S(2)}, u32[]{:S(2)}) collective-permute-start(f32[20,32,128]{2,1,0:T(8,128)} %bitcast.30), channel_id=1, source_target_pairs={{0,4},{1,5},{2,6},{3,7},{4,0},{5,1},{6,2},{7,3},{8,12},{9,13},{10,... | collective-permute-start | bytes 983048 | tf_op jit(solution)/shard_map/ppermute | solution.py:188
  12.1 0.0 collective-permute-start.7
  12.1 0.0 copy-start.2
  12.1 0.0 copy-done.5
  12.1 0.0 copy-start.1
  12.1 0.1 copy.15
  12.2 0.0 copy-start
  12.2 0.0 copy-start.3
  12.2 0.6 %copy-done.2 = s32[1,1,4,2,24]{4,3,2,1,0:T(2,128)S(1)} copy-done((s32[1,1,4,2,24]{4,3,2,1,0:T(2,128)S(1)}, s32[1,1,4,2,24]{4,3,2,1,0:T(2,128)}, u32[]{:S(2)}) %copy-start.2) | copy-done | bytes 792
  12.8 0.0 copy-done.1
  12.8 0.1 copy-done
  12.9 0.1 pad_add_fusion
  13.0 0.5 collective-permute-start
  13.5 0.1 copy.20.near_n.n
  13.6 0.1 stack.39.meta
  13.6 6.5 %collective-permute-done = s32[4,2,73]{2,1,0:T(2,128)S(1)} collective-permute-done((s32[4,2,73]{2,1,0:T(2,128)S(1)}, s32[4,2,73]{2,1,0:T(2,128)S(1)}, u32[]{:S(2)}, u32[]{:S(2)}) %collective-permute-start) | collective-permute-done | bytes 2368 | tf_op jit(solution)/shard_map/ppermute | solution.py:188
  20.2 1.6 %collective-permute-start.8 = (f32[20,32,128]{2,1,0:T(8,128)}, f32[20,32,128]{2,1,0:T(8,128)S(1)}, u32[]{:S(2)}, u32[]{:S(2)}) collective-permute-start(f32[20,32,128]{2,1,0:T(8,128)} %bitcast.32), channel_id=1, source_target_pairs={{0,12},{1,13},{2,14},{3,15},{4,8},{5,9},{6,10},{7,11},{8,4},{9,5},... | collective-permute-start | bytes 983048 | tf_op jit(solution)/shard_map/ppermute | solution.py:188
  21.8 0.0 collective-permute-done.2.q2
  21.8 4.2 %collective-permute-start.4 = (f32[2,128,128]{2,1,0:T(8,128)S(1)}, f32[2,128,128]{2,1,0:T(8,128)S(1)}, u32[]{:S(2)}, u32[]{:S(2)}) collective-permute-start(f32[2,128,128]{2,1,0:T(8,128)S(1)} %collective-permute-done.1.q1), channel_id=1, source_target_pairs={{0,2},{1,3},{2,0},{3,1},{4,6},{5,7},{6,4},{7,5},{8,10},{9,11},{10,... | collective-permute-start | bytes 393224 | tf_op jit(solution)/shard_map/ppermute | solution.py:188
  26.1 0.0 collective-permute-done.3.r1
  26.1 0.0 collective-permute-start.5
  26.1 0.1 fusion
  26.1 0.1 slice.19
  26.2 0.1 copy.16
  26.3 0.1 copy.19.far_n.n
  26.4 3.1 %collective-permute-done.4.r2 = f32[2,128,128]{2,1,0:T(8,128)S(1)} collective-permute-done((f32[2,128,128]{2,1,0:T(8,128)S(1)}, f32[2,128,128]{2,1,0:T(8,128)S(1)}, u32[]{:S(2)}, u32[]{:S(2)}) %collective-permute-start.4) | collective-permute-done | bytes 131104 | tf_op jit(solution)/shard_map/ppermute | solution.py:188
  29.5 2.3 %collective-permute-done.5.r3 = f32[2,128,128]{2,1,0:T(8,128)S(1)} collective-permute-done((f32[2,128,128]{2,1,0:T(8,128)S(1)}, f32[2,128,128]{2,1,0:T(8,128)S(1)}, u32[]{:S(2)}, u32[]{:S(2)}) %collective-permute-start.5) | collective-permute-done | bytes 131104 | tf_op jit(solution)/shard_map/ppermute | solution.py:188
  31.8 0.0 collective-permute-done.6.right_y
  31.8 0.0 collective-permute-done.7.right_z
  31.8 0.0 copy-done.3
  31.8 0.0 copy-start.4
  31.8 0.9 %copy-done.4 = f32[1,2,4,4096]{3,2,1,0:T(4,128)S(1)} copy-done((f32[1,2,4,4096]{3,2,1,0:T(4,128)S(1)}, f32[1,2,4,4096]{3,2,1,0:T(4,128)}, u32[]{:S(2)}) %copy-start.4) | copy-done | bytes 131096
  32.7 5.9 %three_panels.1 = (f32[12,32,128]{2,1,0:T(8,128)S(1)}, f32[12,32,128]{2,1,0:T(8,128)S(1)}, bf16[256,256]{1,0:T(8,128)(2,1)S(1)}, bf16[256,256]{1,0:T(8,128)(2,1)S(1)}) custom-call(s32[8]{0:T(128)S(1)} %stack.39.meta, s32[4,2,24]{2,1,0:T(2,128)S(1)} %bitcast.22, s32[4,2,24]{2,1,0:T(2,128)S(1)} %bitcast.25, s32[4,2,24]{2,1,0:T(2,128)S(1)} %bitcast.28, ...), custom_call_target="tpu_custom_call" | custom-call | flops 3000000000 | bytes 4194304 | tf_op jit(solution)/shard_map/three_panels/pallas_call | solution.py:225
  38.7 0.0 collective-permute-done.8.right
  38.7 1.6 %far_panel.1 = f32[12,32,128]{2,1,0:T(8,128)S(1)} custom-call(s32[8]{0:T(128)S(1)} %stack.39.meta, s32[4,2,24]{2,1,0:T(2,128)S(1)} %get-tuple-element.15.far_l.l, s32[4,2,24]{2,1,0:T(2,128)S(1)} %get-tuple-element.14.far_r.r, s32[4,2,24]{2,1,0:T(2,128)S(1)} %get-tuple-element.13.far_s.s, s32[4,2]{1,0:T(4,128)S(1)} %copy.19.far_n.n, ...), custom_call_target="tpu_custom_call" | custom-call | flops 1000000000 | bytes 4194304 | tf_op jit(solution)/shard_map/far_panel/pallas_call | solution.py:231
  40.3 0.1 collective-permute-start.9
  40.3 1.6 %near_panel.1 = f32[12,32,128]{2,1,0:T(8,128)S(1)} custom-call(s32[8]{0:T(128)S(1)} %stack.39.meta, s32[4,2,24]{2,1,0:T(2,128)S(1)} %bitcast.23, s32[4,2,24]{2,1,0:T(2,128)S(1)} %bitcast.26, s32[4,2,24]{2,1,0:T(2,128)S(1)} %bitcast.29, s32[4,2]{1,0:T(4,128)S(1)} %copy.20.near_n.n, bf16[256,256]{1,0:T(8,128)(2,1)S(1)} %get-tuple-element.9.left, ...), custom_call_target="tpu_custom_call" | custom-call | flops 1000000000 | bytes 4194304 | tf_op jit(solution)/shard_map/near_panel/pallas_call | solution.py:235
  41.9 10.0 %collective-permute-done.9 = f32[12,32,128]{2,1,0:T(8,128)S(1)} collective-permute-done((f32[12,32,128]{2,1,0:T(8,128)S(1)}, f32[12,32,128]{2,1,0:T(8,128)S(1)}, u32[]{:S(2)}, u32[]{:S(2)}) %collective-permute-start.9) | collective-permute-done | bytes 196640 | tf_op jit(solution)/shard_map/ppermute | solution.py:188
  51.9 0.7 %add.35 = f32[12,32,128]{2,1,0:T(8,128)} add(f32[12,32,128]{2,1,0:T(8,128)S(1)} %near_panel.1, f32[12,32,128]{2,1,0:T(8,128)S(1)} %collective-permute-done.9) | non-fusion elementwise | flops 49152 | bytes 589824 | tf_op jit(solution)/shard_map/add | solution.py:238
Async XLA Ops:
  0.0 10.5 %collective-permute-start.1 = (f32[2,128,128]{2,1,0:T(8,128)}, f32[2,128,128]{2,1,0:T(8,128)S(1)}, u32[]{:S(2)}, u32[]{:S(2)}) collective-permute-start(f32[2,128,128]{2,1,0:T(8,128)} %bitcast.34), channel_id=1, source_target_pairs={{0,2},{1,3},{2,18},{3,19},{4,6},{5,7},{6,22},{7,23},{8,10},{9,11},... | collective-permute-start | bytes 393224 | tf_op jit(solution)/shard_map/ppermute | solution.py:188
  2.9 18.9 %collective-permute-start.2 = (f32[2,128,128]{2,1,0:T(8,128)}, f32[2,128,128]{2,1,0:T(8,128)S(1)}, u32[]{:S(2)}, u32[]{:S(2)}) collective-permute-start(f32[2,128,128]{2,1,0:T(8,128)} %bitcast.35), channel_id=1, source_target_pairs={{0,1},{1,0},{2,3},{3,2},{4,5},{5,4},{6,7},{7,6},{8,9},{9,8},{10,11... | collective-permute-start | bytes 393224 | tf_op jit(solution)/shard_map/ppermute | solution.py:188
  10.6 15.5 %collective-permute-start.3 = (f32[2,128,128]{2,1,0:T(8,128)S(1)}, f32[2,128,128]{2,1,0:T(8,128)S(1)}, u32[]{:S(2)}, u32[]{:S(2)}) collective-permute-start(f32[2,128,128]{2,1,0:T(8,128)S(1)} %collective-permute-done.1.q1), channel_id=1, source_target_pairs={{0,1},{1,0},{2,3},{3,2},{4,5},{5,4},{6,7},{7,6},{8,9},{9,8},{10,11... | collective-permute-start | bytes 393224 | tf_op jit(solution)/shard_map/ppermute | solution.py:188
  10.6 1.6 %copy-start.5 = (s32[1,1,4,2]{2,3,1,0:T(2,128)S(1)}, s32[1,1,4,2]{2,3,1,0:T(2,128)}, u32[]{:S(2)}) copy-start(s32[1,1,4,2]{2,3,1,0:T(2,128)} %param.11) | copy-start | bytes 100
  10.6 21.3 %collective-permute-start.6 = (f32[20,32,128]{2,1,0:T(8,128)}, f32[20,32,128]{2,1,0:T(8,128)S(1)}, u32[]{:S(2)}, u32[]{:S(2)}) collective-permute-start(f32[20,32,128]{2,1,0:T(8,128)} %bitcast.30), channel_id=1, source_target_pairs={{0,4},{1,5},{2,6},{3,7},{4,0},{5,1},{6,2},{7,3},{8,12},{9,13},{10,... | collective-permute-start | bytes 983048 | tf_op jit(solution)/shard_map/ppermute | solution.py:188
  12.1 19.7 %collective-permute-start.7 = (f32[20,32,128]{2,1,0:T(8,128)}, f32[20,32,128]{2,1,0:T(8,128)S(1)}, u32[]{:S(2)}, u32[]{:S(2)}) collective-permute-start(f32[20,32,128]{2,1,0:T(8,128)} %bitcast.31), channel_id=1, source_target_pairs={{0,8},{1,9},{2,10},{3,11},{4,12},{5,13},{6,14},{7,15},{8,0},{9,1},... | collective-permute-start | bytes 983048 | tf_op jit(solution)/shard_map/ppermute | solution.py:188
  12.1 0.7 %copy-start.2 = (s32[1,1,4,2,24]{4,3,2,1,0:T(2,128)S(1)}, s32[1,1,4,2,24]{4,3,2,1,0:T(2,128)}, u32[]{:S(2)}) copy-start(s32[1,1,4,2,24]{4,3,2,1,0:T(2,128)} %param.10) | copy-start | bytes 2308
  12.1 0.7 %copy-start.1 = (s32[1,1,4,2,24]{4,3,2,1,0:T(2,128)S(1)}, s32[1,1,4,2,24]{4,3,2,1,0:T(2,128)}, u32[]{:S(2)}) copy-start(s32[1,1,4,2,24]{4,3,2,1,0:T(2,128)} %param.9) | copy-start | bytes 2308
  12.2 0.7 %copy-start = (s32[1,1,4,2,24]{4,3,2,1,0:T(2,128)S(1)}, s32[1,1,4,2,24]{4,3,2,1,0:T(2,128)}, u32[]{:S(2)}) copy-start(s32[1,1,4,2,24]{4,3,2,1,0:T(2,128)} %param.8) | copy-start | bytes 2308
  12.2 19.6 %copy-start.3 = (f32[1,1,20,4096]{3,1,2,0:T(1,128)S(1)}, f32[1,1,20,4096]{3,1,2,0:T(1,128)}, u32[]{:S(2)}) copy-start(f32[1,1,20,4096]{3,1,2,0:T(1,128)} %param.7) | copy-start | bytes 983044
  13.0 7.2 %collective-permute-start = (s32[4,2,73]{2,1,0:T(2,128)S(1)}, s32[4,2,73]{2,1,0:T(2,128)S(1)}, u32[]{:S(2)}, u32[]{:S(2)}) collective-permute-start(s32[4,2,73]{2,1,0:T(2,128)S(1)} %pad_add_fusion), channel_id=1, source_target_pairs={{0,16},{1,17},{2,18},{3,19},{4,20},{5,21},{6,22},{7,23},{8,24},{9,... | collective-permute-start | bytes 7016 | tf_op jit(solution)/shard_map/ppermute | solution.py:188
  20.2 18.5 %collective-permute-start.8 = (f32[20,32,128]{2,1,0:T(8,128)}, f32[20,32,128]{2,1,0:T(8,128)S(1)}, u32[]{:S(2)}, u32[]{:S(2)}) collective-permute-start(f32[20,32,128]{2,1,0:T(8,128)} %bitcast.32), channel_id=1, source_target_pairs={{0,12},{1,13},{2,14},{3,15},{4,8},{5,9},{6,10},{7,11},{8,4},{9,5},... | collective-permute-start | bytes 983048 | tf_op jit(solution)/shard_map/ppermute | solution.py:188
  21.8 7.7 %collective-permute-start.4 = (f32[2,128,128]{2,1,0:T(8,128)S(1)}, f32[2,128,128]{2,1,0:T(8,128)S(1)}, u32[]{:S(2)}, u32[]{:S(2)}) collective-permute-start(f32[2,128,128]{2,1,0:T(8,128)S(1)} %collective-permute-done.1.q1), channel_id=1, source_target_pairs={{0,2},{1,3},{2,0},{3,1},{4,6},{5,7},{6,4},{7,5},{8,10},{9,11},{10,... | collective-permute-start | bytes 393224 | tf_op jit(solution)/shard_map/ppermute | solution.py:188
  26.1 5.8 %collective-permute-start.5 = (f32[2,128,128]{2,1,0:T(8,128)S(1)}, f32[2,128,128]{2,1,0:T(8,128)S(1)}, u32[]{:S(2)}, u32[]{:S(2)}) collective-permute-start(f32[2,128,128]{2,1,0:T(8,128)S(1)} %collective-permute-done.1.q1), channel_id=1, source_target_pairs={{0,3},{1,2},{2,1},{3,0},{4,7},{5,6},{6,5},{7,4},{8,11},{9,10},{10,... | collective-permute-start | bytes 393224 | tf_op jit(solution)/shard_map/ppermute | solution.py:188
  31.8 0.9 %copy-start.4 = (f32[1,2,4,4096]{3,2,1,0:T(4,128)S(1)}, f32[1,2,4,4096]{3,2,1,0:T(4,128)}, u32[]{:S(2)}) copy-start(f32[1,2,4,4096]{3,2,1,0:T(4,128)} %param.6) | copy-start | bytes 393220
  40.3 11.7 %collective-permute-start.9 = (f32[12,32,128]{2,1,0:T(8,128)S(1)}, f32[12,32,128]{2,1,0:T(8,128)S(1)}, u32[]{:S(2)}, u32[]{:S(2)}) collective-permute-start(f32[12,32,128]{2,1,0:T(8,128)S(1)} %far_panel.1), channel_id=1, source_target_pairs={{0,16},{1,17},{2,18},{3,19},{4,20},{5,21},{6,22},{7,23},{8,24},{9,... | collective-permute-start | bytes 589832 | tf_op jit(solution)/shard_map/ppermute | solution.py:188

commit v2 on v1

v2 whole, which is shorter than its diff:
```python
import functools

import jax
import jax.numpy as jnp
from jax import lax
from jax.experimental import pallas as pl
from jax.experimental.pallas import tpu as pltpu
from jax.sharding import PartitionSpec as P

TILE_SIDE = 64
LEFT_SLOTS = 4
RIGHT_SLOTS = 20
SINK_SLOTS = 12
PRODUCTS = 24
SECTIONS = 4
HALF = TILE_SIDE // 2
LANES = 2 * TILE_SIDE
LEFT_ROWS = 2 * LEFT_SLOTS * HALF
LIST_ROWS = 32
AXES = ("row", "col")
MIB = 1 << 20


def in_low_half(shape):
    return lax.broadcasted_iota(jnp.int32, shape, 1) % LANES < TILE_SIDE


def spread_table():
    shape = (2 * LANES, 8 * TILE_SIDE)
    source = lax.broadcasted_iota(jnp.int32, shape, 0)
    target = lax.broadcasted_iota(jnp.int32, shape, 1)
    place = target % TILE_SIDE
    part = target // TILE_SIDE % 2
    odd_row = target // (4 * TILE_SIDE)
    inner = 2 * (place % HALF) + place // HALF
    return (source == part * LANES + odd_row * TILE_SIDE + inner).astype(jnp.bfloat16)


def spread_left(blocks, table):
    high = blocks.astype(jnp.bfloat16)
    low = (blocks - high.astype(jnp.float32)).astype(jnp.bfloat16)
    both = jnp.concatenate([high, low], axis=1)
    wide = jnp.dot(both, table, preferred_element_type=jnp.float32).astype(jnp.bfloat16)
    return jnp.concatenate([wide[:, : 4 * TILE_SIDE], wide[:, 4 * TILE_SIDE :]], axis=0)


def slots_in_order(panel_ref, half):
    first = half * LEFT_SLOTS * HALF
    return jnp.concatenate(
        [panel_ref[pl.ds(first + slot, HALF, stride=LEFT_SLOTS), :] for slot in range(LEFT_SLOTS)], axis=0
    )


def right_pair(first, second):
    low_half = in_low_half((HALF, LANES))
    first_turned = pltpu.roll(first, TILE_SIDE, 1)
    second_turned = pltpu.roll(second, TILE_SIDE, 1)
    even = jnp.where(low_half, first, second_turned)
    odd = jnp.where(low_half, first_turned, second)
    rows = jnp.concatenate([even, odd], axis=0)
    high = rows.astype(jnp.bfloat16)
    low = (rows - high.astype(jnp.float32)).astype(jnp.bfloat16)
    return jnp.concatenate([high, high, low, low], axis=0)


def all_products(lefts, right_ref, product_refs):
    rows = LEFT_SLOTS * HALF
    left = lefts[0] if len(lefts) == 1 else jnp.concatenate(lefts, axis=0)
    low_half = in_low_half((HALF, LANES))
    for slot in range(0, RIGHT_SLOTS, 4):
        weights = jnp.concatenate(
            [right_pair(right_ref[slot + n], right_ref[slot + n + 1]) for n in (0, 2)], axis=1
        )
        result = jnp.dot(left, weights, preferred_element_type=jnp.float32)
        for t, product_ref in enumerate(product_refs):
            for l in range(LEFT_SLOTS):
                for n in (0, 2):
                    start = t * 2 * rows + l * HALF
                    even = result[start : start + HALF, n * TILE_SIDE : (n + 2) * TILE_SIDE]
                    odd = result[start + rows : start + rows + HALF, n * TILE_SIDE : (n + 2) * TILE_SIDE]
                    place = l * RIGHT_SLOTS + slot + n
                    product_ref[place] = jnp.where(low_half, even, pltpu.roll(odd, TILE_SIDE, 1))
                    product_ref[place + 1] = jnp.where(low_half, pltpu.roll(even, TILE_SIDE, 1), odd)


def add_listed(total_ref, product_ref, lists, section, half):
    for p in range(PRODUCTS):
        product, sink = lists.entry(section, half, p)
        total_ref[sink] += product_ref[product]


class OwnLists:
    def __init__(self, refs):
        self.refs = refs

    def entry(self, section, half, p):
        left, right, sink = (ref[section, half, p] for ref in self.refs[:3])
        live = self.refs[3][section, half]
        return left * RIGHT_SLOTS + right, jnp.where(p < live, sink, SINK_SLOTS)


class SentLists:
    def __init__(self, panel_ref, whole, numbers, semaphore):
        left, right, sink, live = (
            panel_ref[LEFT_ROWS + 8 * n : LEFT_ROWS + 8 * (n + 1), :].astype(jnp.int32) for n in range(4)
        )
        here = lax.broadcasted_iota(jnp.int32, left.shape, 1) < live
        whole[...] = (left * RIGHT_SLOTS + right) * 16 + jnp.where(here, sink, SINK_SLOTS)
        copy = pltpu.make_async_copy(whole, numbers, semaphore)
        copy.start()
        copy.wait()
        self.numbers = numbers

    def entry(self, section, half, p):
        number = self.numbers[section * 2 + half, p]
        return number >> 4, number & 15


class Place:
    def __init__(self):
        self.cols = lax.axis_size("col")
        row, self.col = lax.axis_index("row"), lax.axis_index("col")
        self.pair, self.half = row // 2, row % 2
        self.inside = self.col // 2 == self.pair // 2

    def which_left(self, level):
        return (self.pair + self.col + level) % 2

    def section(self, level, far):
        target = self.pair ^ 3 if far else self.pair
        return ((self.pair ^ level) - target - self.col + 2 * self.cols) % self.cols


def stage_kernel(left, left_list, right_list, sink_list, counts, left_out, rows_out, semaphore):
    copy = pltpu.make_async_copy(left, left_out, semaphore)
    copy.start()
    rows_out[...] = jnp.zeros_like(rows_out)
    for n, ref in enumerate((left_list, right_list, sink_list)):
        for section in range(SECTIONS):
            start = 8 * n + 2 * section
            rows_out[start : start + 2, :PRODUCTS] = ref[section].astype(jnp.float32)
    live = counts[...].astype(jnp.float32)
    for section in range(SECTIONS):
        for half in range(2):
            row = 24 + 2 * section + half
            one = live[section : section + 1, half : half + 1]
            rows_out[row : row + 1, :] = jnp.broadcast_to(one, (1, LANES))
    copy.wait()


def pick_kernel(left, beside, rows, near_out, far_out):
    inside = Place().inside

    @pl.when(inside)
    def _():
        near_out[...] = left[...]
        far_out[:LEFT_ROWS, :] = beside[...]

    @pl.when(jnp.logical_not(inside))
    def _():
        near_out[...] = beside[...]
        far_out[:LEFT_ROWS, :] = left[...]

    far_out[LEFT_ROWS:, :] = rows[...]


def spread_panels(lefts, panels):
    table = spread_table()
    for which, panel in enumerate(panels):
        for half in range(2):
            lefts[which, half] = spread_left(slots_in_order(panel, half), table)


def add_panels(panels, product_ref, total_ref, lists, lefts, place, far):
    for blocks, level, half in panels:
        all_products([lefts[place.which_left(level), half]], blocks, [product_ref])
        add_listed(total_ref, product_ref, lists, place.section(level, far), half)


def far_kernel(
    left_a, left_b, own, right_y, right_z,
    out, left_out, lefts, total, products, whole, numbers, semaphore,
):
    lists = SentLists(left_a, whole, numbers, semaphore)
    place = Place()
    half = place.half
    spread_panels(lefts, (left_a, left_b))
    left_out[...] = lefts[place.which_left(1), 1 - half]
    total[...] = jnp.zeros_like(total)
    panels = ((own, 0, half), (right_y, 0, 1 - half), (right_z, 1, half))
    add_panels(panels, products, total, lists, lefts, place, True)
    out[...] = total[:SINK_SLOTS]


def far_last_kernel(
    left_a, left, right_0, right_1, before, out, total, products, whole, numbers, semaphore
):
    lists = SentLists(left_a, whole, numbers, semaphore)
    place = Place()
    total[:SINK_SLOTS] = before[...]
    all_products([left[...]], Joined(right_0, right_1), [products])
    add_listed(total, products, lists, place.section(1, True), 1 - place.half)
    out[...] = total[:SINK_SLOTS]


def near_kernel(
    l, r, s, n, left_a, left_b, own, right_y, right_z, right_0, right_1, out, lefts, total, products
):
    place = Place()
    half = place.half
    spread_panels(lefts, (left_a, left_b))
    total[...] = jnp.zeros_like(total)
    panels = (
        (own, 0, half), (right_y, 0, 1 - half), (right_z, 1, half), (Joined(right_0, right_1), 1, 1 - half),
    )
    add_panels(panels, products, total, OwnLists((l, r, s, n)), lefts, place, False)
    out[...] = total[:SINK_SLOTS]


class Joined:
    def __init__(self, first, second):
        self.first, self.second = first, second

    def __getitem__(self, index):
        size = self.first.shape[0]
        return self.first[index] if index < size else self.second[index - size]


def pair_kernel(l, r, s, n, left, right_0, right_1, before, out, total, products, *, section):
    table = spread_table()
    total[:SINK_SLOTS] = before[...]
    for half, right in ((0, right_0), (1, right_1)):
        all_products([spread_left(slots_in_order(left, half), table)], right, [products])
        add_listed(total, products, OwnLists((l, r, s, n)), section, half)
    out[...] = total[:SINK_SLOTS]


STAGE_COST = 2 * 10**9
PICK_COST = 0
ANY = pl.BlockSpec(memory_space=pl.ANY)
SMEM = pl.BlockSpec(memory_space=pltpu.SMEM)
VMEM = pl.BlockSpec(memory_space=pltpu.VMEM)
SUMS = (SINK_SLOTS, HALF, LANES)
TOTAL = pltpu.VMEM((SINK_SLOTS + 1, HALF, LANES), jnp.float32)
PRODUCT_TABLE = pltpu.VMEM((LEFT_SLOTS * RIGHT_SLOTS, HALF, LANES), jnp.float32)
SPREAD = (2 * LEFT_SLOTS * HALF, 4 * TILE_SIDE)


def call(kernel, specs, outs, scratch, flops, name):
    return pl.pallas_call(
        kernel,
        out_shape=outs,
        in_specs=specs,
        out_specs=jax.tree.map(lambda _: VMEM, outs),
        scratch_shapes=scratch,
        compiler_params=pltpu.CompilerParams(vmem_limit_bytes=24 * MIB),
        cost_estimate=pl.CostEstimate(flops=flops, bytes_accessed=4 * MIB, transcendentals=0),
        name=name,
    )


def sums():
    return jax.ShapeDtypeStruct(SUMS, jnp.float32)


def left_panel(more):
    return jax.ShapeDtypeStruct((LEFT_ROWS + more, LANES), jnp.float32)


def spread_shape():
    return jax.ShapeDtypeStruct(SPREAD, jnp.bfloat16)


def left_view(panels):
    return panels.reshape(2, LEFT_SLOTS, HALF, LANES).transpose(0, 2, 1, 3).reshape(LEFT_ROWS, LANES)


def grouped(left, right, lists):
    cols = lax.axis_size("col")

    def device(pair, parity, col):
        return (2 * pair + parity) * cols + col

    def send(value, to):
        where = [
            (device(pair, parity, col), device(*to(pair, parity, col)))
            for pair in range(cols)
            for parity in range(2)
            for col in range(cols)
        ]
        return lax.ppermute(value, AXES, where)

    def y_next(pair, parity, col):
        return (pair, 1 - parity, col)

    def z_next(pair, parity, col):
        return (pair ^ 1, parity, col)

    def z_far(pair, parity, col):
        return (pair ^ 3, parity, col)

    def col_next(flip):
        return lambda pair, parity, col: (pair, parity, col ^ flip)

    beside = send(left, col_next(2))
    right_y = send(right, y_next)
    right_z = send(right, z_next)
    own_left, list_rows = call(
        stage_kernel, [ANY] + [VMEM] * 4, (left_panel(0), jax.ShapeDtypeStruct((LIST_ROWS, LANES), jnp.float32)),
        [pltpu.SemaphoreType.DMA(())], STAGE_COST, "stage",
    )(left, *lists)
    near_a, far_a = call(
        pick_kernel, [VMEM] * 3, (left_panel(0), left_panel(LIST_ROWS)), [], PICK_COST, "pick"
    )(own_left, beside, list_rows)
    far_a = send(far_a, z_far)
    cut = RIGHT_SLOTS // 2
    right_0 = send(right_z[:cut], y_next)
    right_1 = send(right_y[cut:], z_next)
    far_b = send(far_a, col_next(1))
    near_b = send(near_a, col_next(1))

    spread = pltpu.VMEM((2, 2) + SPREAD, jnp.bfloat16)
    sent = [
        pltpu.VMEM((8, LANES), jnp.int32),
        pltpu.SMEM((8, LANES), jnp.int32),
        pltpu.SemaphoreType.DMA(()),
    ]
    far, far_left = call(
        far_kernel, [VMEM] * 5, (sums(), spread_shape()), [spread, TOTAL, PRODUCT_TABLE, *sent], 0, "far_three"
    )(far_a, far_b, right, right_y, right_z)
    far = call(far_last_kernel, [VMEM] * 5, sums(), [TOTAL, PRODUCT_TABLE, *sent], 10**9, "far_last")(
        far_a, far_left, right_0, right_1, far
    )
    received = send(far, z_far)
    near = call(near_kernel, [SMEM] * 4 + [VMEM] * 7, sums(), [spread, TOTAL, PRODUCT_TABLE], 3 * 10**9, "near_all")(
        *lists, near_a, near_b, right, right_y, right_z, right_0, right_1
    )
    return near + received


def shifted(shard, axis, by):
    devices = lax.axis_size(axis)
    return lax.ppermute(shard, axis, [(i, (i + by) % devices) for i in range(devices)])


def windowed(left, right, lists):
    cols = lax.axis_size("col")
    half_row, parity = lax.axis_index("row") // 2, lax.axis_index("row") % 2
    column = lax.axis_index("col")
    bits = cols.bit_length() - 1
    for bit in range(bits):
        right = jnp.where(column // (1 << bit) % 2 == 1, shifted(right, "row", -(2 << bit)), right)
        left = jnp.where(half_row // (1 << bit) % 2 == 1, shifted(left, "col", -(1 << bit)), left)
    total = jnp.zeros(SUMS, jnp.float32)
    for section in range(SECTIONS):
        swap = [(i, i ^ 1) for i in range(lax.axis_size("row"))]
        partner = lax.ppermute(right, "row", swap)
        kernel = functools.partial(pair_kernel, section=section)
        total = call(kernel, [SMEM] * 4 + [VMEM] * 4, sums(), [TOTAL, PRODUCT_TABLE], 2 * 10**9, "panel_pair")(
            *lists, left,
            jnp.where(parity == 0, right, partner), jnp.where(parity == 0, partner, right), total,
        )
        if section + 1 < SECTIONS:
            right = shifted(right, "row", -2)
            left = shifted(left, "col", -1)
    return total


def per_device(left_blocks, right_blocks, left_slots, right_slots, sink_slots, live_counts):
    left = left_view(left_blocks[0])
    right = right_blocks.reshape(RIGHT_SLOTS, HALF, LANES)
    lists = (left_slots[0, 0], right_slots[0, 0], sink_slots[0, 0], live_counts[0, 0])
    plan = grouped if lax.axis_size("col") == SECTIONS == 4 else windowed
    return plan(left, right, lists).reshape(1, 1, SINK_SLOTS, TILE_SIDE * TILE_SIDE)


def solution(mesh):
    return jax.shard_map(
        per_device,
        mesh=mesh,
        in_specs=(
            P("row", "col", None, None),
            P("row", "col", None, None),
            P("row", "col", None, None, None),
            P("row", "col", None, None, None),
            P("row", "col", None, None, None),
            P("row", "col", None, None),
        ),
        out_specs=P("row", "col", None, None),
        check_vma=False,
    )
```

time: 52.8 us -> 33.4 us (0.63)
  waiting for transfers between devices: 29.6 us -> 6.09 us
  starting transfers between devices: 10.9 us -> 14.9 us
  local copies, waits for them, and re-layouts: 2.21 us -> 1.64 us
    ppermute x10 -> x9, waiting for transfers between devices: 29.6 us -> 6.09 us  [send(): return lax.ppermute(value, AXES, where)]
    ppermute x10 -> x9, starting transfers between devices: 10.9 us -> 14.9 us  [send(): return lax.ppermute(value, AXES, where)]
    pallas_call x3 -> x5, Pallas kernels: 9.09 us -> 9.33 us  [the longest x1 4.83 us: grouped(): call(near_kernel, [SMEM] * 4 + [VMEM] * 7, sums(), [spread, TOTAL, PRODUC...]
  transfers between devices with their start and end apart: 10 -> 9, of which waited for: 5 -> 4; matrix products, arithmetic and copies ran while one was open for 1% -> 0% of each run, Pallas kernels for 14% -> 28%
where the time goes in v2:
time: 33.4 us; the launch traced here: 32.8 us
  starting transfers between devices  14.9 us (45%)
  Pallas kernels  9.33 us (28%)
  waiting for transfers between devices  6.09 us (18%)
  local copies, waits for them, and re-layouts  1.64 us (5%)
  other arithmetic  0.7 us (2%)
    ppermute x9, starting transfers between devices, send(): return lax.ppermute(value, AXES, where)  14.9 us
    ppermute x9, waiting for transfers between devices, send(): return lax.ppermute(value, AXES, where)  6.09 us
    pallas_call x1, Pallas kernels, grouped(): call(near_kernel, [SMEM] * 4 + [VMEM] * 7, sums(), [spread, TOTAL, PRODUC...  4.83 us
    pallas_call x1, Pallas kernels, grouped(): call(far_kernel, [VMEM] * 5, (sums(), spread_shape()), [spread, TOTAL, PR...  2.81 us
    unnamed x12, local copies, waits for them, and re-layouts  1.52 us
    pallas_call x1, Pallas kernels, grouped(): call(far_last_kernel, [VMEM] * 5, sums(), [TOTAL, PRODUCT_TABLE, *sent],...  1.45 us
    add x1, other arithmetic, grouped(): return near + received  0.7 us
  transfers between devices with their start and end apart: 9, of which 4 were waited for; matrix products, arithmetic and copies ran while one was open for 0% of the time, Pallas kernels for 28%

profile of v2, /device:TPU:0, one launch (start us, length us, event | category | flops | bytes accessed | tf_op | source)
XLA Modules:
  0.0 32.8 jit_solution(16136245935771930125)
XLA Ops:
  0.0 0.0 copy-start.5
  0.0 3.0 %collective-permute-start.3 = (f32[20,32,128]{2,1,0:T(8,128)}, f32[20,32,128]{2,1,0:T(8,128)S(1)}, u32[]{:S(2)}, u32[]{:S(2)}) collective-permute-start(f32[20,32,128]{2,1,0:T(8,128)} %bitcast.11), channel_id=1, source_target_pairs={{0,8},{1,9},{2,10},{3,11},{4,12},{5,13},{6,14},{7,15},{8,0},{9,1},... | collective-permute-start | bytes 983048 | tf_op jit(solution)/shard_map/ppermute | solution.py:291
  3.0 1.5 %collective-permute-start.2 = (f32[20,32,128]{2,1,0:T(8,128)}, f32[20,32,128]{2,1,0:T(8,128)S(1)}, u32[]{:S(2)}, u32[]{:S(2)}) collective-permute-start(f32[20,32,128]{2,1,0:T(8,128)} %bitcast.12), channel_id=1, source_target_pairs={{0,4},{1,5},{2,6},{3,7},{4,0},{5,1},{6,2},{7,3},{8,12},{9,13},{10,... | collective-permute-start | bytes 983048 | tf_op jit(solution)/shard_map/ppermute | solution.py:291
  4.5 0.0 copy-start.4
  4.5 1.5 %collective-permute-start = (f32[256,128]{1,0:T(8,128)}, f32[256,128]{1,0:T(8,128)S(1)}, u32[]{:S(2)}, u32[]{:S(2)}) collective-permute-start(f32[256,128]{1,0:T(8,128)} %bitcast.15), channel_id=1, source_target_pairs={{0,2},{1,3},{2,0},{3,1},{4,6},{5,7},{6,4},{7,5},{8,10},{9,11},{10,... | collective-permute-start | bytes 393224 | tf_op jit(solution)/shard_map/ppermute | solution.py:291
  6.0 0.0 copy-done.5
  6.0 0.0 copy-start.2
  6.0 0.0 copy-start.3
  6.0 0.1 copy.13.counts.n
  6.1 0.0 copy-done.4
  6.1 0.6 %copy-done.2 = s32[1,1,4,2,24]{4,3,2,1,0:T(2,128)S(1)} copy-done((s32[1,1,4,2,24]{4,3,2,1,0:T(2,128)S(1)}, s32[1,1,4,2,24]{4,3,2,1,0:T(2,128)}, u32[]{:S(2)}) %copy-start.2) | copy-done | bytes 792
  6.7 0.0 copy-done.3
  6.7 0.0 copy-start.1
  6.7 0.9 %copy-done.1 = f32[1,2,4,4096]{3,2,1,0:T(4,128)S(1)} copy-done((f32[1,2,4,4096]{3,2,1,0:T(4,128)S(1)}, f32[1,2,4,4096]{3,2,1,0:T(4,128)}, u32[]{:S(2)}) %copy-start.1) | copy-done | bytes 131096
  7.7 0.2 stage.1
  7.9 1.9 %collective-permute-done.beside = f32[256,128]{1,0:T(8,128)S(1)} collective-permute-done((f32[256,128]{1,0:T(8,128)}, f32[256,128]{1,0:T(8,128)S(1)}, u32[]{:S(2)}, u32[]{:S(2)}) %collective-permute-start) | collective-permute-done | bytes 131104 | tf_op jit(solution)/shard_map/ppermute | solution.py:291
  9.8 0.0 copy-start
  9.8 2.5 %collective-permute-start.6 = (f32[288,128]{1,0:T(8,128)S(1)}, f32[288,128]{1,0:T(8,128)S(1)}, u32[]{:S(2)}, u32[]{:S(2)}) collective-permute-start(f32[288,128]{1,0:T(8,128)S(1)} %get-tuple-element.14), channel_id=1, source_target_pairs={{0,24},{1,25},{2,26},{3,27},{4,28},{5,29},{6,30},{7,31},{8,16},{9,... | collective-permute-start | bytes 442376 | tf_op jit(solution)/shard_map/ppermute | solution.py:291
  12.3 0.0 collective-permute-done.3.right_z
  12.3 0.6 %collective-permute-start.4 = (f32[10,32,128]{2,1,0:T(8,128)S(1)}, f32[10,32,128]{2,1,0:T(8,128)S(1)}, u32[]{:S(2)}, u32[]{:S(2)}) collective-permute-start(f32[10,32,128]{2,1,0:T(8,128)S(1)} %slice.8), channel_id=1, source_target_pairs={{0,4},{1,5},{2,6},{3,7},{4,0},{5,1},{6,2},{7,3},{8,12},{9,13},{10,... | collective-permute-start | bytes 491528 | tf_op jit(solution)/shard_map/ppermute | solution.py:291
  12.9 0.0 collective-permute-done.2.right_y
  12.9 1.8 %collective-permute-start.5 = (f32[10,32,128]{2,1,0:T(8,128)S(1)}, f32[10,32,128]{2,1,0:T(8,128)S(1)}, u32[]{:S(2)}, u32[]{:S(2)}) collective-permute-start(f32[10,32,128]{2,1,0:T(8,128)S(1)} %slice.9), channel_id=1, source_target_pairs={{0,8},{1,9},{2,10},{3,11},{4,12},{5,13},{6,14},{7,15},{8,0},{9,1},... | collective-permute-start | bytes 491528 | tf_op jit(solution)/shard_map/ppermute | solution.py:291
  14.7 2.8 %collective-permute-done.6.left_a = f32[288,128]{1,0:T(8,128)S(1)} collective-permute-done((f32[288,128]{1,0:T(8,128)S(1)}, f32[288,128]{1,0:T(8,128)S(1)}, u32[]{:S(2)}, u32[]{:S(2)}) %collective-permute-start.6) | collective-permute-done | bytes 147488 | tf_op jit(solution)/shard_map/ppermute | solution.py:291
  17.5 0.0 collective-permute-start.7
  17.5 0.5 %collective-permute-start.1 = (f32[256,128]{1,0:T(8,128)S(1)}, f32[256,128]{1,0:T(8,128)S(1)}, u32[]{:S(2)}, u32[]{:S(2)}) collective-permute-start(f32[256,128]{1,0:T(8,128)S(1)} %get-tuple-element.13.left_a), channel_id=1, source_target_pairs={{0,1},{1,0},{2,3},{3,2},{4,5},{5,4},{6,7},{7,6},{8,9},{9,8},{10,11... | collective-permute-start | bytes 393224 | tf_op jit(solution)/shard_map/ppermute | solution.py:291
  18.0 0.9 %collective-permute-done.7.left_b = f32[288,128]{1,0:T(8,128)S(1)} collective-permute-done((f32[288,128]{1,0:T(8,128)S(1)}, f32[288,128]{1,0:T(8,128)S(1)}, u32[]{:S(2)}, u32[]{:S(2)}) %collective-permute-start.7) | collective-permute-done | bytes 147488 | tf_op jit(solution)/shard_map/ppermute | solution.py:291
  18.8 0.0 copy-done
  18.8 2.8 %far_three.1 = (f32[12,32,128]{2,1,0:T(8,128)S(1)}, bf16[256,256]{1,0:T(8,128)(2,1)S(1)}) custom-call(f32[288,128]{1,0:T(8,128)S(1)} %collective-permute-done.6.left_a, f32[288,128]{1,0:T(8,128)S(1)} %collective-permute-done.7.left_b, f32[20,32,128]{2,1,0:T(8,128)S(1)} %bitcast.13, f32[20,32,128]{2,1,0:T(8,128)S(1)} %collective-permute-done.2.right_y, ...), custom_call_target="tpu_custom_call" | custom-call | bytes 4194304 | tf_op jit(solution)/shard_map/far_three/pallas_call | solution.py:328
  21.7 0.0 collective-permute-done.4.right_0
  21.7 0.0 collective-permute-done.5.right_1
  21.7 1.4 %far_last.1 = f32[12,32,128]{2,1,0:T(8,128)S(1)} custom-call(f32[288,128]{1,0:T(8,128)S(1)} %collective-permute-done.6.left_a, bf16[256,256]{1,0:T(8,128)(2,1)S(1)} %get-tuple-element.15.left, f32[10,32,128]{2,1,0:T(8,128)S(1)} %collective-permute-done.4.right_0, f32[10,32,128]{2,1,0:T(8,128)S(1)} %collective-permute-done.5.right_1, ...), custom_call_target="tpu_custom_call" | custom-call | flops 1000000000 | bytes 4194304 | tf_op jit(solution)/shard_map/far_last/pallas_call | solution.py:331
  23.1 3.5 %collective-permute-start.8 = (f32[12,32,128]{2,1,0:T(8,128)S(1)}, f32[12,32,128]{2,1,0:T(8,128)S(1)}, u32[]{:S(2)}, u32[]{:S(2)}) collective-permute-start(f32[12,32,128]{2,1,0:T(8,128)S(1)} %far_last.1), channel_id=1, source_target_pairs={{0,24},{1,25},{2,26},{3,27},{4,28},{5,29},{6,30},{7,31},{8,16},{9,... | collective-permute-start | bytes 589832 | tf_op jit(solution)/shard_map/ppermute | solution.py:291
  26.6 0.0 collective-permute-done.1.left_b
  26.6 4.8 %near_all.1 = f32[12,32,128]{2,1,0:T(8,128)S(1)} custom-call(s32[4,2,24]{2,1,0:T(2,128)S(1)} %bitcast.18, s32[4,2,24]{2,1,0:T(2,128)S(1)} %bitcast.20, s32[4,2,24]{2,1,0:T(2,128)S(1)} %bitcast.22, s32[4,2]{1,0:T(4,128)S(1)} %copy.13.counts.n, f32[256,128]{1,0:T(8,128)S(1)} %get-tuple-element.13.left_a, f32[256,128]{1,0:T(8,128)S(1)} %collective-permute-done.1.left_b, ...), custom_call_target="tpu_custom_call" | custom-call | flops 3000000000 | bytes 4194304 | tf_op jit(solution)/shard_map/near_all/pallas_call | solution.py:335
  31.5 0.6 %collective-permute-done.8 = f32[12,32,128]{2,1,0:T(8,128)S(1)} collective-permute-done((f32[12,32,128]{2,1,0:T(8,128)S(1)}, f32[12,32,128]{2,1,0:T(8,128)S(1)}, u32[]{:S(2)}, u32[]{:S(2)}) %collective-permute-start.8) | collective-permute-done | bytes 196640 | tf_op jit(solution)/shard_map/ppermute | solution.py:291
  32.1 0.7 %add.3 = f32[12,32,128]{2,1,0:T(8,128)} add(f32[12,32,128]{2,1,0:T(8,128)S(1)} %near_all.1, f32[12,32,128]{2,1,0:T(8,128)S(1)} %collective-permute-done.8) | non-fusion elementwise | flops 49152 | bytes 589824 | tf_op jit(solution)/shard_map/add | solution.py:338
  (3 shorter events, 0.0 us)
Async XLA Ops:
  0.0 6.0 %copy-start.5 = (s32[1,1,4,2]{2,3,1,0:T(2,128)S(1)}, s32[1,1,4,2]{2,3,1,0:T(2,128)}, u32[]{:S(2)}) copy-start(s32[1,1,4,2]{2,3,1,0:T(2,128)} %param.11) | copy-start | bytes 100
  0.0 12.3 %collective-permute-start.3 = (f32[20,32,128]{2,1,0:T(8,128)}, f32[20,32,128]{2,1,0:T(8,128)S(1)}, u32[]{:S(2)}, u32[]{:S(2)}) collective-permute-start(f32[20,32,128]{2,1,0:T(8,128)} %bitcast.11), channel_id=1, source_target_pairs={{0,8},{1,9},{2,10},{3,11},{4,12},{5,13},{6,14},{7,15},{8,0},{9,1},... | collective-permute-start | bytes 983048 | tf_op jit(solution)/shard_map/ppermute | solution.py:291
  3.0 9.9 %collective-permute-start.2 = (f32[20,32,128]{2,1,0:T(8,128)}, f32[20,32,128]{2,1,0:T(8,128)S(1)}, u32[]{:S(2)}, u32[]{:S(2)}) collective-permute-start(f32[20,32,128]{2,1,0:T(8,128)} %bitcast.12), channel_id=1, source_target_pairs={{0,4},{1,5},{2,6},{3,7},{4,0},{5,1},{6,2},{7,3},{8,12},{9,13},{10,... | collective-permute-start | bytes 983048 | tf_op jit(solution)/shard_map/ppermute | solution.py:291
  4.5 1.6 %copy-start.4 = (s32[1,1,4,2,24]{4,3,2,1,0:T(2,128)S(1)}, s32[1,1,4,2,24]{4,3,2,1,0:T(2,128)}, u32[]{:S(2)}) copy-start(s32[1,1,4,2,24]{4,3,2,1,0:T(2,128)} %param.10) | copy-start | bytes 2308
  4.5 5.2 %collective-permute-start = (f32[256,128]{1,0:T(8,128)}, f32[256,128]{1,0:T(8,128)S(1)}, u32[]{:S(2)}, u32[]{:S(2)}) collective-permute-start(f32[256,128]{1,0:T(8,128)} %bitcast.15), channel_id=1, source_target_pairs={{0,2},{1,3},{2,0},{3,1},{4,6},{5,7},{6,4},{7,5},{8,10},{9,11},{10,... | collective-permute-start | bytes 393224 | tf_op jit(solution)/shard_map/ppermute | solution.py:291
  6.0 0.7 %copy-start.2 = (s32[1,1,4,2,24]{4,3,2,1,0:T(2,128)S(1)}, s32[1,1,4,2,24]{4,3,2,1,0:T(2,128)}, u32[]{:S(2)}) copy-start(s32[1,1,4,2,24]{4,3,2,1,0:T(2,128)} %param.8) | copy-start | bytes 2308
  6.0 0.7 %copy-start.3 = (s32[1,1,4,2,24]{4,3,2,1,0:T(2,128)S(1)}, s32[1,1,4,2,24]{4,3,2,1,0:T(2,128)}, u32[]{:S(2)}) copy-start(s32[1,1,4,2,24]{4,3,2,1,0:T(2,128)} %param.9) | copy-start | bytes 2308
  6.7 0.9 %copy-start.1 = (f32[1,2,4,4096]{3,2,1,0:T(4,128)S(1)}, f32[1,2,4,4096]{3,2,1,0:T(4,128)}, u32[]{:S(2)}) copy-start(f32[1,2,4,4096]{3,2,1,0:T(4,128)} %param.6) | copy-start | bytes 393220
  9.8 9.1 %copy-start = (f32[1,1,20,4096]{3,1,2,0:T(1,128)S(1)}, f32[1,1,20,4096]{3,1,2,0:T(1,128)}, u32[]{:S(2)}) copy-start(f32[1,1,20,4096]{3,1,2,0:T(1,128)} %param.7) | copy-start | bytes 983044
  9.8 7.7 %collective-permute-start.6 = (f32[288,128]{1,0:T(8,128)S(1)}, f32[288,128]{1,0:T(8,128)S(1)}, u32[]{:S(2)}, u32[]{:S(2)}) collective-permute-start(f32[288,128]{1,0:T(8,128)S(1)} %get-tuple-element.14), channel_id=1, source_target_pairs={{0,24},{1,25},{2,26},{3,27},{4,28},{5,29},{6,30},{7,31},{8,16},{9,... | collective-permute-start | bytes 442376 | tf_op jit(solution)/shard_map/ppermute | solution.py:291
  12.3 9.3 %collective-permute-start.4 = (f32[10,32,128]{2,1,0:T(8,128)S(1)}, f32[10,32,128]{2,1,0:T(8,128)S(1)}, u32[]{:S(2)}, u32[]{:S(2)}) collective-permute-start(f32[10,32,128]{2,1,0:T(8,128)S(1)} %slice.8), channel_id=1, source_target_pairs={{0,4},{1,5},{2,6},{3,7},{4,0},{5,1},{6,2},{7,3},{8,12},{9,13},{10,... | collective-permute-start | bytes 491528 | tf_op jit(solution)/shard_map/ppermute | solution.py:291
  12.9 8.8 %collective-permute-start.5 = (f32[10,32,128]{2,1,0:T(8,128)S(1)}, f32[10,32,128]{2,1,0:T(8,128)S(1)}, u32[]{:S(2)}, u32[]{:S(2)}) collective-permute-start(f32[10,32,128]{2,1,0:T(8,128)S(1)} %slice.9), channel_id=1, source_target_pairs={{0,8},{1,9},{2,10},{3,11},{4,12},{5,13},{6,14},{7,15},{8,0},{9,1},... | collective-permute-start | bytes 491528 | tf_op jit(solution)/shard_map/ppermute | solution.py:291
  17.5 1.4 %collective-permute-start.7 = (f32[288,128]{1,0:T(8,128)S(1)}, f32[288,128]{1,0:T(8,128)S(1)}, u32[]{:S(2)}, u32[]{:S(2)}) collective-permute-start(f32[288,128]{1,0:T(8,128)S(1)} %collective-permute-done.6.left_a), channel_id=1, source_target_pairs={{0,1},{1,0},{2,3},{3,2},{4,5},{5,4},{6,7},{7,6},{8,9},{9,8},{10,11... | collective-permute-start | bytes 442376 | tf_op jit(solution)/shard_map/ppermute | solution.py:291
  17.5 9.2 %collective-permute-start.1 = (f32[256,128]{1,0:T(8,128)S(1)}, f32[256,128]{1,0:T(8,128)S(1)}, u32[]{:S(2)}, u32[]{:S(2)}) collective-permute-start(f32[256,128]{1,0:T(8,128)S(1)} %get-tuple-element.13.left_a), channel_id=1, source_target_pairs={{0,1},{1,0},{2,3},{3,2},{4,5},{5,4},{6,7},{7,6},{8,9},{9,8},{10,11... | collective-permute-start | bytes 393224 | tf_op jit(solution)/shard_map/ppermute | solution.py:291
  23.1 8.9 %collective-permute-start.8 = (f32[12,32,128]{2,1,0:T(8,128)S(1)}, f32[12,32,128]{2,1,0:T(8,128)S(1)}, u32[]{:S(2)}, u32[]{:S(2)}) collective-permute-start(f32[12,32,128]{2,1,0:T(8,128)S(1)} %far_last.1), channel_id=1, source_target_pairs={{0,24},{1,25},{2,26},{3,27},{4,28},{5,29},{6,30},{7,31},{8,16},{9,... | collective-permute-start | bytes 589832 | tf_op jit(solution)/shard_map/ppermute | solution.py:291

commit v3 on v2

--- a/solution.py
+++ b/solution.py
@@ -17,6 +17,7 @@
 LANES = 2 * TILE_SIDE
 LEFT_ROWS = 2 * LEFT_SLOTS * HALF
 LIST_ROWS = 32
+ODD_SINKS = 16
 AXES = ("row", "col")
 MIB = 1 << 20
 
@@ -51,36 +52,47 @@
     )
 
 
+def in_parts(rows):
+    high = rows.astype(jnp.bfloat16)
+    low = (rows - high.astype(jnp.float32)).astype(jnp.bfloat16)
+    return jnp.concatenate([high, high, low, low], axis=0)
+
+
 def right_pair(first, second):
     low_half = in_low_half((HALF, LANES))
     first_turned = pltpu.roll(first, TILE_SIDE, 1)
     second_turned = pltpu.roll(second, TILE_SIDE, 1)
-    even = jnp.where(low_half, first, second_turned)
-    odd = jnp.where(low_half, first_turned, second)
-    rows = jnp.concatenate([even, odd], axis=0)
-    high = rows.astype(jnp.bfloat16)
-    low = (rows - high.astype(jnp.float32)).astype(jnp.bfloat16)
-    return jnp.concatenate([high, high, low, low], axis=0)
-
-
-def all_products(lefts, right_ref, product_refs):
+    one = [jnp.where(low_half, first, second_turned), jnp.where(low_half, first_turned, second)]
+    other = [jnp.where(low_half, second, first_turned), jnp.where(low_half, second_turned, first)]
+    return in_parts(jnp.concatenate(one, axis=0)), in_parts(jnp.concatenate(other, axis=0))
+
+
+def all_products(left, right_ref, product_ref):
     rows = LEFT_SLOTS * HALF
-    left = lefts[0] if len(lefts) == 1 else jnp.concatenate(lefts, axis=0)
     low_half = in_low_half((HALF, LANES))
     for slot in range(0, RIGHT_SLOTS, 4):
-        weights = jnp.concatenate(
-            [right_pair(right_ref[slot + n], right_ref[slot + n + 1]) for n in (0, 2)], axis=1
+        pairs = [right_pair(right_ref[slot + n], right_ref[slot + n + 1]) for n in (0, 2)]
+        even, odd = (
+            jnp.dot(part, jnp.concatenate(tables, axis=1), preferred_element_type=jnp.float32)
+            for part, tables in zip((left[:rows], left[rows:]), zip(*pairs))
         )
-        result = jnp.dot(left, weights, preferred_element_type=jnp.float32)
-        for t, product_ref in enumerate(product_refs):
-            for l in range(LEFT_SLOTS):
-                for n in (0, 2):
-                    start = t * 2 * rows + l * HALF
-                    even = result[start : start + HALF, n * TILE_SIDE : (n + 2) * TILE_SIDE]
-                    odd = result[start + rows : start + rows + HALF, n * TILE_SIDE : (n + 2) * TILE_SIDE]
-                    place = l * RIGHT_SLOTS + slot + n
-                    product_ref[place] = jnp.where(low_half, even, pltpu.roll(odd, TILE_SIDE, 1))
-                    product_ref[place + 1] = jnp.where(low_half, pltpu.roll(even, TILE_SIDE, 1), odd)
+        for l in range(LEFT_SLOTS):
+            for n in (0, 2):
+                where = (slice(l * HALF, (l + 1) * HALF), slice(n * TILE_SIDE, (n + 2) * TILE_SIDE))
+                place = l * RIGHT_SLOTS + slot + n
+                product_ref[place] = jnp.where(low_half, even[where], odd[where])
+                product_ref[place + 1] = jnp.where(low_half, odd[where], even[where])
+
+
+def start_total(total_ref, before=None):
+    total_ref[...] = jnp.zeros_like(total_ref)
+    if before is not None:
+        total_ref[:SINK_SLOTS] = before[...]
+
+
+def whole_total(total_ref):
+    turned = total_ref[ODD_SINKS : ODD_SINKS + SINK_SLOTS].reshape(SINK_SLOTS * HALF, LANES)
+    return total_ref[:SINK_SLOTS] + pltpu.roll(turned, TILE_SIDE, 1).reshape(SUMS)
 
 
 def add_listed(total_ref, product_ref, lists, section, half):
@@ -96,7 +108,7 @@
     def entry(self, section, half, p):
         left, right, sink = (ref[section, half, p] for ref in self.refs[:3])
         live = self.refs[3][section, half]
-        return left * RIGHT_SLOTS + right, jnp.where(p < live, sink, SINK_SLOTS)
+        return left * RIGHT_SLOTS + right, right % 2 * ODD_SINKS + jnp.where(p < live, sink, SINK_SLOTS)
 
 
 class SentLists:
@@ -105,7 +117,8 @@
             panel_ref[LEFT_ROWS + 8 * n : LEFT_ROWS + 8 * (n + 1), :].astype(jnp.int32) for n in range(4)
         )
         here = lax.broadcasted_iota(jnp.int32, left.shape, 1) < live
-        whole[...] = (left * RIGHT_SLOTS + right) * 16 + jnp.where(here, sink, SINK_SLOTS)
+        sink = right % 2 * ODD_SINKS + jnp.where(here, sink, SINK_SLOTS)
+        whole[...] = (left * RIGHT_SLOTS + right) * 2 * ODD_SINKS + sink
         copy = pltpu.make_async_copy(whole, numbers, semaphore)
         copy.start()
         copy.wait()
@@ -113,7 +126,7 @@
 
     def entry(self, section, half, p):
         number = self.numbers[section * 2 + half, p]
-        return number >> 4, number & 15
+        return number // (2 * ODD_SINKS), number % (2 * ODD_SINKS)
 
 
 class Place:
@@ -173,7 +186,7 @@
 
 def add_panels(panels, product_ref, total_ref, lists, lefts, place, far):
     for blocks, level, half in panels:
-        all_products([lefts[place.which_left(level), half]], blocks, [product_ref])
+        all_products(lefts[place.which_left(level), half], blocks, product_ref)
         add_listed(total_ref, product_ref, lists, place.section(level, far), half)
 
 
@@ -186,62 +199,53 @@
     half = place.half
     spread_panels(lefts, (left_a, left_b))
     left_out[...] = lefts[place.which_left(1), 1 - half]
-    total[...] = jnp.zeros_like(total)
+    start_total(total)
     panels = ((own, 0, half), (right_y, 0, 1 - half), (right_z, 1, half))
     add_panels(panels, products, total, lists, lefts, place, True)
-    out[...] = total[:SINK_SLOTS]
+    out[...] = whole_total(total)
 
 
 def far_last_kernel(
-    left_a, left, right_0, right_1, before, out, total, products, whole, numbers, semaphore
+    left_a, left, right_d, before, out, total, products, whole, numbers, semaphore
 ):
     lists = SentLists(left_a, whole, numbers, semaphore)
     place = Place()
-    total[:SINK_SLOTS] = before[...]
-    all_products([left[...]], Joined(right_0, right_1), [products])
+    start_total(total, before)
+    all_products(left[...], right_d, products)
     add_listed(total, products, lists, place.section(1, True), 1 - place.half)
-    out[...] = total[:SINK_SLOTS]
+    out[...] = whole_total(total)
 
 
 def near_kernel(
-    l, r, s, n, left_a, left_b, own, right_y, right_z, right_0, right_1, out, lefts, total, products
+    l, r, s, n, left_a, left_b, own, right_y, right_z, right_d, out, lefts, total, products
 ):
     place = Place()
     half = place.half
     spread_panels(lefts, (left_a, left_b))
-    total[...] = jnp.zeros_like(total)
+    start_total(total)
     panels = (
-        (own, 0, half), (right_y, 0, 1 - half), (right_z, 1, half), (Joined(right_0, right_1), 1, 1 - half),
+        (own, 0, half), (right_y, 0, 1 - half), (right_z, 1, half), (right_d, 1, 1 - half),
     )
     add_panels(panels, products, total, OwnLists((l, r, s, n)), lefts, place, False)
-    out[...] = total[:SINK_SLOTS]
-
-
-class Joined:
-    def __init__(self, first, second):
-        self.first, self.second = first, second
-
-    def __getitem__(self, index):
-        size = self.first.shape[0]
-        return self.first[index] if index < size else self.second[index - size]
+    out[...] = whole_total(total)
 
 
 def pair_kernel(l, r, s, n, left, right_0, right_1, before, out, total, products, *, section):
     table = spread_table()
-    total[:SINK_SLOTS] = before[...]
+    start_total(total, before)
     for half, right in ((0, right_0), (1, right_1)):
-        all_products([spread_left(slots_in_order(left, half), table)], right, [products])
+        all_products(spread_left(slots_in_order(left, half), table), right, products)
         add_listed(total, products, OwnLists((l, r, s, n)), section, half)
-    out[...] = total[:SINK_SLOTS]
-
-
-STAGE_COST = 2 * 10**9
+    out[...] = whole_total(total)
+
+
+STAGE_COST = 0
 PICK_COST = 0
 ANY = pl.BlockSpec(memory_space=pl.ANY)
 SMEM = pl.BlockSpec(memory_space=pltpu.SMEM)
 VMEM = pl.BlockSpec(memory_space=pltpu.VMEM)
 SUMS = (SINK_SLOTS, HALF, LANES)
-TOTAL = pltpu.VMEM((SINK_SLOTS + 1, HALF, LANES), jnp.float32)
+TOTAL = pltpu.VMEM((2 * ODD_SINKS, HALF, LANES), jnp.float32)
 PRODUCT_TABLE = pltpu.VMEM((LEFT_SLOTS * RIGHT_SLOTS, HALF, LANES), jnp.float32)
 SPREAD = (2 * LEFT_SLOTS * HALF, 4 * TILE_SIDE)
 
@@ -254,7 +258,7 @@
         out_specs=jax.tree.map(lambda _: VMEM, outs),
         scratch_shapes=scratch,
         compiler_params=pltpu.CompilerParams(vmem_limit_bytes=24 * MIB),
-        cost_estimate=pl.CostEstimate(flops=flops, bytes_accessed=4 * MIB, transcendentals=0),
+        cost_estimate=pl.CostEstimate(flops=flops, bytes_accessed=0, transcendentals=0),
         name=name,
     )
 
@@ -313,9 +317,7 @@
         pick_kernel, [VMEM] * 3, (left_panel(0), left_panel(LIST_ROWS)), [], PICK_COST, "pick"
     )(own_left, beside, list_rows)
     far_a = send(far_a, z_far)
-    cut = RIGHT_SLOTS // 2
-    right_0 = send(right_z[:cut], y_next)
-    right_1 = send(right_y[cut:], z_next)
+    right_d = send(right_z, y_next)
     far_b = send(far_a, col_next(1))
     near_b = send(near_a, col_next(1))
 
@@ -326,14 +328,14 @@
         pltpu.SemaphoreType.DMA(()),
     ]
     far, far_left = call(
-        far_kernel, [VMEM] * 5, (sums(), spread_shape()), [spread, TOTAL, PRODUCT_TABLE, *sent], 0, "far_three"
+        far_kernel, [VMEM] * 5, (sums(), spread_shape()), [spread, TOTAL, PRODUCT_TABLE, *sent], 10**9, "far_three"
     )(far_a, far_b, right, right_y, right_z)
-    far = call(far_last_kernel, [VMEM] * 5, sums(), [TOTAL, PRODUCT_TABLE, *sent], 10**9, "far_last")(
-        far_a, far_left, right_0, right_1, far
+    far = call(far_last_kernel, [VMEM] * 4, sums(), [TOTAL, PRODUCT_TABLE, *sent], 10**9, "far_last")(
+        far_a, far_left, right_d, far
     )
     received = send(far, z_far)
-    near = call(near_kernel, [SMEM] * 4 + [VMEM] * 7, sums(), [spread, TOTAL, PRODUCT_TABLE], 3 * 10**9, "near_all")(
-        *lists, near_a, near_b, right, right_y, right_z, right_0, right_1
+    near = call(near_kernel, [SMEM] * 4 + [VMEM] * 6, sums(), [spread, TOTAL, PRODUCT_TABLE], 3 * 10**9, "near_all")(
+        *lists, near_a, near_b, right, right_y, right_z, right_d
     )
     return near + received
 

time: 33.4 us -> 31.7 us (0.949)
  Pallas kernels: 9.33 us -> 6.63 us
  waiting for transfers between devices: 6.09 us -> 6.98 us
    pallas_call x2, Pallas kernels: 6.28 us -> 4.05 us  [the longest x1 2.74 us: grouped(): call(near_kernel, [SMEM] * 4 + [VMEM] * 6, sums(), [spread, TOTAL, PRODUC...]
    ppermute x9 -> x8, waiting for transfers between devices: 6.09 us -> 6.98 us  [send(): return lax.ppermute(value, AXES, where)]
    pallas_call x1, Pallas kernels: 2.81 us -> 2.34 us  [grouped(): call(far_kernel, [VMEM] * 5, (sums(), spread_shape()), [spread, TOTAL, PR...]
    ppermute x9 -> x8, starting transfers between devices: 14.9 us -> 15.1 us  [send(): return lax.ppermute(value, AXES, where)]
  transfers between devices with their start and end apart: 9 -> 8, of which waited for: 4 -> 6; matrix products, arithmetic and copies ran while one was open for 0% -> 0% of each run, Pallas kernels for 28% -> 21%
where the time goes in v3:
time: 31.7 us; the launch traced here: 31.1 us
  starting transfers between devices  15.1 us (48%)
  waiting for transfers between devices  6.98 us (22%)
  Pallas kernels  6.63 us (21%)
  local copies, waits for them, and re-layouts  1.61 us (5%)
  other arithmetic  0.7 us (2%)
    ppermute x8, starting transfers between devices, send(): return lax.ppermute(value, AXES, where)  15.1 us
    ppermute x8, waiting for transfers between devices, send(): return lax.ppermute(value, AXES, where)  6.98 us
    pallas_call x1, Pallas kernels, grouped(): call(near_kernel, [SMEM] * 4 + [VMEM] * 6, sums(), [spread, TOTAL, PRODUC...  2.74 us
    pallas_call x1, Pallas kernels, grouped(): call(far_kernel, [VMEM] * 5, (sums(), spread_shape()), [spread, TOTAL, PR...  2.34 us
    unnamed x12, local copies, waits for them, and re-layouts  1.52 us
    pallas_call x1, Pallas kernels, grouped(): call(far_last_kernel, [VMEM] * 4, sums(), [TOTAL, PRODUCT_TABLE, *sent],...  1.3 us
    add x1, other arithmetic, grouped(): return near + received  0.7 us
  transfers between devices with their start and end apart: 8, of which 6 were waited for; matrix products, arithmetic and copies ran while one was open for 0% of the time, Pallas kernels for 21%

profile of v3, /device:TPU:0, one launch (start us, length us, event | category | flops | bytes accessed | tf_op | source)
XLA Modules:
  0.0 31.1 jit_solution(14254481930691800922)
XLA Ops:
  0.0 0.0 copy-start.5
  0.0 3.0 %collective-permute-start.3 = (f32[20,32,128]{2,1,0:T(8,128)}, f32[20,32,128]{2,1,0:T(8,128)S(1)}, u32[]{:S(2)}, u32[]{:S(2)}) collective-permute-start(f32[20,32,128]{2,1,0:T(8,128)} %bitcast.19), channel_id=1, source_target_pairs={{0,8},{1,9},{2,10},{3,11},{4,12},{5,13},{6,14},{7,15},{8,0},{9,1},... | collective-permute-start | bytes 983048 | tf_op jit(solution)/shard_map/ppermute | solution.py:295
  3.0 0.0 copy-start.3
  3.0 1.5 %collective-permute-start = (f32[256,128]{1,0:T(8,128)}, f32[256,128]{1,0:T(8,128)S(1)}, u32[]{:S(2)}, u32[]{:S(2)}) collective-permute-start(f32[256,128]{1,0:T(8,128)} %bitcast.11), channel_id=1, source_target_pairs={{0,2},{1,3},{2,0},{3,1},{4,6},{5,7},{6,4},{7,5},{8,10},{9,11},{10,... | collective-permute-start | bytes 393224 | tf_op jit(solution)/shard_map/ppermute | solution.py:295
  4.5 1.5 %collective-permute-start.2 = (f32[20,32,128]{2,1,0:T(8,128)}, f32[20,32,128]{2,1,0:T(8,128)S(1)}, u32[]{:S(2)}, u32[]{:S(2)}) collective-permute-start(f32[20,32,128]{2,1,0:T(8,128)} %bitcast.20), channel_id=1, source_target_pairs={{0,4},{1,5},{2,6},{3,7},{4,0},{5,1},{6,2},{7,3},{8,12},{9,13},{10,... | collective-permute-start | bytes 983048 | tf_op jit(solution)/shard_map/ppermute | solution.py:295
  6.0 0.0 copy-done.5
  6.0 0.0 copy-start.1
  6.0 0.0 copy-start.2
  6.0 0.1 copy.13.counts.n
  6.1 0.0 copy-done.3
  6.1 0.6 %copy-done.1 = s32[1,1,4,2,24]{4,3,2,1,0:T(2,128)S(1)} copy-done((s32[1,1,4,2,24]{4,3,2,1,0:T(2,128)S(1)}, s32[1,1,4,2,24]{4,3,2,1,0:T(2,128)}, u32[]{:S(2)}) %copy-start.1) | copy-done | bytes 792
  6.7 0.0 copy-done.2
  6.7 0.0 copy-start
  6.7 0.9 %copy-done = f32[1,2,4,4096]{3,2,1,0:T(4,128)S(1)} copy-done((f32[1,2,4,4096]{3,2,1,0:T(4,128)S(1)}, f32[1,2,4,4096]{3,2,1,0:T(4,128)}, u32[]{:S(2)}) %copy-start) | copy-done | bytes 131096
  7.7 0.0 copy-start.4
  7.7 0.2 stage.1
  7.9 0.3 %collective-permute-done.beside = f32[256,128]{1,0:T(8,128)S(1)} collective-permute-done((f32[256,128]{1,0:T(8,128)}, f32[256,128]{1,0:T(8,128)S(1)}, u32[]{:S(2)}, u32[]{:S(2)}) %collective-permute-start) | collective-permute-done | bytes 131104 | tf_op jit(solution)/shard_map/ppermute | solution.py:295
  8.2 2.5 %collective-permute-start.5 = (f32[288,128]{1,0:T(8,128)S(1)}, f32[288,128]{1,0:T(8,128)S(1)}, u32[]{:S(2)}, u32[]{:S(2)}) collective-permute-start(f32[288,128]{1,0:T(8,128)S(1)} %get-tuple-element.14), channel_id=1, source_target_pairs={{0,24},{1,25},{2,26},{3,27},{4,28},{5,29},{6,30},{7,31},{8,16},{9,... | collective-permute-start | bytes 442376 | tf_op jit(solution)/shard_map/ppermute | solution.py:295
  10.8 0.2 collective-permute-done.3.right_z
  10.9 1.7 %collective-permute-start.4 = (f32[20,32,128]{2,1,0:T(8,128)S(1)}, f32[20,32,128]{2,1,0:T(8,128)S(1)}, u32[]{:S(2)}, u32[]{:S(2)}) collective-permute-start(f32[20,32,128]{2,1,0:T(8,128)S(1)} %collective-permute-done.3.right_z), channel_id=1, source_target_pairs={{0,4},{1,5},{2,6},{3,7},{4,0},{5,1},{6,2},{7,3},{8,12},{9,13},{10,... | collective-permute-start | bytes 983048 | tf_op jit(solution)/shard_map/ppermute | solution.py:295
  12.6 3.8 %collective-permute-done.5.left_a = f32[288,128]{1,0:T(8,128)S(1)} collective-permute-done((f32[288,128]{1,0:T(8,128)S(1)}, f32[288,128]{1,0:T(8,128)S(1)}, u32[]{:S(2)}, u32[]{:S(2)}) %collective-permute-start.5) | collective-permute-done | bytes 147488 | tf_op jit(solution)/shard_map/ppermute | solution.py:295
  16.4 0.0 collective-permute-start.6
  16.4 0.5 %collective-permute-start.1 = (f32[256,128]{1,0:T(8,128)S(1)}, f32[256,128]{1,0:T(8,128)S(1)}, u32[]{:S(2)}, u32[]{:S(2)}) collective-permute-start(f32[256,128]{1,0:T(8,128)S(1)} %get-tuple-element.13.left_a), channel_id=1, source_target_pairs={{0,1},{1,0},{2,3},{3,2},{4,5},{5,4},{6,7},{7,6},{8,9},{9,8},{10,11... | collective-permute-start | bytes 393224 | tf_op jit(solution)/shard_map/ppermute | solution.py:295
  16.9 0.0 collective-permute-done.2.right_y
  16.9 0.9 %collective-permute-done.6.left_b = f32[288,128]{1,0:T(8,128)S(1)} collective-permute-done((f32[288,128]{1,0:T(8,128)S(1)}, f32[288,128]{1,0:T(8,128)S(1)}, u32[]{:S(2)}, u32[]{:S(2)}) %collective-permute-start.6) | collective-permute-done | bytes 147488 | tf_op jit(solution)/shard_map/ppermute | solution.py:295
  17.8 0.0 copy-done.4
  17.8 2.3 %far_three.1 = (f32[12,32,128]{2,1,0:T(8,128)S(1)}, bf16[256,256]{1,0:T(8,128)(2,1)S(1)}) custom-call(f32[288,128]{1,0:T(8,128)S(1)} %collective-permute-done.5.left_a, f32[288,128]{1,0:T(8,128)S(1)} %collective-permute-done.6.left_b, f32[20,32,128]{2,1,0:T(8,128)S(1)} %bitcast.21, f32[20,32,128]{2,1,0:T(8,128)S(1)} %collective-permute-done.2.right_y, ...), custom_call_target="tpu_custom_call" | custom-call | flops 1000000000 | tf_op jit(solution)/shard_map/far_three/pallas_call | solution.py:330
  20.1 0.5 %collective-permute-done.4.right_d = f32[20,32,128]{2,1,0:T(8,128)S(1)} collective-permute-done((f32[20,32,128]{2,1,0:T(8,128)S(1)}, f32[20,32,128]{2,1,0:T(8,128)S(1)}, u32[]{:S(2)}, u32[]{:S(2)}) %collective-permute-start.4) | collective-permute-done | bytes 327712 | tf_op jit(solution)/shard_map/ppermute | solution.py:295
  20.6 1.3 %far_last.1 = f32[12,32,128]{2,1,0:T(8,128)S(1)} custom-call(f32[288,128]{1,0:T(8,128)S(1)} %collective-permute-done.5.left_a, bf16[256,256]{1,0:T(8,128)(2,1)S(1)} %get-tuple-element.15.left, f32[20,32,128]{2,1,0:T(8,128)S(1)} %collective-permute-done.4.right_d, f32[12,32,128]{2,1,0:T(8,128)S(1)} %get-tuple-element.16.before), custom_call_target="tpu_custom_call" | custom-call | flops 1000000000 | tf_op jit(solution)/shard_map/far_last/pallas_call | solution.py:333
  22.0 4.4 %collective-permute-start.7 = (f32[12,32,128]{2,1,0:T(8,128)S(1)}, f32[12,32,128]{2,1,0:T(8,128)S(1)}, u32[]{:S(2)}, u32[]{:S(2)}) collective-permute-start(f32[12,32,128]{2,1,0:T(8,128)S(1)} %far_last.1), channel_id=1, source_target_pairs={{0,24},{1,25},{2,26},{3,27},{4,28},{5,29},{6,30},{7,31},{8,16},{9,... | collective-permute-start | bytes 589832 | tf_op jit(solution)/shard_map/ppermute | solution.py:295
  26.3 0.0 collective-permute-done.1.left_b
  26.3 2.7 %near_all.1 = f32[12,32,128]{2,1,0:T(8,128)S(1)} custom-call(s32[4,2,24]{2,1,0:T(2,128)S(1)} %bitcast.14, s32[4,2,24]{2,1,0:T(2,128)S(1)} %bitcast.16, s32[4,2,24]{2,1,0:T(2,128)S(1)} %bitcast.18, s32[4,2]{1,0:T(4,128)S(1)} %copy.13.counts.n, f32[256,128]{1,0:T(8,128)S(1)} %get-tuple-element.13.left_a, f32[256,128]{1,0:T(8,128)S(1)} %collective-permute-done.1.left_b, ...), custom_call_target="tpu_custom_call" | custom-call | flops 3000000000 | tf_op jit(solution)/shard_map/near_all/pallas_call | solution.py:337
  29.1 1.3 %collective-permute-done.7 = f32[12,32,128]{2,1,0:T(8,128)S(1)} collective-permute-done((f32[12,32,128]{2,1,0:T(8,128)S(1)}, f32[12,32,128]{2,1,0:T(8,128)S(1)}, u32[]{:S(2)}, u32[]{:S(2)}) %collective-permute-start.7) | collective-permute-done | bytes 196640 | tf_op jit(solution)/shard_map/ppermute | solution.py:295
  30.4 0.7 %add.3 = f32[12,32,128]{2,1,0:T(8,128)} add(f32[12,32,128]{2,1,0:T(8,128)S(1)} %near_all.1, f32[12,32,128]{2,1,0:T(8,128)S(1)} %collective-permute-done.7) | non-fusion elementwise | flops 49152 | bytes 589824 | tf_op jit(solution)/shard_map/add | solution.py:340
  (1 shorter events, 0.0 us)
Async XLA Ops:
  0.0 6.0 %copy-start.5 = (s32[1,1,4,2]{2,3,1,0:T(2,128)S(1)}, s32[1,1,4,2]{2,3,1,0:T(2,128)}, u32[]{:S(2)}) copy-start(s32[1,1,4,2]{2,3,1,0:T(2,128)} %param.11) | copy-start | bytes 100
  0.0 10.9 %collective-permute-start.3 = (f32[20,32,128]{2,1,0:T(8,128)}, f32[20,32,128]{2,1,0:T(8,128)S(1)}, u32[]{:S(2)}, u32[]{:S(2)}) collective-permute-start(f32[20,32,128]{2,1,0:T(8,128)} %bitcast.19), channel_id=1, source_target_pairs={{0,8},{1,9},{2,10},{3,11},{4,12},{5,13},{6,14},{7,15},{8,0},{9,1},... | collective-permute-start | bytes 983048 | tf_op jit(solution)/shard_map/ppermute | solution.py:295
  3.0 3.1 %copy-start.3 = (s32[1,1,4,2,24]{4,3,2,1,0:T(2,128)S(1)}, s32[1,1,4,2,24]{4,3,2,1,0:T(2,128)}, u32[]{:S(2)}) copy-start(s32[1,1,4,2,24]{4,3,2,1,0:T(2,128)} %param.10) | copy-start | bytes 2308
  3.0 5.2 %collective-permute-start = (f32[256,128]{1,0:T(8,128)}, f32[256,128]{1,0:T(8,128)S(1)}, u32[]{:S(2)}, u32[]{:S(2)}) collective-permute-start(f32[256,128]{1,0:T(8,128)} %bitcast.11), channel_id=1, source_target_pairs={{0,2},{1,3},{2,0},{3,1},{4,6},{5,7},{6,4},{7,5},{8,10},{9,11},{10,... | collective-permute-start | bytes 393224 | tf_op jit(solution)/shard_map/ppermute | solution.py:295
  4.5 12.4 %collective-permute-start.2 = (f32[20,32,128]{2,1,0:T(8,128)}, f32[20,32,128]{2,1,0:T(8,128)S(1)}, u32[]{:S(2)}, u32[]{:S(2)}) collective-permute-start(f32[20,32,128]{2,1,0:T(8,128)} %bitcast.20), channel_id=1, source_target_pairs={{0,4},{1,5},{2,6},{3,7},{4,0},{5,1},{6,2},{7,3},{8,12},{9,13},{10,... | collective-permute-start | bytes 983048 | tf_op jit(solution)/shard_map/ppermute | solution.py:295
  6.0 0.7 %copy-start.1 = (s32[1,1,4,2,24]{4,3,2,1,0:T(2,128)S(1)}, s32[1,1,4,2,24]{4,3,2,1,0:T(2,128)}, u32[]{:S(2)}) copy-start(s32[1,1,4,2,24]{4,3,2,1,0:T(2,128)} %param.8) | copy-start | bytes 2308
  6.0 0.7 %copy-start.2 = (s32[1,1,4,2,24]{4,3,2,1,0:T(2,128)S(1)}, s32[1,1,4,2,24]{4,3,2,1,0:T(2,128)}, u32[]{:S(2)}) copy-start(s32[1,1,4,2,24]{4,3,2,1,0:T(2,128)} %param.9) | copy-start | bytes 2308
  6.7 0.9 %copy-start = (f32[1,2,4,4096]{3,2,1,0:T(4,128)S(1)}, f32[1,2,4,4096]{3,2,1,0:T(4,128)}, u32[]{:S(2)}) copy-start(f32[1,2,4,4096]{3,2,1,0:T(4,128)} %param.6) | copy-start | bytes 393220
  7.7 10.1 %copy-start.4 = (f32[1,1,20,4096]{3,1,2,0:T(1,128)S(1)}, f32[1,1,20,4096]{3,1,2,0:T(1,128)}, u32[]{:S(2)}) copy-start(f32[1,1,20,4096]{3,1,2,0:T(1,128)} %param.7) | copy-start | bytes 983044
  8.2 8.2 %collective-permute-start.5 = (f32[288,128]{1,0:T(8,128)S(1)}, f32[288,128]{1,0:T(8,128)S(1)}, u32[]{:S(2)}, u32[]{:S(2)}) collective-permute-start(f32[288,128]{1,0:T(8,128)S(1)} %get-tuple-element.14), channel_id=1, source_target_pairs={{0,24},{1,25},{2,26},{3,27},{4,28},{5,29},{6,30},{7,31},{8,16},{9,... | collective-permute-start | bytes 442376 | tf_op jit(solution)/shard_map/ppermute | solution.py:295
  10.9 9.7 %collective-permute-start.4 = (f32[20,32,128]{2,1,0:T(8,128)S(1)}, f32[20,32,128]{2,1,0:T(8,128)S(1)}, u32[]{:S(2)}, u32[]{:S(2)}) collective-permute-start(f32[20,32,128]{2,1,0:T(8,128)S(1)} %collective-permute-done.3.right_z), channel_id=1, source_target_pairs={{0,4},{1,5},{2,6},{3,7},{4,0},{5,1},{6,2},{7,3},{8,12},{9,13},{10,... | collective-permute-start | bytes 983048 | tf_op jit(solution)/shard_map/ppermute | solution.py:295
  16.4 1.4 %collective-permute-start.6 = (f32[288,128]{1,0:T(8,128)S(1)}, f32[288,128]{1,0:T(8,128)S(1)}, u32[]{:S(2)}, u32[]{:S(2)}) collective-permute-start(f32[288,128]{1,0:T(8,128)S(1)} %collective-permute-done.5.left_a), channel_id=1, source_target_pairs={{0,1},{1,0},{2,3},{3,2},{4,5},{5,4},{6,7},{7,6},{8,9},{9,8},{10,11... | collective-permute-start | bytes 442376 | tf_op jit(solution)/shard_map/ppermute | solution.py:295
  16.4 9.9 %collective-permute-start.1 = (f32[256,128]{1,0:T(8,128)S(1)}, f32[256,128]{1,0:T(8,128)S(1)}, u32[]{:S(2)}, u32[]{:S(2)}) collective-permute-start(f32[256,128]{1,0:T(8,128)S(1)} %get-tuple-element.13.left_a), channel_id=1, source_target_pairs={{0,1},{1,0},{2,3},{3,2},{4,5},{5,4},{6,7},{7,6},{8,9},{9,8},{10,11... | collective-permute-start | bytes 393224 | tf_op jit(solution)/shard_map/ppermute | solution.py:295
  22.0 8.5 %collective-permute-start.7 = (f32[12,32,128]{2,1,0:T(8,128)S(1)}, f32[12,32,128]{2,1,0:T(8,128)S(1)}, u32[]{:S(2)}, u32[]{:S(2)}) collective-permute-start(f32[12,32,128]{2,1,0:T(8,128)S(1)} %far_last.1), channel_id=1, source_target_pairs={{0,24},{1,25},{2,26},{3,27},{4,28},{5,29},{6,30},{7,31},{8,16},{9,... | collective-permute-start | bytes 589832 | tf_op jit(solution)/shard_map/ppermute | solution.py:295

commit v4 on v3

--- a/solution.py
+++ b/solution.py
@@ -16,7 +16,8 @@
 HALF = TILE_SIDE // 2
 LANES = 2 * TILE_SIDE
 LEFT_ROWS = 2 * LEFT_SLOTS * HALF
-LIST_ROWS = 32
+LIST_ROWS = 2 * SECTIONS
+LIST_LANES = LANES // 4
 ODD_SINKS = 16
 AXES = ("row", "col")
 MIB = 1 << 20
@@ -112,21 +113,23 @@
 
 
 class SentLists:
-    def __init__(self, panel_ref, whole, numbers, semaphore):
-        left, right, sink, live = (
-            panel_ref[LEFT_ROWS + 8 * n : LEFT_ROWS + 8 * (n + 1), :].astype(jnp.int32) for n in range(4)
-        )
-        here = lax.broadcasted_iota(jnp.int32, left.shape, 1) < live
-        sink = right % 2 * ODD_SINKS + jnp.where(here, sink, SINK_SLOTS)
-        whole[...] = (left * RIGHT_SLOTS + right) * 2 * ODD_SINKS + sink
-        copy = pltpu.make_async_copy(whole, numbers, semaphore)
-        copy.start()
-        copy.wait()
+    def __init__(self, numbers):
         self.numbers = numbers
 
     def entry(self, section, half, p):
         number = self.numbers[section * 2 + half, p]
         return number // (2 * ODD_SINKS), number % (2 * ODD_SINKS)
+
+
+def merge_kernel(panel_ref, numbers, whole, semaphore):
+    rows = panel_ref[LEFT_ROWS:, :].astype(jnp.int32)
+    left, right, sink, live = (pltpu.roll(rows, LANES - n * LIST_LANES, 1) if n else rows for n in range(4))
+    here = lax.broadcasted_iota(jnp.int32, left.shape, 1) < live
+    sink = right % 2 * ODD_SINKS + jnp.where(here, sink, SINK_SLOTS)
+    whole[...] = (left * RIGHT_SLOTS + right) * 2 * ODD_SINKS + sink
+    copy = pltpu.make_async_copy(whole, numbers, semaphore)
+    copy.start()
+    copy.wait()
 
 
 class Place:
@@ -148,16 +151,15 @@
     copy = pltpu.make_async_copy(left, left_out, semaphore)
     copy.start()
     rows_out[...] = jnp.zeros_like(rows_out)
-    for n, ref in enumerate((left_list, right_list, sink_list)):
-        for section in range(SECTIONS):
-            start = 8 * n + 2 * section
-            rows_out[start : start + 2, :PRODUCTS] = ref[section].astype(jnp.float32)
     live = counts[...].astype(jnp.float32)
     for section in range(SECTIONS):
+        rows = slice(2 * section, 2 * section + 2)
+        for n, ref in enumerate((left_list, right_list, sink_list)):
+            rows_out[rows, n * LIST_LANES : n * LIST_LANES + PRODUCTS] = ref[section].astype(jnp.float32)
         for half in range(2):
-            row = 24 + 2 * section + half
             one = live[section : section + 1, half : half + 1]
-            rows_out[row : row + 1, :] = jnp.broadcast_to(one, (1, LANES))
+            row = 2 * section + half
+            rows_out[row : row + 1, 3 * LIST_LANES :] = jnp.broadcast_to(one, (1, LIST_LANES))
     copy.wait()
 
 
@@ -191,10 +193,9 @@
 
 
 def far_kernel(
-    left_a, left_b, own, right_y, right_z,
-    out, left_out, lefts, total, products, whole, numbers, semaphore,
+    numbers, left_a, left_b, own, right_y, right_z, out, left_out, lefts, total, products
 ):
-    lists = SentLists(left_a, whole, numbers, semaphore)
+    lists = SentLists(numbers)
     place = Place()
     half = place.half
     spread_panels(lefts, (left_a, left_b))
@@ -206,9 +207,9 @@
 
 
 def far_last_kernel(
-    left_a, left, right_d, before, out, total, products, whole, numbers, semaphore
+    numbers, left, right_d, before, out, total, products
 ):
-    lists = SentLists(left_a, whole, numbers, semaphore)
+    lists = SentLists(numbers)
     place = Place()
     start_total(total, before)
     all_products(left[...], right_d, products)
@@ -255,7 +256,7 @@
         kernel,
         out_shape=outs,
         in_specs=specs,
-        out_specs=jax.tree.map(lambda _: VMEM, outs),
+        out_specs=jax.tree.map(lambda out: SMEM if out.dtype == jnp.int32 else VMEM, outs),
         scratch_shapes=scratch,
         compiler_params=pltpu.CompilerParams(vmem_limit_bytes=24 * MIB),
         cost_estimate=pl.CostEstimate(flops=flops, bytes_accessed=0, transcendentals=0),
@@ -322,16 +323,15 @@
     near_b = send(near_a, col_next(1))
 
     spread = pltpu.VMEM((2, 2) + SPREAD, jnp.bfloat16)
-    sent = [
-        pltpu.VMEM((8, LANES), jnp.int32),
-        pltpu.SMEM((8, LANES), jnp.int32),
-        pltpu.SemaphoreType.DMA(()),
-    ]
+    numbers = call(
+        merge_kernel, [VMEM], pltpu.SMEM((2 * SECTIONS, LANES), jnp.int32),
+        [pltpu.VMEM((2 * SECTIONS, LANES), jnp.int32), pltpu.SemaphoreType.DMA(())], 0, "merge",
+    )(far_a)
     far, far_left = call(
-        far_kernel, [VMEM] * 5, (sums(), spread_shape()), [spread, TOTAL, PRODUCT_TABLE, *sent], 10**9, "far_three"
-    )(far_a, far_b, right, right_y, right_z)
-    far = call(far_last_kernel, [VMEM] * 4, sums(), [TOTAL, PRODUCT_TABLE, *sent], 10**9, "far_last")(
-        far_a, far_left, right_d, far
+        far_kernel, [SMEM] + [VMEM] * 5, (sums(), spread_shape()), [spread, TOTAL, PRODUCT_TABLE], 10**9, "far_three"
+    )(numbers, far_a, far_b, right, right_y, right_z)
+    far = call(far_last_kernel, [SMEM] + [VMEM] * 3, sums(), [TOTAL, PRODUCT_TABLE], 10**9, "far_last")(
+        numbers, far_left, right_d, far
     )
     received = send(far, z_far)
     near = call(near_kernel, [SMEM] * 4 + [VMEM] * 6, sums(), [spread, TOTAL, PRODUCT_TABLE], 3 * 10**9, "near_all")(

time: 31.7 us -> 30.1 us (0.950); the launches traced: 31.1 us -> 30 us
  starting transfers between devices: 15.1 us -> 13.6 us
  waiting for transfers between devices: 6.98 us -> 7.89 us
  Pallas kernels: 6.63 us -> 6.06 us
    ppermute x8, starting transfers between devices: 15.1 us -> 13.6 us  [send(): return lax.ppermute(value, AXES, where)]
    ppermute x8, waiting for transfers between devices: 6.98 us -> 7.89 us  [send(): return lax.ppermute(value, AXES, where)]
    pallas_call x2 -> x3, Pallas kernels: 3.64 us -> 3.08 us  [the longest x1 1.72 us: grouped(): call(far_kernel, [SMEM] + [VMEM] * 5, (sums(), spread_shape()), [spread,...]
  transfers between devices with their start and end apart: 8 -> 8, of which waited for: 6 -> 6; matrix products, arithmetic and copies ran while one was open for 0% -> 0% of each run, Pallas kernels for 21% -> 20%
where the time goes in v4:
time: 30.1 us; the launch traced here: 30 us
  starting transfers between devices  13.6 us (45%)
  waiting for transfers between devices  7.89 us (26%)
  Pallas kernels  6.06 us (20%)
  local copies, waits for them, and re-layouts  1.61 us (5%)
  other arithmetic  0.7 us (2%)
    ppermute x8, starting transfers between devices, send(): return lax.ppermute(value, AXES, where)  13.6 us
    ppermute x8, waiting for transfers between devices, send(): return lax.ppermute(value, AXES, where)  7.89 us
    pallas_call x1, Pallas kernels, grouped(): call(near_kernel, [SMEM] * 4 + [VMEM] * 6, sums(), [spread, TOTAL, PRODUC...  2.73 us
    pallas_call x1, Pallas kernels, grouped(): call(far_kernel, [SMEM] + [VMEM] * 5, (sums(), spread_shape()), [spread,...  1.72 us
    unnamed x12, local copies, waits for them, and re-layouts  1.52 us
    add x1, other arithmetic, grouped(): return near + received  0.7 us
    pallas_call x1, Pallas kernels, grouped(): call(merge_kernel, [VMEM], pltpu.SMEM((2 * SECTIONS, LANES), jnp.int32),...  0.69 us
    pallas_call x1, Pallas kernels, grouped(): call(far_last_kernel, [SMEM] + [VMEM] * 3, sums(), [TOTAL, PRODUCT_TABLE]...  0.68 us
  transfers between devices with their start and end apart: 8, of which 6 were waited for; matrix products, arithmetic and copies ran while one was open for 0% of the time, Pallas kernels for 20%

profile of v4, /device:TPU:0, one launch (start us, length us, event | category | flops | bytes accessed | tf_op | source)
XLA Modules:
  0.0 30.0 jit_solution(13952199280104847835)
XLA Ops:
  0.0 0.0 copy-start.5
  0.0 3.0 %collective-permute-start.3 = (f32[20,32,128]{2,1,0:T(8,128)}, f32[20,32,128]{2,1,0:T(8,128)S(1)}, u32[]{:S(2)}, u32[]{:S(2)}) collective-permute-start(f32[20,32,128]{2,1,0:T(8,128)} %bitcast.19), channel_id=1, source_target_pairs={{0,8},{1,9},{2,10},{3,11},{4,12},{5,13},{6,14},{7,15},{8,0},{9,1},... | collective-permute-start | bytes 983048 | tf_op jit(solution)/shard_map/ppermute | solution.py:296
  3.0 0.0 copy-start.3
  3.0 1.5 %collective-permute-start = (f32[256,128]{1,0:T(8,128)}, f32[256,128]{1,0:T(8,128)S(1)}, u32[]{:S(2)}, u32[]{:S(2)}) collective-permute-start(f32[256,128]{1,0:T(8,128)} %bitcast.11), channel_id=1, source_target_pairs={{0,2},{1,3},{2,0},{3,1},{4,6},{5,7},{6,4},{7,5},{8,10},{9,11},{10,... | collective-permute-start | bytes 393224 | tf_op jit(solution)/shard_map/ppermute | solution.py:296
  4.5 1.5 %collective-permute-start.2 = (f32[20,32,128]{2,1,0:T(8,128)}, f32[20,32,128]{2,1,0:T(8,128)S(1)}, u32[]{:S(2)}, u32[]{:S(2)}) collective-permute-start(f32[20,32,128]{2,1,0:T(8,128)} %bitcast.20), channel_id=1, source_target_pairs={{0,4},{1,5},{2,6},{3,7},{4,0},{5,1},{6,2},{7,3},{8,12},{9,13},{10,... | collective-permute-start | bytes 983048 | tf_op jit(solution)/shard_map/ppermute | solution.py:296
  6.0 0.0 copy-done.5
  6.0 0.0 copy-start.1
  6.0 0.0 copy-start.2
  6.0 0.1 copy.13.counts.n
  6.1 0.0 copy-done.3
  6.1 0.6 %copy-done.1 = s32[1,1,4,2,24]{4,3,2,1,0:T(2,128)S(1)} copy-done((s32[1,1,4,2,24]{4,3,2,1,0:T(2,128)S(1)}, s32[1,1,4,2,24]{4,3,2,1,0:T(2,128)}, u32[]{:S(2)}) %copy-start.1) | copy-done | bytes 792
  6.7 0.0 copy-done.2
  6.7 0.0 copy-start
  6.7 0.9 %copy-done = f32[1,2,4,4096]{3,2,1,0:T(4,128)S(1)} copy-done((f32[1,2,4,4096]{3,2,1,0:T(4,128)S(1)}, f32[1,2,4,4096]{3,2,1,0:T(4,128)}, u32[]{:S(2)}) %copy-start) | copy-done | bytes 131096
  7.7 0.0 copy-start.4
  7.7 0.2 stage.1
  7.9 0.3 %collective-permute-done.beside = f32[256,128]{1,0:T(8,128)S(1)} collective-permute-done((f32[256,128]{1,0:T(8,128)}, f32[256,128]{1,0:T(8,128)S(1)}, u32[]{:S(2)}, u32[]{:S(2)}) %collective-permute-start) | collective-permute-done | bytes 131104 | tf_op jit(solution)/shard_map/ppermute | solution.py:296
  8.2 2.5 %collective-permute-start.5 = (f32[264,128]{1,0:T(8,128)S(1)}, f32[264,128]{1,0:T(8,128)S(1)}, u32[]{:S(2)}, u32[]{:S(2)}) collective-permute-start(f32[264,128]{1,0:T(8,128)S(1)} %get-tuple-element.14), channel_id=1, source_target_pairs={{0,24},{1,25},{2,26},{3,27},{4,28},{5,29},{6,30},{7,31},{8,16},{9,... | collective-permute-start | bytes 405512 | tf_op jit(solution)/shard_map/ppermute | solution.py:296
  10.8 0.2 collective-permute-done.3.right_z
  10.9 1.7 %collective-permute-start.4 = (f32[20,32,128]{2,1,0:T(8,128)S(1)}, f32[20,32,128]{2,1,0:T(8,128)S(1)}, u32[]{:S(2)}, u32[]{:S(2)}) collective-permute-start(f32[20,32,128]{2,1,0:T(8,128)S(1)} %collective-permute-done.3.right_z), channel_id=1, source_target_pairs={{0,4},{1,5},{2,6},{3,7},{4,0},{5,1},{6,2},{7,3},{8,12},{9,13},{10,... | collective-permute-start | bytes 983048 | tf_op jit(solution)/shard_map/ppermute | solution.py:296
  12.6 3.5 %collective-permute-done.5.panel_ref.left_a = f32[264,128]{1,0:T(8,128)S(1)} collective-permute-done((f32[264,128]{1,0:T(8,128)S(1)}, f32[264,128]{1,0:T(8,128)S(1)}, u32[]{:S(2)}, u32[]{:S(2)}) %collective-permute-start.5) | collective-permute-done | bytes 135200 | tf_op jit(solution)/shard_map/ppermute | solution.py:296
  16.1 0.0 collective-permute-start.6
  16.1 0.5 %collective-permute-start.1 = (f32[256,128]{1,0:T(8,128)S(1)}, f32[256,128]{1,0:T(8,128)S(1)}, u32[]{:S(2)}, u32[]{:S(2)}) collective-permute-start(f32[256,128]{1,0:T(8,128)S(1)} %get-tuple-element.13.left_a), channel_id=1, source_target_pairs={{0,1},{1,0},{2,3},{3,2},{4,5},{5,4},{6,7},{7,6},{8,9},{9,8},{10,11... | collective-permute-start | bytes 393224 | tf_op jit(solution)/shard_map/ppermute | solution.py:296
  16.7 0.7 %merge.1.numbers = s32[8,128]{1,0:T(8,128)S(4)} custom-call(f32[264,128]{1,0:T(8,128)S(1)} %collective-permute-done.5.panel_ref.left_a), custom_call_target="tpu_custom_call" | custom-call | tf_op jit(solution)/shard_map/merge/pallas_call | solution.py:326
  17.3 0.0 collective-permute-done.2.right_y
  17.4 0.1 collective-permute-done.6.left_b
  17.5 0.0 copy-done.4
  17.5 1.7 %far_three.1 = (f32[12,32,128]{2,1,0:T(8,128)S(1)}, bf16[256,256]{1,0:T(8,128)(2,1)S(1)}) custom-call(s32[8,128]{1,0:T(8,128)S(4)} %merge.1.numbers, f32[264,128]{1,0:T(8,128)S(1)} %collective-permute-done.5.panel_ref.left_a, f32[264,128]{1,0:T(8,128)S(1)} %collective-permute-done.6.left_b, f32[20,32,128]{2,1,0:T(8,128)S(1)} %bitcast.21, ...), custom_call_target="tpu_custom_call" | custom-call | flops 1000000000 | tf_op jit(solution)/shard_map/far_three/pallas_call | solution.py:330
  19.2 1.4 %collective-permute-done.4.right_d = f32[20,32,128]{2,1,0:T(8,128)S(1)} collective-permute-done((f32[20,32,128]{2,1,0:T(8,128)S(1)}, f32[20,32,128]{2,1,0:T(8,128)S(1)}, u32[]{:S(2)}, u32[]{:S(2)}) %collective-permute-start.4) | collective-permute-done | bytes 327712 | tf_op jit(solution)/shard_map/ppermute | solution.py:296
  20.6 0.7 %far_last.1 = f32[12,32,128]{2,1,0:T(8,128)S(1)} custom-call(s32[8,128]{1,0:T(8,128)S(4)} %merge.1.numbers, bf16[256,256]{1,0:T(8,128)(2,1)S(1)} %get-tuple-element.15.left, f32[20,32,128]{2,1,0:T(8,128)S(1)} %collective-permute-done.4.right_d, f32[12,32,128]{2,1,0:T(8,128)S(1)} %get-tuple-element.16.before), custom_call_target="tpu_custom_call" | custom-call | flops 1000000000 | tf_op jit(solution)/shard_map/far_last/pallas_call | solution.py:333
  21.3 2.9 %collective-permute-start.7 = (f32[12,32,128]{2,1,0:T(8,128)S(1)}, f32[12,32,128]{2,1,0:T(8,128)S(1)}, u32[]{:S(2)}, u32[]{:S(2)}) collective-permute-start(f32[12,32,128]{2,1,0:T(8,128)S(1)} %far_last.1), channel_id=1, source_target_pairs={{0,24},{1,25},{2,26},{3,27},{4,28},{5,29},{6,30},{7,31},{8,16},{9,... | collective-permute-start | bytes 589832 | tf_op jit(solution)/shard_map/ppermute | solution.py:296
  24.2 0.0 collective-permute-done.1.left_b
  24.2 2.7 %near_all.1 = f32[12,32,128]{2,1,0:T(8,128)S(1)} custom-call(s32[4,2,24]{2,1,0:T(2,128)S(1)} %bitcast.14, s32[4,2,24]{2,1,0:T(2,128)S(1)} %bitcast.16, s32[4,2,24]{2,1,0:T(2,128)S(1)} %bitcast.18, s32[4,2]{1,0:T(4,128)S(1)} %copy.13.counts.n, f32[256,128]{1,0:T(8,128)S(1)} %get-tuple-element.13.left_a, f32[256,128]{1,0:T(8,128)S(1)} %collective-permute-done.1.left_b, ...), custom_call_target="tpu_custom_call" | custom-call | flops 3000000000 | tf_op jit(solution)/shard_map/near_all/pallas_call | solution.py:337
  26.9 2.3 %collective-permute-done.7 = f32[12,32,128]{2,1,0:T(8,128)S(1)} collective-permute-done((f32[12,32,128]{2,1,0:T(8,128)S(1)}, f32[12,32,128]{2,1,0:T(8,128)S(1)}, u32[]{:S(2)}, u32[]{:S(2)}) %collective-permute-start.7) | collective-permute-done | bytes 196640 | tf_op jit(solution)/shard_map/ppermute | solution.py:296
  29.3 0.7 %add.3 = f32[12,32,128]{2,1,0:T(8,128)} add(f32[12,32,128]{2,1,0:T(8,128)S(1)} %near_all.1, f32[12,32,128]{2,1,0:T(8,128)S(1)} %collective-permute-done.7) | non-fusion elementwise | flops 49152 | bytes 589824 | tf_op jit(solution)/shard_map/add | solution.py:340
  (1 shorter events, 0.0 us)
Async XLA Ops:
  0.0 6.0 %copy-start.5 = (s32[1,1,4,2]{2,3,1,0:T(2,128)S(1)}, s32[1,1,4,2]{2,3,1,0:T(2,128)}, u32[]{:S(2)}) copy-start(s32[1,1,4,2]{2,3,1,0:T(2,128)} %param.11) | copy-start | bytes 100
  0.0 10.9 %collective-permute-start.3 = (f32[20,32,128]{2,1,0:T(8,128)}, f32[20,32,128]{2,1,0:T(8,128)S(1)}, u32[]{:S(2)}, u32[]{:S(2)}) collective-permute-start(f32[20,32,128]{2,1,0:T(8,128)} %bitcast.19), channel_id=1, source_target_pairs={{0,8},{1,9},{2,10},{3,11},{4,12},{5,13},{6,14},{7,15},{8,0},{9,1},... | collective-permute-start | bytes 983048 | tf_op jit(solution)/shard_map/ppermute | solution.py:296
  3.0 3.1 %copy-start.3 = (s32[1,1,4,2,24]{4,3,2,1,0:T(2,128)S(1)}, s32[1,1,4,2,24]{4,3,2,1,0:T(2,128)}, u32[]{:S(2)}) copy-start(s32[1,1,4,2,24]{4,3,2,1,0:T(2,128)} %param.10) | copy-start | bytes 2308
  3.0 5.2 %collective-permute-start = (f32[256,128]{1,0:T(8,128)}, f32[256,128]{1,0:T(8,128)S(1)}, u32[]{:S(2)}, u32[]{:S(2)}) collective-permute-start(f32[256,128]{1,0:T(8,128)} %bitcast.11), channel_id=1, source_target_pairs={{0,2},{1,3},{2,0},{3,1},{4,6},{5,7},{6,4},{7,5},{8,10},{9,11},{10,... | collective-permute-start | bytes 393224 | tf_op jit(solution)/shard_map/ppermute | solution.py:296
  4.5 12.8 %collective-permute-start.2 = (f32[20,32,128]{2,1,0:T(8,128)}, f32[20,32,128]{2,1,0:T(8,128)S(1)}, u32[]{:S(2)}, u32[]{:S(2)}) collective-permute-start(f32[20,32,128]{2,1,0:T(8,128)} %bitcast.20), channel_id=1, source_target_pairs={{0,4},{1,5},{2,6},{3,7},{4,0},{5,1},{6,2},{7,3},{8,12},{9,13},{10,... | collective-permute-start | bytes 983048 | tf_op jit(solution)/shard_map/ppermute | solution.py:296
  6.0 0.7 %copy-start.1 = (s32[1,1,4,2,24]{4,3,2,1,0:T(2,128)S(1)}, s32[1,1,4,2,24]{4,3,2,1,0:T(2,128)}, u32[]{:S(2)}) copy-start(s32[1,1,4,2,24]{4,3,2,1,0:T(2,128)} %param.8) | copy-start | bytes 2308
  6.0 0.7 %copy-start.2 = (s32[1,1,4,2,24]{4,3,2,1,0:T(2,128)S(1)}, s32[1,1,4,2,24]{4,3,2,1,0:T(2,128)}, u32[]{:S(2)}) copy-start(s32[1,1,4,2,24]{4,3,2,1,0:T(2,128)} %param.9) | copy-start | bytes 2308
  6.7 0.9 %copy-start = (f32[1,2,4,4096]{3,2,1,0:T(4,128)S(1)}, f32[1,2,4,4096]{3,2,1,0:T(4,128)}, u32[]{:S(2)}) copy-start(f32[1,2,4,4096]{3,2,1,0:T(4,128)} %param.6) | copy-start | bytes 393220
  7.7 9.8 %copy-start.4 = (f32[1,1,20,4096]{3,1,2,0:T(1,128)S(1)}, f32[1,1,20,4096]{3,1,2,0:T(1,128)}, u32[]{:S(2)}) copy-start(f32[1,1,20,4096]{3,1,2,0:T(1,128)} %param.7) | copy-start | bytes 983044
  8.2 7.9 %collective-permute-start.5 = (f32[264,128]{1,0:T(8,128)S(1)}, f32[264,128]{1,0:T(8,128)S(1)}, u32[]{:S(2)}, u32[]{:S(2)}) collective-permute-start(f32[264,128]{1,0:T(8,128)S(1)} %get-tuple-element.14), channel_id=1, source_target_pairs={{0,24},{1,25},{2,26},{3,27},{4,28},{5,29},{6,30},{7,31},{8,16},{9,... | collective-permute-start | bytes 405512 | tf_op jit(solution)/shard_map/ppermute | solution.py:296
  10.9 9.7 %collective-permute-start.4 = (f32[20,32,128]{2,1,0:T(8,128)S(1)}, f32[20,32,128]{2,1,0:T(8,128)S(1)}, u32[]{:S(2)}, u32[]{:S(2)}) collective-permute-start(f32[20,32,128]{2,1,0:T(8,128)S(1)} %collective-permute-done.3.right_z), channel_id=1, source_target_pairs={{0,4},{1,5},{2,6},{3,7},{4,0},{5,1},{6,2},{7,3},{8,12},{9,13},{10,... | collective-permute-start | bytes 983048 | tf_op jit(solution)/shard_map/ppermute | solution.py:296
  16.1 1.4 %collective-permute-start.6 = (f32[264,128]{1,0:T(8,128)S(1)}, f32[264,128]{1,0:T(8,128)S(1)}, u32[]{:S(2)}, u32[]{:S(2)}) collective-permute-start(f32[264,128]{1,0:T(8,128)S(1)} %collective-permute-done.5.panel_ref.left_a), channel_id=1, source_target_pairs={{0,1},{1,0},{2,3},{3,2},{4,5},{5,4},{6,7},{7,6},{8,9},{9,8},{10,11... | collective-permute-start | bytes 405512 | tf_op jit(solution)/shard_map/ppermute | solution.py:296
  16.1 8.0 %collective-permute-start.1 = (f32[256,128]{1,0:T(8,128)S(1)}, f32[256,128]{1,0:T(8,128)S(1)}, u32[]{:S(2)}, u32[]{:S(2)}) collective-permute-start(f32[256,128]{1,0:T(8,128)S(1)} %get-tuple-element.13.left_a), channel_id=1, source_target_pairs={{0,1},{1,0},{2,3},{3,2},{4,5},{5,4},{6,7},{7,6},{8,9},{9,8},{10,11... | collective-permute-start | bytes 393224 | tf_op jit(solution)/shard_map/ppermute | solution.py:296
  21.3 7.9 %collective-permute-start.7 = (f32[12,32,128]{2,1,0:T(8,128)S(1)}, f32[12,32,128]{2,1,0:T(8,128)S(1)}, u32[]{:S(2)}, u32[]{:S(2)}) collective-permute-start(f32[12,32,128]{2,1,0:T(8,128)S(1)} %far_last.1), channel_id=1, source_target_pairs={{0,24},{1,25},{2,26},{3,27},{4,28},{5,29},{6,30},{7,31},{8,16},{9,... | collective-permute-start | bytes 589832 | tf_op jit(solution)/shard_map/ppermute | solution.py:296

commit v5 on v4

--- a/solution.py
+++ b/solution.py
@@ -18,7 +18,8 @@
 LEFT_ROWS = 2 * LEFT_SLOTS * HALF
 LIST_ROWS = 2 * SECTIONS
 LIST_LANES = LANES // 4
-ODD_SINKS = 16
+SINK_BITS = 5
+ODD_SINKS = 1 << (SINK_BITS - 1)
 AXES = ("row", "col")
 MIB = 1 << 20
 
@@ -109,7 +110,8 @@
     def entry(self, section, half, p):
         left, right, sink = (ref[section, half, p] for ref in self.refs[:3])
         live = self.refs[3][section, half]
-        return left * RIGHT_SLOTS + right, right % 2 * ODD_SINKS + jnp.where(p < live, sink, SINK_SLOTS)
+        odd = (right & 1) * ODD_SINKS
+        return left * RIGHT_SLOTS + right, odd + jnp.where(p < live, sink, SINK_SLOTS)
 
 
 class SentLists:
@@ -118,7 +120,7 @@
 
     def entry(self, section, half, p):
         number = self.numbers[section * 2 + half, p]
-        return number // (2 * ODD_SINKS), number % (2 * ODD_SINKS)
+        return number >> SINK_BITS, number & (2 * ODD_SINKS - 1)
 
 
 def merge_kernel(panel_ref, numbers, whole, semaphore):
@@ -126,7 +128,8 @@
     left, right, sink, live = (pltpu.roll(rows, LANES - n * LIST_LANES, 1) if n else rows for n in range(4))
     here = lax.broadcasted_iota(jnp.int32, left.shape, 1) < live
     sink = right % 2 * ODD_SINKS + jnp.where(here, sink, SINK_SLOTS)
-    whole[...] = (left * RIGHT_SLOTS + right) * 2 * ODD_SINKS + sink
+    product = jnp.where(here, left * RIGHT_SLOTS + right, 0)
+    whole[...] = product * 2 * ODD_SINKS + sink
     copy = pltpu.make_async_copy(whole, numbers, semaphore)
     copy.start()
     copy.wait()

time: 30.1 us -> 30.1 us (level)
  waiting for transfers between devices: 7.89 us -> 8.31 us
  Pallas kernels: 6.06 us -> 5.66 us
    ppermute x8, waiting for transfers between devices: 7.89 us -> 8.31 us  [send(): return lax.ppermute(value, AXES, where)]
  transfers between devices with their start and end apart: 8 -> 8, of which waited for: 6 -> 6; matrix products, arithmetic and copies ran while one was open for 0% -> 0% of each run, Pallas kernels for 20% -> 19%
where the time goes in v5:
time: 30.1 us; the launch traced here: 30 us
  starting transfers between devices  13.6 us (45%)
  waiting for transfers between devices  8.31 us (28%)
  Pallas kernels  5.66 us (19%)
  local copies, waits for them, and re-layouts  1.61 us (5%)
  other arithmetic  0.7 us (2%)
    ppermute x8, starting transfers between devices, send(): return lax.ppermute(value, AXES, where)  13.6 us
    ppermute x8, waiting for transfers between devices, send(): return lax.ppermute(value, AXES, where)  8.31 us
    pallas_call x1, Pallas kernels, grouped(): call(near_kernel, [SMEM] * 4 + [VMEM] * 6, sums(), [spread, TOTAL, PRODUC...  2.62 us
    unnamed x12, local copies, waits for them, and re-layouts  1.52 us
    pallas_call x1, Pallas kernels, grouped(): call(far_kernel, [SMEM] + [VMEM] * 5, (sums(), spread_shape()), [spread,...  1.44 us
    add x1, other arithmetic, grouped(): return near + received  0.7 us
    pallas_call x1, Pallas kernels, grouped(): call(merge_kernel, [VMEM], pltpu.SMEM((2 * SECTIONS, LANES), jnp.int32),...  0.69 us
    pallas_call x1, Pallas kernels, grouped(): call(far_last_kernel, [SMEM] + [VMEM] * 3, sums(), [TOTAL, PRODUCT_TABLE]...  0.66 us
  transfers between devices with their start and end apart: 8, of which 6 were waited for; matrix products, arithmetic and copies ran while one was open for 0% of the time, Pallas kernels for 19%

profile of v5, /device:TPU:0, one launch (start us, length us, event | category | flops | bytes accessed | tf_op | source)
XLA Modules:
  0.0 30.0 jit_solution(6013980335837821480)
XLA Ops:
  0.0 0.0 copy-start.5
  0.0 3.0 %collective-permute-start.3 = (f32[20,32,128]{2,1,0:T(8,128)}, f32[20,32,128]{2,1,0:T(8,128)S(1)}, u32[]{:S(2)}, u32[]{:S(2)}) collective-permute-start(f32[20,32,128]{2,1,0:T(8,128)} %bitcast.19), channel_id=1, source_target_pairs={{0,8},{1,9},{2,10},{3,11},{4,12},{5,13},{6,14},{7,15},{8,0},{9,1},... | collective-permute-start | bytes 983048 | tf_op jit(solution)/shard_map/ppermute | solution.py:299
  3.0 0.0 copy-start.3
  3.0 1.5 %collective-permute-start = (f32[256,128]{1,0:T(8,128)}, f32[256,128]{1,0:T(8,128)S(1)}, u32[]{:S(2)}, u32[]{:S(2)}) collective-permute-start(f32[256,128]{1,0:T(8,128)} %bitcast.11), channel_id=1, source_target_pairs={{0,2},{1,3},{2,0},{3,1},{4,6},{5,7},{6,4},{7,5},{8,10},{9,11},{10,... | collective-permute-start | bytes 393224 | tf_op jit(solution)/shard_map/ppermute | solution.py:299
  4.5 1.5 %collective-permute-start.2 = (f32[20,32,128]{2,1,0:T(8,128)}, f32[20,32,128]{2,1,0:T(8,128)S(1)}, u32[]{:S(2)}, u32[]{:S(2)}) collective-permute-start(f32[20,32,128]{2,1,0:T(8,128)} %bitcast.20), channel_id=1, source_target_pairs={{0,4},{1,5},{2,6},{3,7},{4,0},{5,1},{6,2},{7,3},{8,12},{9,13},{10,... | collective-permute-start | bytes 983048 | tf_op jit(solution)/shard_map/ppermute | solution.py:299
  6.0 0.0 copy-done.5
  6.0 0.0 copy-start.1
  6.0 0.0 copy-start.2
  6.0 0.1 copy.13.counts.n
  6.1 0.0 copy-done.3
  6.1 0.6 %copy-done.1 = s32[1,1,4,2,24]{4,3,2,1,0:T(2,128)S(1)} copy-done((s32[1,1,4,2,24]{4,3,2,1,0:T(2,128)S(1)}, s32[1,1,4,2,24]{4,3,2,1,0:T(2,128)}, u32[]{:S(2)}) %copy-start.1) | copy-done | bytes 792
  6.7 0.0 copy-done.2
  6.7 0.0 copy-start
  6.7 0.9 %copy-done = f32[1,2,4,4096]{3,2,1,0:T(4,128)S(1)} copy-done((f32[1,2,4,4096]{3,2,1,0:T(4,128)S(1)}, f32[1,2,4,4096]{3,2,1,0:T(4,128)}, u32[]{:S(2)}) %copy-start) | copy-done | bytes 131096
  7.7 0.0 copy-start.4
  7.7 0.2 stage.1
  7.9 0.3 %collective-permute-done.beside = f32[256,128]{1,0:T(8,128)S(1)} collective-permute-done((f32[256,128]{1,0:T(8,128)}, f32[256,128]{1,0:T(8,128)S(1)}, u32[]{:S(2)}, u32[]{:S(2)}) %collective-permute-start) | collective-permute-done | bytes 131104 | tf_op jit(solution)/shard_map/ppermute | solution.py:299
  8.2 2.5 %collective-permute-start.5 = (f32[264,128]{1,0:T(8,128)S(1)}, f32[264,128]{1,0:T(8,128)S(1)}, u32[]{:S(2)}, u32[]{:S(2)}) collective-permute-start(f32[264,128]{1,0:T(8,128)S(1)} %get-tuple-element.14), channel_id=1, source_target_pairs={{0,24},{1,25},{2,26},{3,27},{4,28},{5,29},{6,30},{7,31},{8,16},{9,... | collective-permute-start | bytes 405512 | tf_op jit(solution)/shard_map/ppermute | solution.py:299
  10.8 0.2 collective-permute-done.3.right_z
  10.9 1.7 %collective-permute-start.4 = (f32[20,32,128]{2,1,0:T(8,128)S(1)}, f32[20,32,128]{2,1,0:T(8,128)S(1)}, u32[]{:S(2)}, u32[]{:S(2)}) collective-permute-start(f32[20,32,128]{2,1,0:T(8,128)S(1)} %collective-permute-done.3.right_z), channel_id=1, source_target_pairs={{0,4},{1,5},{2,6},{3,7},{4,0},{5,1},{6,2},{7,3},{8,12},{9,13},{10,... | collective-permute-start | bytes 983048 | tf_op jit(solution)/shard_map/ppermute | solution.py:299
  12.6 3.5 %collective-permute-done.5.panel_ref.left_a = f32[264,128]{1,0:T(8,128)S(1)} collective-permute-done((f32[264,128]{1,0:T(8,128)S(1)}, f32[264,128]{1,0:T(8,128)S(1)}, u32[]{:S(2)}, u32[]{:S(2)}) %collective-permute-start.5) | collective-permute-done | bytes 135200 | tf_op jit(solution)/shard_map/ppermute | solution.py:299
  16.1 0.0 collective-permute-start.6
  16.1 0.5 %collective-permute-start.1 = (f32[256,128]{1,0:T(8,128)S(1)}, f32[256,128]{1,0:T(8,128)S(1)}, u32[]{:S(2)}, u32[]{:S(2)}) collective-permute-start(f32[256,128]{1,0:T(8,128)S(1)} %get-tuple-element.13.left_a), channel_id=1, source_target_pairs={{0,1},{1,0},{2,3},{3,2},{4,5},{5,4},{6,7},{7,6},{8,9},{9,8},{10,11... | collective-permute-start | bytes 393224 | tf_op jit(solution)/shard_map/ppermute | solution.py:299
  16.7 0.7 %merge.1.numbers = s32[8,128]{1,0:T(8,128)S(4)} custom-call(f32[264,128]{1,0:T(8,128)S(1)} %collective-permute-done.5.panel_ref.left_a), custom_call_target="tpu_custom_call" | custom-call | tf_op jit(solution)/shard_map/merge/pallas_call | solution.py:329
  17.3 0.0 collective-permute-done.2.right_y
  17.4 0.1 collective-permute-done.6.left_b
  17.5 0.0 copy-done.4
  17.5 1.4 %far_three.1 = (f32[12,32,128]{2,1,0:T(8,128)S(1)}, bf16[256,256]{1,0:T(8,128)(2,1)S(1)}) custom-call(s32[8,128]{1,0:T(8,128)S(4)} %merge.1.numbers, f32[264,128]{1,0:T(8,128)S(1)} %collective-permute-done.5.panel_ref.left_a, f32[264,128]{1,0:T(8,128)S(1)} %collective-permute-done.6.left_b, f32[20,32,128]{2,1,0:T(8,128)S(1)} %bitcast.21, ...), custom_call_target="tpu_custom_call" | custom-call | flops 1000000000 | tf_op jit(solution)/shard_map/far_three/pallas_call | solution.py:333
  18.9 1.7 %collective-permute-done.4.right_d = f32[20,32,128]{2,1,0:T(8,128)S(1)} collective-permute-done((f32[20,32,128]{2,1,0:T(8,128)S(1)}, f32[20,32,128]{2,1,0:T(8,128)S(1)}, u32[]{:S(2)}, u32[]{:S(2)}) %collective-permute-start.4) | collective-permute-done | bytes 327712 | tf_op jit(solution)/shard_map/ppermute | solution.py:299
  20.6 0.7 %far_last.1 = f32[12,32,128]{2,1,0:T(8,128)S(1)} custom-call(s32[8,128]{1,0:T(8,128)S(4)} %merge.1.numbers, bf16[256,256]{1,0:T(8,128)(2,1)S(1)} %get-tuple-element.15.left, f32[20,32,128]{2,1,0:T(8,128)S(1)} %collective-permute-done.4.right_d, f32[12,32,128]{2,1,0:T(8,128)S(1)} %get-tuple-element.16.before), custom_call_target="tpu_custom_call" | custom-call | flops 1000000000 | tf_op jit(solution)/shard_map/far_last/pallas_call | solution.py:336
  21.3 2.8 %collective-permute-start.7 = (f32[12,32,128]{2,1,0:T(8,128)S(1)}, f32[12,32,128]{2,1,0:T(8,128)S(1)}, u32[]{:S(2)}, u32[]{:S(2)}) collective-permute-start(f32[12,32,128]{2,1,0:T(8,128)S(1)} %far_last.1), channel_id=1, source_target_pairs={{0,24},{1,25},{2,26},{3,27},{4,28},{5,29},{6,30},{7,31},{8,16},{9,... | collective-permute-start | bytes 589832 | tf_op jit(solution)/shard_map/ppermute | solution.py:299
  24.2 0.0 collective-permute-done.1.left_b
  24.2 2.6 %near_all.1 = f32[12,32,128]{2,1,0:T(8,128)S(1)} custom-call(s32[4,2,24]{2,1,0:T(2,128)S(1)} %bitcast.14, s32[4,2,24]{2,1,0:T(2,128)S(1)} %bitcast.16, s32[4,2,24]{2,1,0:T(2,128)S(1)} %bitcast.18, s32[4,2]{1,0:T(4,128)S(1)} %copy.13.counts.n, f32[256,128]{1,0:T(8,128)S(1)} %get-tuple-element.13.left_a, f32[256,128]{1,0:T(8,128)S(1)} %collective-permute-done.1.left_b, ...), custom_call_target="tpu_custom_call" | custom-call | flops 3000000000 | tf_op jit(solution)/shard_map/near_all/pallas_call | solution.py:340
  26.8 2.5 %collective-permute-done.7 = f32[12,32,128]{2,1,0:T(8,128)S(1)} collective-permute-done((f32[12,32,128]{2,1,0:T(8,128)S(1)}, f32[12,32,128]{2,1,0:T(8,128)S(1)}, u32[]{:S(2)}, u32[]{:S(2)}) %collective-permute-start.7) | collective-permute-done | bytes 196640 | tf_op jit(solution)/shard_map/ppermute | solution.py:299
  29.3 0.7 %add.3 = f32[12,32,128]{2,1,0:T(8,128)} add(f32[12,32,128]{2,1,0:T(8,128)S(1)} %near_all.1, f32[12,32,128]{2,1,0:T(8,128)S(1)} %collective-permute-done.7) | non-fusion elementwise | flops 49152 | bytes 589824 | tf_op jit(solution)/shard_map/add | solution.py:343
  (1 shorter events, 0.0 us)
Async XLA Ops:
  0.0 6.0 %copy-start.5 = (s32[1,1,4,2]{2,3,1,0:T(2,128)S(1)}, s32[1,1,4,2]{2,3,1,0:T(2,128)}, u32[]{:S(2)}) copy-start(s32[1,1,4,2]{2,3,1,0:T(2,128)} %param.11) | copy-start | bytes 100
  0.0 10.9 %collective-permute-start.3 = (f32[20,32,128]{2,1,0:T(8,128)}, f32[20,32,128]{2,1,0:T(8,128)S(1)}, u32[]{:S(2)}, u32[]{:S(2)}) collective-permute-start(f32[20,32,128]{2,1,0:T(8,128)} %bitcast.19), channel_id=1, source_target_pairs={{0,8},{1,9},{2,10},{3,11},{4,12},{5,13},{6,14},{7,15},{8,0},{9,1},... | collective-permute-start | bytes 983048 | tf_op jit(solution)/shard_map/ppermute | solution.py:299
  3.0 3.1 %copy-start.3 = (s32[1,1,4,2,24]{4,3,2,1,0:T(2,128)S(1)}, s32[1,1,4,2,24]{4,3,2,1,0:T(2,128)}, u32[]{:S(2)}) copy-start(s32[1,1,4,2,24]{4,3,2,1,0:T(2,128)} %param.10) | copy-start | bytes 2308
  3.0 5.2 %collective-permute-start = (f32[256,128]{1,0:T(8,128)}, f32[256,128]{1,0:T(8,128)S(1)}, u32[]{:S(2)}, u32[]{:S(2)}) collective-permute-start(f32[256,128]{1,0:T(8,128)} %bitcast.11), channel_id=1, source_target_pairs={{0,2},{1,3},{2,0},{3,1},{4,6},{5,7},{6,4},{7,5},{8,10},{9,11},{10,... | collective-permute-start | bytes 393224 | tf_op jit(solution)/shard_map/ppermute | solution.py:299
  4.5 12.8 %collective-permute-start.2 = (f32[20,32,128]{2,1,0:T(8,128)}, f32[20,32,128]{2,1,0:T(8,128)S(1)}, u32[]{:S(2)}, u32[]{:S(2)}) collective-permute-start(f32[20,32,128]{2,1,0:T(8,128)} %bitcast.20), channel_id=1, source_target_pairs={{0,4},{1,5},{2,6},{3,7},{4,0},{5,1},{6,2},{7,3},{8,12},{9,13},{10,... | collective-permute-start | bytes 983048 | tf_op jit(solution)/shard_map/ppermute | solution.py:299
  6.0 0.7 %copy-start.1 = (s32[1,1,4,2,24]{4,3,2,1,0:T(2,128)S(1)}, s32[1,1,4,2,24]{4,3,2,1,0:T(2,128)}, u32[]{:S(2)}) copy-start(s32[1,1,4,2,24]{4,3,2,1,0:T(2,128)} %param.8) | copy-start | bytes 2308
  6.0 0.7 %copy-start.2 = (s32[1,1,4,2,24]{4,3,2,1,0:T(2,128)S(1)}, s32[1,1,4,2,24]{4,3,2,1,0:T(2,128)}, u32[]{:S(2)}) copy-start(s32[1,1,4,2,24]{4,3,2,1,0:T(2,128)} %param.9) | copy-start | bytes 2308
  6.7 0.9 %copy-start = (f32[1,2,4,4096]{3,2,1,0:T(4,128)S(1)}, f32[1,2,4,4096]{3,2,1,0:T(4,128)}, u32[]{:S(2)}) copy-start(f32[1,2,4,4096]{3,2,1,0:T(4,128)} %param.6) | copy-start | bytes 393220
  7.7 9.8 %copy-start.4 = (f32[1,1,20,4096]{3,1,2,0:T(1,128)S(1)}, f32[1,1,20,4096]{3,1,2,0:T(1,128)}, u32[]{:S(2)}) copy-start(f32[1,1,20,4096]{3,1,2,0:T(1,128)} %param.7) | copy-start | bytes 983044
  8.2 7.9 %collective-permute-start.5 = (f32[264,128]{1,0:T(8,128)S(1)}, f32[264,128]{1,0:T(8,128)S(1)}, u32[]{:S(2)}, u32[]{:S(2)}) collective-permute-start(f32[264,128]{1,0:T(8,128)S(1)} %get-tuple-element.14), channel_id=1, source_target_pairs={{0,24},{1,25},{2,26},{3,27},{4,28},{5,29},{6,30},{7,31},{8,16},{9,... | collective-permute-start | bytes 405512 | tf_op jit(solution)/shard_map/ppermute | solution.py:299
  10.9 9.7 %collective-permute-start.4 = (f32[20,32,128]{2,1,0:T(8,128)S(1)}, f32[20,32,128]{2,1,0:T(8,128)S(1)}, u32[]{:S(2)}, u32[]{:S(2)}) collective-permute-start(f32[20,32,128]{2,1,0:T(8,128)S(1)} %collective-permute-done.3.right_z), channel_id=1, source_target_pairs={{0,4},{1,5},{2,6},{3,7},{4,0},{5,1},{6,2},{7,3},{8,12},{9,13},{10,... | collective-permute-start | bytes 983048 | tf_op jit(solution)/shard_map/ppermute | solution.py:299
  16.1 1.4 %collective-permute-start.6 = (f32[264,128]{1,0:T(8,128)S(1)}, f32[264,128]{1,0:T(8,128)S(1)}, u32[]{:S(2)}, u32[]{:S(2)}) collective-permute-start(f32[264,128]{1,0:T(8,128)S(1)} %collective-permute-done.5.panel_ref.left_a), channel_id=1, source_target_pairs={{0,1},{1,0},{2,3},{3,2},{4,5},{5,4},{6,7},{7,6},{8,9},{9,8},{10,11... | collective-permute-start | bytes 405512 | tf_op jit(solution)/shard_map/ppermute | solution.py:299
  16.1 8.0 %collective-permute-start.1 = (f32[256,128]{1,0:T(8,128)S(1)}, f32[256,128]{1,0:T(8,128)S(1)}, u32[]{:S(2)}, u32[]{:S(2)}) collective-permute-start(f32[256,128]{1,0:T(8,128)S(1)} %get-tuple-element.13.left_a), channel_id=1, source_target_pairs={{0,1},{1,0},{2,3},{3,2},{4,5},{5,4},{6,7},{7,6},{8,9},{9,8},{10,11... | collective-permute-start | bytes 393224 | tf_op jit(solution)/shard_map/ppermute | solution.py:299
  21.3 7.9 %collective-permute-start.7 = (f32[12,32,128]{2,1,0:T(8,128)S(1)}, f32[12,32,128]{2,1,0:T(8,128)S(1)}, u32[]{:S(2)}, u32[]{:S(2)}) collective-permute-start(f32[12,32,128]{2,1,0:T(8,128)S(1)} %far_last.1), channel_id=1, source_target_pairs={{0,24},{1,25},{2,26},{3,27},{4,28},{5,29},{6,30},{7,31},{8,16},{9,... | collective-permute-start | bytes 589832 | tf_op jit(solution)/shard_map/ppermute | solution.py:299

commit v6 on v5

--- a/solution.py
+++ b/solution.py
@@ -150,9 +150,10 @@
         return ((self.pair ^ level) - target - self.col + 2 * self.cols) % self.cols
 
 
-def stage_kernel(left, left_list, right_list, sink_list, counts, left_out, rows_out, semaphore):
+def stage_kernel(left, left_list, right_list, sink_list, counts, left_out, rows_out, table_out, semaphore):
     copy = pltpu.make_async_copy(left, left_out, semaphore)
     copy.start()
+    table_out[...] = spread_table()
     rows_out[...] = jnp.zeros_like(rows_out)
     live = counts[...].astype(jnp.float32)
     for section in range(SECTIONS):
@@ -182,8 +183,7 @@
     far_out[LEFT_ROWS:, :] = rows[...]
 
 
-def spread_panels(lefts, panels):
-    table = spread_table()
+def spread_panels(lefts, panels, table):
     for which, panel in enumerate(panels):
         for half in range(2):
             lefts[which, half] = spread_left(slots_in_order(panel, half), table)
@@ -196,12 +196,12 @@
 
 
 def far_kernel(
-    numbers, left_a, left_b, own, right_y, right_z, out, left_out, lefts, total, products
+    numbers, table, left_a, left_b, own, right_y, right_z, out, left_out, lefts, total, products
 ):
     lists = SentLists(numbers)
     place = Place()
     half = place.half
-    spread_panels(lefts, (left_a, left_b))
+    spread_panels(lefts, (left_a, left_b), table[...])
     left_out[...] = lefts[place.which_left(1), 1 - half]
     start_total(total)
     panels = ((own, 0, half), (right_y, 0, 1 - half), (right_z, 1, half))
@@ -214,18 +214,18 @@
 ):
     lists = SentLists(numbers)
     place = Place()
-    start_total(total, before)
+    start_total(total)
     all_products(left[...], right_d, products)
     add_listed(total, products, lists, place.section(1, True), 1 - place.half)
-    out[...] = whole_total(total)
+    out[...] = before[...] + whole_total(total)
 
 
 def near_kernel(
-    l, r, s, n, left_a, left_b, own, right_y, right_z, right_d, out, lefts, total, products
+    l, r, s, n, table, left_a, left_b, own, right_y, right_z, right_d, out, lefts, total, products
 ):
     place = Place()
     half = place.half
-    spread_panels(lefts, (left_a, left_b))
+    spread_panels(lefts, (left_a, left_b), table[...])
     start_total(total)
     panels = (
         (own, 0, half), (right_y, 0, 1 - half), (right_z, 1, half), (right_d, 1, 1 - half),
@@ -313,8 +313,9 @@
     beside = send(left, col_next(2))
     right_y = send(right, y_next)
     right_z = send(right, z_next)
-    own_left, list_rows = call(
-        stage_kernel, [ANY] + [VMEM] * 4, (left_panel(0), jax.ShapeDtypeStruct((LIST_ROWS, LANES), jnp.float32)),
+    own_left, list_rows, table = call(
+        stage_kernel, [ANY] + [VMEM] * 4, (left_panel(0), jax.ShapeDtypeStruct((LIST_ROWS, LANES), jnp.float32),
+         jax.ShapeDtypeStruct((2 * LANES, 8 * TILE_SIDE), jnp.bfloat16)),
         [pltpu.SemaphoreType.DMA(())], STAGE_COST, "stage",
     )(left, *lists)
     near_a, far_a = call(
@@ -331,14 +332,14 @@
         [pltpu.VMEM((2 * SECTIONS, LANES), jnp.int32), pltpu.SemaphoreType.DMA(())], 0, "merge",
     )(far_a)
     far, far_left = call(
-        far_kernel, [SMEM] + [VMEM] * 5, (sums(), spread_shape()), [spread, TOTAL, PRODUCT_TABLE], 10**9, "far_three"
-    )(numbers, far_a, far_b, right, right_y, right_z)
-    far = call(far_last_kernel, [SMEM] + [VMEM] * 3, sums(), [TOTAL, PRODUCT_TABLE], 10**9, "far_last")(
+        far_kernel, [SMEM] + [VMEM] * 6, (sums(), spread_shape()), [spread, TOTAL, PRODUCT_TABLE], 10**9, "far_three"
+    )(numbers, table, far_a, far_b, right, right_y, right_z)
+    far = call(far_last_kernel, [SMEM] + [VMEM] * 3, sums(), [TOTAL, PRODUCT_TABLE], 0, "far_last")(
         numbers, far_left, right_d, far
     )
     received = send(far, z_far)
-    near = call(near_kernel, [SMEM] * 4 + [VMEM] * 6, sums(), [spread, TOTAL, PRODUCT_TABLE], 3 * 10**9, "near_all")(
-        *lists, near_a, near_b, right, right_y, right_z, right_d
+    near = call(near_kernel, [SMEM] * 4 + [VMEM] * 7, sums(), [spread, TOTAL, PRODUCT_TABLE], 3 * 10**9, "near_all")(
+        *lists, table, near_a, near_b, right, right_y, right_z, right_d
     )
     return near + received
 

time: 30.1 us -> 30.1 us (level)
  no operation moved by 1% of the time
where the time goes in v6:
time: 30.1 us; the launch traced here: 30 us
  starting transfers between devices  13.6 us (45%)
  waiting for transfers between devices  8.34 us (28%)
  Pallas kernels  5.63 us (19%)
  local copies, waits for them, and re-layouts  1.61 us (5%)
  other arithmetic  0.7 us (2%)
    ppermute x8, starting transfers between devices, send(): return lax.ppermute(value, AXES, where)  13.6 us
    ppermute x8, waiting for transfers between devices, send(): return lax.ppermute(value, AXES, where)  8.34 us
    pallas_call x1, Pallas kernels, grouped(): call(near_kernel, [SMEM] * 4 + [VMEM] * 7, sums(), [spread, TOTAL, PRODUC...  2.59 us
    unnamed x12, local copies, waits for them, and re-layouts  1.52 us
    pallas_call x1, Pallas kernels, grouped(): call(far_kernel, [SMEM] + [VMEM] * 6, (sums(), spread_shape()), [spread,...  1.4 us
    add x1, other arithmetic, grouped(): return near + received  0.7 us
    pallas_call x1, Pallas kernels, grouped(): call(merge_kernel, [VMEM], pltpu.SMEM((2 * SECTIONS, LANES), jnp.int32),...  0.69 us
    pallas_call x1, Pallas kernels, grouped(): call(far_last_kernel, [SMEM] + [VMEM] * 3, sums(), [TOTAL, PRODUCT_TABLE]...  0.67 us
  transfers between devices with their start and end apart: 8, of which 6 were waited for; matrix products, arithmetic and copies ran while one was open for 0% of the time, Pallas kernels for 19%

profile of v6, /device:TPU:0, one launch (start us, length us, event | category | flops | bytes accessed | tf_op | source)
XLA Modules:
  0.0 30.0 jit_solution(10602869475319298253)
XLA Ops:
  0.0 0.0 copy-start.5
  0.0 3.0 %collective-permute-start.3 = (f32[20,32,128]{2,1,0:T(8,128)}, f32[20,32,128]{2,1,0:T(8,128)S(1)}, u32[]{:S(2)}, u32[]{:S(2)}) collective-permute-start(f32[20,32,128]{2,1,0:T(8,128)} %bitcast.19), channel_id=1, source_target_pairs={{0,8},{1,9},{2,10},{3,11},{4,12},{5,13},{6,14},{7,15},{8,0},{9,1},... | collective-permute-start | bytes 983048 | tf_op jit(solution)/shard_map/ppermute | solution.py:299
  3.0 0.0 copy-start.3
  3.0 1.5 %collective-permute-start = (f32[256,128]{1,0:T(8,128)}, f32[256,128]{1,0:T(8,128)S(1)}, u32[]{:S(2)}, u32[]{:S(2)}) collective-permute-start(f32[256,128]{1,0:T(8,128)} %bitcast.11), channel_id=1, source_target_pairs={{0,2},{1,3},{2,0},{3,1},{4,6},{5,7},{6,4},{7,5},{8,10},{9,11},{10,... | collective-permute-start | bytes 393224 | tf_op jit(solution)/shard_map/ppermute | solution.py:299
  4.5 1.5 %collective-permute-start.2 = (f32[20,32,128]{2,1,0:T(8,128)}, f32[20,32,128]{2,1,0:T(8,128)S(1)}, u32[]{:S(2)}, u32[]{:S(2)}) collective-permute-start(f32[20,32,128]{2,1,0:T(8,128)} %bitcast.20), channel_id=1, source_target_pairs={{0,4},{1,5},{2,6},{3,7},{4,0},{5,1},{6,2},{7,3},{8,12},{9,13},{10,... | collective-permute-start | bytes 983048 | tf_op jit(solution)/shard_map/ppermute | solution.py:299
  6.0 0.0 copy-done.5
  6.0 0.0 copy-start.1
  6.0 0.0 copy-start.2
  6.0 0.1 copy.13.counts.n
  6.1 0.0 copy-done.3
  6.1 0.6 %copy-done.1 = s32[1,1,4,2,24]{4,3,2,1,0:T(2,128)S(1)} copy-done((s32[1,1,4,2,24]{4,3,2,1,0:T(2,128)S(1)}, s32[1,1,4,2,24]{4,3,2,1,0:T(2,128)}, u32[]{:S(2)}) %copy-start.1) | copy-done | bytes 792
  6.7 0.0 copy-done.2
  6.7 0.0 copy-start
  6.7 0.9 %copy-done = f32[1,2,4,4096]{3,2,1,0:T(4,128)S(1)} copy-done((f32[1,2,4,4096]{3,2,1,0:T(4,128)S(1)}, f32[1,2,4,4096]{3,2,1,0:T(4,128)}, u32[]{:S(2)}) %copy-start) | copy-done | bytes 131096
  7.7 0.0 copy-start.4
  7.7 0.3 stage.1
  7.9 0.3 collective-permute-done.beside
  8.2 2.5 %collective-permute-start.5 = (f32[264,128]{1,0:T(8,128)S(1)}, f32[264,128]{1,0:T(8,128)S(1)}, u32[]{:S(2)}, u32[]{:S(2)}) collective-permute-start(f32[264,128]{1,0:T(8,128)S(1)} %get-tuple-element.16), channel_id=1, source_target_pairs={{0,24},{1,25},{2,26},{3,27},{4,28},{5,29},{6,30},{7,31},{8,16},{9,... | collective-permute-start | bytes 405512 | tf_op jit(solution)/shard_map/ppermute | solution.py:299
  10.8 0.2 collective-permute-done.3.right_z
  10.9 1.7 %collective-permute-start.4 = (f32[20,32,128]{2,1,0:T(8,128)S(1)}, f32[20,32,128]{2,1,0:T(8,128)S(1)}, u32[]{:S(2)}, u32[]{:S(2)}) collective-permute-start(f32[20,32,128]{2,1,0:T(8,128)S(1)} %collective-permute-done.3.right_z), channel_id=1, source_target_pairs={{0,4},{1,5},{2,6},{3,7},{4,0},{5,1},{6,2},{7,3},{8,12},{9,13},{10,... | collective-permute-start | bytes 983048 | tf_op jit(solution)/shard_map/ppermute | solution.py:299
  12.6 3.5 %collective-permute-done.5.panel_ref.left_a = f32[264,128]{1,0:T(8,128)S(1)} collective-permute-done((f32[264,128]{1,0:T(8,128)S(1)}, f32[264,128]{1,0:T(8,128)S(1)}, u32[]{:S(2)}, u32[]{:S(2)}) %collective-permute-start.5) | collective-permute-done | bytes 135200 | tf_op jit(solution)/shard_map/ppermute | solution.py:299
  16.1 0.0 collective-permute-start.6
  16.1 0.5 %collective-permute-start.1 = (f32[256,128]{1,0:T(8,128)S(1)}, f32[256,128]{1,0:T(8,128)S(1)}, u32[]{:S(2)}, u32[]{:S(2)}) collective-permute-start(f32[256,128]{1,0:T(8,128)S(1)} %get-tuple-element.15.left_a), channel_id=1, source_target_pairs={{0,1},{1,0},{2,3},{3,2},{4,5},{5,4},{6,7},{7,6},{8,9},{9,8},{10,11... | collective-permute-start | bytes 393224 | tf_op jit(solution)/shard_map/ppermute | solution.py:299
  16.7 0.7 %merge.1.numbers = s32[8,128]{1,0:T(8,128)S(4)} custom-call(f32[264,128]{1,0:T(8,128)S(1)} %collective-permute-done.5.panel_ref.left_a), custom_call_target="tpu_custom_call" | custom-call | tf_op jit(solution)/shard_map/merge/pallas_call | solution.py:330
  17.3 0.0 collective-permute-done.2.right_y
  17.4 0.1 collective-permute-done.6.left_b
  17.5 0.0 copy-done.4
  17.5 1.4 %far_three.1 = (f32[12,32,128]{2,1,0:T(8,128)S(1)}, bf16[256,256]{1,0:T(8,128)(2,1)S(1)}) custom-call(s32[8,128]{1,0:T(8,128)S(4)} %merge.1.numbers, bf16[256,512]{1,0:T(8,128)(2,1)S(1)} %get-tuple-element.12.table, f32[264,128]{1,0:T(8,128)S(1)} %collective-permute-done.5.panel_ref.left_a, f32[264,128]{1,0:T(8,128)S(1)} %collective-permute-done.6.left_b, ...), custom_call_target="tpu_custom_call" | custom-call | flops 1000000000 | tf_op jit(solution)/shard_map/far_three/pallas_call | solution.py:334
  18.9 1.7 %collective-permute-done.4.right_d = f32[20,32,128]{2,1,0:T(8,128)S(1)} collective-permute-done((f32[20,32,128]{2,1,0:T(8,128)S(1)}, f32[20,32,128]{2,1,0:T(8,128)S(1)}, u32[]{:S(2)}, u32[]{:S(2)}) %collective-permute-start.4) | collective-permute-done | bytes 327712 | tf_op jit(solution)/shard_map/ppermute | solution.py:299
  20.6 0.7 %far_last.1 = f32[12,32,128]{2,1,0:T(8,128)S(1)} custom-call(s32[8,128]{1,0:T(8,128)S(4)} %merge.1.numbers, bf16[256,256]{1,0:T(8,128)(2,1)S(1)} %get-tuple-element.17.left, f32[20,32,128]{2,1,0:T(8,128)S(1)} %collective-permute-done.4.right_d, f32[12,32,128]{2,1,0:T(8,128)S(1)} %get-tuple-element.18.before), custom_call_target="tpu_custom_call" | custom-call | tf_op jit(solution)/shard_map/far_last/pallas_call | solution.py:337
  21.3 2.9 %collective-permute-start.7 = (f32[12,32,128]{2,1,0:T(8,128)S(1)}, f32[12,32,128]{2,1,0:T(8,128)S(1)}, u32[]{:S(2)}, u32[]{:S(2)}) collective-permute-start(f32[12,32,128]{2,1,0:T(8,128)S(1)} %far_last.1), channel_id=1, source_target_pairs={{0,24},{1,25},{2,26},{3,27},{4,28},{5,29},{6,30},{7,31},{8,16},{9,... | collective-permute-start | bytes 589832 | tf_op jit(solution)/shard_map/ppermute | solution.py:299
  24.2 0.0 collective-permute-done.1.left_b
  24.2 2.6 %near_all.1 = f32[12,32,128]{2,1,0:T(8,128)S(1)} custom-call(s32[4,2,24]{2,1,0:T(2,128)S(1)} %bitcast.14, s32[4,2,24]{2,1,0:T(2,128)S(1)} %bitcast.16, s32[4,2,24]{2,1,0:T(2,128)S(1)} %bitcast.18, s32[4,2]{1,0:T(4,128)S(1)} %copy.13.counts.n, bf16[256,512]{1,0:T(8,128)(2,1)S(1)} %get-tuple-element.12.table, f32[256,128]{1,0:T(8,128)S(1)} %get-tuple-element.15.left_a, ...), custom_call_target="tpu_custom_call" | custom-call | flops 3000000000 | tf_op jit(solution)/shard_map/near_all/pallas_call | solution.py:341
  26.8 2.5 %collective-permute-done.7 = f32[12,32,128]{2,1,0:T(8,128)S(1)} collective-permute-done((f32[12,32,128]{2,1,0:T(8,128)S(1)}, f32[12,32,128]{2,1,0:T(8,128)S(1)}, u32[]{:S(2)}, u32[]{:S(2)}) %collective-permute-start.7) | collective-permute-done | bytes 196640 | tf_op jit(solution)/shard_map/ppermute | solution.py:299
  29.3 0.7 %add.3 = f32[12,32,128]{2,1,0:T(8,128)} add(f32[12,32,128]{2,1,0:T(8,128)S(1)} %near_all.1, f32[12,32,128]{2,1,0:T(8,128)S(1)} %collective-permute-done.7) | non-fusion elementwise | flops 49152 | bytes 589824 | tf_op jit(solution)/shard_map/add | solution.py:344
  (1 shorter events, 0.0 us)
Async XLA Ops:
  0.0 6.0 %copy-start.5 = (s32[1,1,4,2]{2,3,1,0:T(2,128)S(1)}, s32[1,1,4,2]{2,3,1,0:T(2,128)}, u32[]{:S(2)}) copy-start(s32[1,1,4,2]{2,3,1,0:T(2,128)} %param.11) | copy-start | bytes 100
  0.0 10.9 %collective-permute-start.3 = (f32[20,32,128]{2,1,0:T(8,128)}, f32[20,32,128]{2,1,0:T(8,128)S(1)}, u32[]{:S(2)}, u32[]{:S(2)}) collective-permute-start(f32[20,32,128]{2,1,0:T(8,128)} %bitcast.19), channel_id=1, source_target_pairs={{0,8},{1,9},{2,10},{3,11},{4,12},{5,13},{6,14},{7,15},{8,0},{9,1},... | collective-permute-start | bytes 983048 | tf_op jit(solution)/shard_map/ppermute | solution.py:299
  3.0 3.1 %copy-start.3 = (s32[1,1,4,2,24]{4,3,2,1,0:T(2,128)S(1)}, s32[1,1,4,2,24]{4,3,2,1,0:T(2,128)}, u32[]{:S(2)}) copy-start(s32[1,1,4,2,24]{4,3,2,1,0:T(2,128)} %param.10) | copy-start | bytes 2308
  3.0 5.2 %collective-permute-start = (f32[256,128]{1,0:T(8,128)}, f32[256,128]{1,0:T(8,128)S(1)}, u32[]{:S(2)}, u32[]{:S(2)}) collective-permute-start(f32[256,128]{1,0:T(8,128)} %bitcast.11), channel_id=1, source_target_pairs={{0,2},{1,3},{2,0},{3,1},{4,6},{5,7},{6,4},{7,5},{8,10},{9,11},{10,... | collective-permute-start | bytes 393224 | tf_op jit(solution)/shard_map/ppermute | solution.py:299
  4.5 12.8 %collective-permute-start.2 = (f32[20,32,128]{2,1,0:T(8,128)}, f32[20,32,128]{2,1,0:T(8,128)S(1)}, u32[]{:S(2)}, u32[]{:S(2)}) collective-permute-start(f32[20,32,128]{2,1,0:T(8,128)} %bitcast.20), channel_id=1, source_target_pairs={{0,4},{1,5},{2,6},{3,7},{4,0},{5,1},{6,2},{7,3},{8,12},{9,13},{10,... | collective-permute-start | bytes 983048 | tf_op jit(solution)/shard_map/ppermute | solution.py:299
  6.0 0.7 %copy-start.1 = (s32[1,1,4,2,24]{4,3,2,1,0:T(2,128)S(1)}, s32[1,1,4,2,24]{4,3,2,1,0:T(2,128)}, u32[]{:S(2)}) copy-start(s32[1,1,4,2,24]{4,3,2,1,0:T(2,128)} %param.8) | copy-start | bytes 2308
  6.0 0.7 %copy-start.2 = (s32[1,1,4,2,24]{4,3,2,1,0:T(2,128)S(1)}, s32[1,1,4,2,24]{4,3,2,1,0:T(2,128)}, u32[]{:S(2)}) copy-start(s32[1,1,4,2,24]{4,3,2,1,0:T(2,128)} %param.9) | copy-start | bytes 2308
  6.7 0.9 %copy-start = (f32[1,2,4,4096]{3,2,1,0:T(4,128)S(1)}, f32[1,2,4,4096]{3,2,1,0:T(4,128)}, u32[]{:S(2)}) copy-start(f32[1,2,4,4096]{3,2,1,0:T(4,128)} %param.6) | copy-start | bytes 393220
  7.7 9.8 %copy-start.4 = (f32[1,1,20,4096]{3,1,2,0:T(1,128)S(1)}, f32[1,1,20,4096]{3,1,2,0:T(1,128)}, u32[]{:S(2)}) copy-start(f32[1,1,20,4096]{3,1,2,0:T(1,128)} %param.7) | copy-start | bytes 983044
  8.2 7.9 %collective-permute-start.5 = (f32[264,128]{1,0:T(8,128)S(1)}, f32[264,128]{1,0:T(8,128)S(1)}, u32[]{:S(2)}, u32[]{:S(2)}) collective-permute-start(f32[264,128]{1,0:T(8,128)S(1)} %get-tuple-element.16), channel_id=1, source_target_pairs={{0,24},{1,25},{2,26},{3,27},{4,28},{5,29},{6,30},{7,31},{8,16},{9,... | collective-permute-start | bytes 405512 | tf_op jit(solution)/shard_map/ppermute | solution.py:299
  10.9 9.7 %collective-permute-start.4 = (f32[20,32,128]{2,1,0:T(8,128)S(1)}, f32[20,32,128]{2,1,0:T(8,128)S(1)}, u32[]{:S(2)}, u32[]{:S(2)}) collective-permute-start(f32[20,32,128]{2,1,0:T(8,128)S(1)} %collective-permute-done.3.right_z), channel_id=1, source_target_pairs={{0,4},{1,5},{2,6},{3,7},{4,0},{5,1},{6,2},{7,3},{8,12},{9,13},{10,... | collective-permute-start | bytes 983048 | tf_op jit(solution)/shard_map/ppermute | solution.py:299
  16.1 1.4 %collective-permute-start.6 = (f32[264,128]{1,0:T(8,128)S(1)}, f32[264,128]{1,0:T(8,128)S(1)}, u32[]{:S(2)}, u32[]{:S(2)}) collective-permute-start(f32[264,128]{1,0:T(8,128)S(1)} %collective-permute-done.5.panel_ref.left_a), channel_id=1, source_target_pairs={{0,1},{1,0},{2,3},{3,2},{4,5},{5,4},{6,7},{7,6},{8,9},{9,8},{10,11... | collective-permute-start | bytes 405512 | tf_op jit(solution)/shard_map/ppermute | solution.py:299
  16.1 8.0 %collective-permute-start.1 = (f32[256,128]{1,0:T(8,128)S(1)}, f32[256,128]{1,0:T(8,128)S(1)}, u32[]{:S(2)}, u32[]{:S(2)}) collective-permute-start(f32[256,128]{1,0:T(8,128)S(1)} %get-tuple-element.15.left_a), channel_id=1, source_target_pairs={{0,1},{1,0},{2,3},{3,2},{4,5},{5,4},{6,7},{7,6},{8,9},{9,8},{10,11... | collective-permute-start | bytes 393224 | tf_op jit(solution)/shard_map/ppermute | solution.py:299
  21.3 8.0 %collective-permute-start.7 = (f32[12,32,128]{2,1,0:T(8,128)S(1)}, f32[12,32,128]{2,1,0:T(8,128)S(1)}, u32[]{:S(2)}, u32[]{:S(2)}) collective-permute-start(f32[12,32,128]{2,1,0:T(8,128)S(1)} %far_last.1), channel_id=1, source_target_pairs={{0,24},{1,25},{2,26},{3,27},{4,28},{5,29},{6,30},{7,31},{8,16},{9,... | collective-permute-start | bytes 589832 | tf_op jit(solution)/shard_map/ppermute | solution.py:299

commit v7 on v4

--- a/solution.py
+++ b/solution.py
@@ -18,7 +18,8 @@
 LEFT_ROWS = 2 * LEFT_SLOTS * HALF
 LIST_ROWS = 2 * SECTIONS
 LIST_LANES = LANES // 4
-ODD_SINKS = 16
+SINK_BITS = 5
+ODD_SINKS = 1 << (SINK_BITS - 1)
 AXES = ("row", "col")
 MIB = 1 << 20
 
@@ -118,7 +119,7 @@
 
     def entry(self, section, half, p):
         number = self.numbers[section * 2 + half, p]
-        return number // (2 * ODD_SINKS), number % (2 * ODD_SINKS)
+        return number >> SINK_BITS, number & (2 * ODD_SINKS - 1)
 
 
 def merge_kernel(panel_ref, numbers, whole, semaphore):
@@ -211,10 +212,10 @@
 ):
     lists = SentLists(numbers)
     place = Place()
-    start_total(total, before)
+    start_total(total)
     all_products(left[...], right_d, products)
     add_listed(total, products, lists, place.section(1, True), 1 - place.half)
-    out[...] = whole_total(total)
+    out[...] = before[...] + whole_total(total)
 
 
 def near_kernel(

time: 30.1 us -> 30.1 us (level)
  Pallas kernels: 6.06 us -> 5.75 us
    ppermute x8, waiting for transfers between devices: 7.89 us -> 8.19 us  [send(): return lax.ppermute(value, AXES, where)]
  transfers between devices with their start and end apart: 8 -> 8, of which waited for: 6 -> 6; matrix products, arithmetic and copies ran while one was open for 0% -> 0% of each run, Pallas kernels for 20% -> 19%
where the time goes in v7:
time: 30.1 us; the launch traced here: 30 us
  starting transfers between devices  13.6 us (45%)
  waiting for transfers between devices  8.19 us (27%)
  Pallas kernels  5.75 us (19%)
  local copies, waits for them, and re-layouts  1.61 us (5%)
  other arithmetic  0.7 us (2%)
    ppermute x8, starting transfers between devices, send(): return lax.ppermute(value, AXES, where)  13.6 us
    ppermute x8, waiting for transfers between devices, send(): return lax.ppermute(value, AXES, where)  8.19 us
    pallas_call x1, Pallas kernels, grouped(): call(near_kernel, [SMEM] * 4 + [VMEM] * 6, sums(), [spread, TOTAL, PRODUC...  2.73 us
    unnamed x12, local copies, waits for them, and re-layouts  1.52 us
    pallas_call x1, Pallas kernels, grouped(): call(far_kernel, [SMEM] + [VMEM] * 5, (sums(), spread_shape()), [spread,...  1.42 us
    add x1, other arithmetic, grouped(): return near + received  0.7 us
    pallas_call x1, Pallas kernels, grouped(): call(merge_kernel, [VMEM], pltpu.SMEM((2 * SECTIONS, LANES), jnp.int32),...  0.69 us
    pallas_call x1, Pallas kernels, grouped(): call(far_last_kernel, [SMEM] + [VMEM] * 3, sums(), [TOTAL, PRODUCT_TABLE]...  0.66 us
  transfers between devices with their start and end apart: 8, of which 6 were waited for; matrix products, arithmetic and copies ran while one was open for 0% of the time, Pallas kernels for 19%

profile of v7, /device:TPU:0, one launch (start us, length us, event | category | flops | bytes accessed | tf_op | source)
XLA Modules:
  0.0 30.0 jit_solution(13037112879656589733)
XLA Ops:
  0.0 0.0 copy-start.5
  0.0 3.0 %collective-permute-start.3 = (f32[20,32,128]{2,1,0:T(8,128)}, f32[20,32,128]{2,1,0:T(8,128)S(1)}, u32[]{:S(2)}, u32[]{:S(2)}) collective-permute-start(f32[20,32,128]{2,1,0:T(8,128)} %bitcast.19), channel_id=1, source_target_pairs={{0,8},{1,9},{2,10},{3,11},{4,12},{5,13},{6,14},{7,15},{8,0},{9,1},... | collective-permute-start | bytes 983048 | tf_op jit(solution)/shard_map/ppermute | solution.py:297
  3.0 0.0 copy-start.3
  3.0 1.5 %collective-permute-start = (f32[256,128]{1,0:T(8,128)}, f32[256,128]{1,0:T(8,128)S(1)}, u32[]{:S(2)}, u32[]{:S(2)}) collective-permute-start(f32[256,128]{1,0:T(8,128)} %bitcast.11), channel_id=1, source_target_pairs={{0,2},{1,3},{2,0},{3,1},{4,6},{5,7},{6,4},{7,5},{8,10},{9,11},{10,... | collective-permute-start | bytes 393224 | tf_op jit(solution)/shard_map/ppermute | solution.py:297
  4.5 1.5 %collective-permute-start.2 = (f32[20,32,128]{2,1,0:T(8,128)}, f32[20,32,128]{2,1,0:T(8,128)S(1)}, u32[]{:S(2)}, u32[]{:S(2)}) collective-permute-start(f32[20,32,128]{2,1,0:T(8,128)} %bitcast.20), channel_id=1, source_target_pairs={{0,4},{1,5},{2,6},{3,7},{4,0},{5,1},{6,2},{7,3},{8,12},{9,13},{10,... | collective-permute-start | bytes 983048 | tf_op jit(solution)/shard_map/ppermute | solution.py:297
  6.0 0.0 copy-done.5
  6.0 0.0 copy-start.1
  6.0 0.0 copy-start.2
  6.0 0.1 copy.13.counts.n
  6.1 0.0 copy-done.3
  6.1 0.6 %copy-done.1 = s32[1,1,4,2,24]{4,3,2,1,0:T(2,128)S(1)} copy-done((s32[1,1,4,2,24]{4,3,2,1,0:T(2,128)S(1)}, s32[1,1,4,2,24]{4,3,2,1,0:T(2,128)}, u32[]{:S(2)}) %copy-start.1) | copy-done | bytes 792
  6.7 0.0 copy-done.2
  6.7 0.0 copy-start
  6.7 0.9 %copy-done = f32[1,2,4,4096]{3,2,1,0:T(4,128)S(1)} copy-done((f32[1,2,4,4096]{3,2,1,0:T(4,128)S(1)}, f32[1,2,4,4096]{3,2,1,0:T(4,128)}, u32[]{:S(2)}) %copy-start) | copy-done | bytes 131096
  7.7 0.0 copy-start.4
  7.7 0.2 stage.1
  7.9 0.3 %collective-permute-done.beside = f32[256,128]{1,0:T(8,128)S(1)} collective-permute-done((f32[256,128]{1,0:T(8,128)}, f32[256,128]{1,0:T(8,128)S(1)}, u32[]{:S(2)}, u32[]{:S(2)}) %collective-permute-start) | collective-permute-done | bytes 131104 | tf_op jit(solution)/shard_map/ppermute | solution.py:297
  8.2 2.5 %collective-permute-start.5 = (f32[264,128]{1,0:T(8,128)S(1)}, f32[264,128]{1,0:T(8,128)S(1)}, u32[]{:S(2)}, u32[]{:S(2)}) collective-permute-start(f32[264,128]{1,0:T(8,128)S(1)} %get-tuple-element.14), channel_id=1, source_target_pairs={{0,24},{1,25},{2,26},{3,27},{4,28},{5,29},{6,30},{7,31},{8,16},{9,... | collective-permute-start | bytes 405512 | tf_op jit(solution)/shard_map/ppermute | solution.py:297
  10.8 0.2 collective-permute-done.3.right_z
  10.9 1.7 %collective-permute-start.4 = (f32[20,32,128]{2,1,0:T(8,128)S(1)}, f32[20,32,128]{2,1,0:T(8,128)S(1)}, u32[]{:S(2)}, u32[]{:S(2)}) collective-permute-start(f32[20,32,128]{2,1,0:T(8,128)S(1)} %collective-permute-done.3.right_z), channel_id=1, source_target_pairs={{0,4},{1,5},{2,6},{3,7},{4,0},{5,1},{6,2},{7,3},{8,12},{9,13},{10,... | collective-permute-start | bytes 983048 | tf_op jit(solution)/shard_map/ppermute | solution.py:297
  12.6 3.5 %collective-permute-done.5.panel_ref.left_a = f32[264,128]{1,0:T(8,128)S(1)} collective-permute-done((f32[264,128]{1,0:T(8,128)S(1)}, f32[264,128]{1,0:T(8,128)S(1)}, u32[]{:S(2)}, u32[]{:S(2)}) %collective-permute-start.5) | collective-permute-done | bytes 135200 | tf_op jit(solution)/shard_map/ppermute | solution.py:297
  16.1 0.0 collective-permute-start.6
  16.1 0.5 %collective-permute-start.1 = (f32[256,128]{1,0:T(8,128)S(1)}, f32[256,128]{1,0:T(8,128)S(1)}, u32[]{:S(2)}, u32[]{:S(2)}) collective-permute-start(f32[256,128]{1,0:T(8,128)S(1)} %get-tuple-element.13.left_a), channel_id=1, source_target_pairs={{0,1},{1,0},{2,3},{3,2},{4,5},{5,4},{6,7},{7,6},{8,9},{9,8},{10,11... | collective-permute-start | bytes 393224 | tf_op jit(solution)/shard_map/ppermute | solution.py:297
  16.7 0.7 %merge.1.numbers = s32[8,128]{1,0:T(8,128)S(4)} custom-call(f32[264,128]{1,0:T(8,128)S(1)} %collective-permute-done.5.panel_ref.left_a), custom_call_target="tpu_custom_call" | custom-call | tf_op jit(solution)/shard_map/merge/pallas_call | solution.py:327
  17.3 0.0 collective-permute-done.2.right_y
  17.4 0.1 collective-permute-done.6.left_b
  17.5 0.0 copy-done.4
  17.5 1.4 %far_three.1 = (f32[12,32,128]{2,1,0:T(8,128)S(1)}, bf16[256,256]{1,0:T(8,128)(2,1)S(1)}) custom-call(s32[8,128]{1,0:T(8,128)S(4)} %merge.1.numbers, f32[264,128]{1,0:T(8,128)S(1)} %collective-permute-done.5.panel_ref.left_a, f32[264,128]{1,0:T(8,128)S(1)} %collective-permute-done.6.left_b, f32[20,32,128]{2,1,0:T(8,128)S(1)} %bitcast.21, ...), custom_call_target="tpu_custom_call" | custom-call | flops 1000000000 | tf_op jit(solution)/shard_map/far_three/pallas_call | solution.py:331
  18.9 1.7 %collective-permute-done.4.right_d = f32[20,32,128]{2,1,0:T(8,128)S(1)} collective-permute-done((f32[20,32,128]{2,1,0:T(8,128)S(1)}, f32[20,32,128]{2,1,0:T(8,128)S(1)}, u32[]{:S(2)}, u32[]{:S(2)}) %collective-permute-start.4) | collective-permute-done | bytes 327712 | tf_op jit(solution)/shard_map/ppermute | solution.py:297
  20.6 0.7 %far_last.1 = f32[12,32,128]{2,1,0:T(8,128)S(1)} custom-call(s32[8,128]{1,0:T(8,128)S(4)} %merge.1.numbers, bf16[256,256]{1,0:T(8,128)(2,1)S(1)} %get-tuple-element.15.left, f32[20,32,128]{2,1,0:T(8,128)S(1)} %collective-permute-done.4.right_d, f32[12,32,128]{2,1,0:T(8,128)S(1)} %get-tuple-element.16.before), custom_call_target="tpu_custom_call" | custom-call | flops 1000000000 | tf_op jit(solution)/shard_map/far_last/pallas_call | solution.py:334
  21.3 2.9 %collective-permute-start.7 = (f32[12,32,128]{2,1,0:T(8,128)S(1)}, f32[12,32,128]{2,1,0:T(8,128)S(1)}, u32[]{:S(2)}, u32[]{:S(2)}) collective-permute-start(f32[12,32,128]{2,1,0:T(8,128)S(1)} %far_last.1), channel_id=1, source_target_pairs={{0,24},{1,25},{2,26},{3,27},{4,28},{5,29},{6,30},{7,31},{8,16},{9,... | collective-permute-start | bytes 589832 | tf_op jit(solution)/shard_map/ppermute | solution.py:297
  24.2 0.0 collective-permute-done.1.left_b
  24.2 2.7 %near_all.1 = f32[12,32,128]{2,1,0:T(8,128)S(1)} custom-call(s32[4,2,24]{2,1,0:T(2,128)S(1)} %bitcast.14, s32[4,2,24]{2,1,0:T(2,128)S(1)} %bitcast.16, s32[4,2,24]{2,1,0:T(2,128)S(1)} %bitcast.18, s32[4,2]{1,0:T(4,128)S(1)} %copy.13.counts.n, f32[256,128]{1,0:T(8,128)S(1)} %get-tuple-element.13.left_a, f32[256,128]{1,0:T(8,128)S(1)} %collective-permute-done.1.left_b, ...), custom_call_target="tpu_custom_call" | custom-call | flops 3000000000 | tf_op jit(solution)/shard_map/near_all/pallas_call | solution.py:338
  26.9 2.3 %collective-permute-done.7 = f32[12,32,128]{2,1,0:T(8,128)S(1)} collective-permute-done((f32[12,32,128]{2,1,0:T(8,128)S(1)}, f32[12,32,128]{2,1,0:T(8,128)S(1)}, u32[]{:S(2)}, u32[]{:S(2)}) %collective-permute-start.7) | collective-permute-done | bytes 196640 | tf_op jit(solution)/shard_map/ppermute | solution.py:297
  29.3 0.7 %add.3 = f32[12,32,128]{2,1,0:T(8,128)} add(f32[12,32,128]{2,1,0:T(8,128)S(1)} %near_all.1, f32[12,32,128]{2,1,0:T(8,128)S(1)} %collective-permute-done.7) | non-fusion elementwise | flops 49152 | bytes 589824 | tf_op jit(solution)/shard_map/add | solution.py:341
  (1 shorter events, 0.0 us)
Async XLA Ops:
  0.0 6.0 %copy-start.5 = (s32[1,1,4,2]{2,3,1,0:T(2,128)S(1)}, s32[1,1,4,2]{2,3,1,0:T(2,128)}, u32[]{:S(2)}) copy-start(s32[1,1,4,2]{2,3,1,0:T(2,128)} %param.11) | copy-start | bytes 100
  0.0 10.9 %collective-permute-start.3 = (f32[20,32,128]{2,1,0:T(8,128)}, f32[20,32,128]{2,1,0:T(8,128)S(1)}, u32[]{:S(2)}, u32[]{:S(2)}) collective-permute-start(f32[20,32,128]{2,1,0:T(8,128)} %bitcast.19), channel_id=1, source_target_pairs={{0,8},{1,9},{2,10},{3,11},{4,12},{5,13},{6,14},{7,15},{8,0},{9,1},... | collective-permute-start | bytes 983048 | tf_op jit(solution)/shard_map/ppermute | solution.py:297
  3.0 3.1 %copy-start.3 = (s32[1,1,4,2,24]{4,3,2,1,0:T(2,128)S(1)}, s32[1,1,4,2,24]{4,3,2,1,0:T(2,128)}, u32[]{:S(2)}) copy-start(s32[1,1,4,2,24]{4,3,2,1,0:T(2,128)} %param.10) | copy-start | bytes 2308
  3.0 5.2 %collective-permute-start = (f32[256,128]{1,0:T(8,128)}, f32[256,128]{1,0:T(8,128)S(1)}, u32[]{:S(2)}, u32[]{:S(2)}) collective-permute-start(f32[256,128]{1,0:T(8,128)} %bitcast.11), channel_id=1, source_target_pairs={{0,2},{1,3},{2,0},{3,1},{4,6},{5,7},{6,4},{7,5},{8,10},{9,11},{10,... | collective-permute-start | bytes 393224 | tf_op jit(solution)/shard_map/ppermute | solution.py:297
  4.5 12.8 %collective-permute-start.2 = (f32[20,32,128]{2,1,0:T(8,128)}, f32[20,32,128]{2,1,0:T(8,128)S(1)}, u32[]{:S(2)}, u32[]{:S(2)}) collective-permute-start(f32[20,32,128]{2,1,0:T(8,128)} %bitcast.20), channel_id=1, source_target_pairs={{0,4},{1,5},{2,6},{3,7},{4,0},{5,1},{6,2},{7,3},{8,12},{9,13},{10,... | collective-permute-start | bytes 983048 | tf_op jit(solution)/shard_map/ppermute | solution.py:297
  6.0 0.7 %copy-start.1 = (s32[1,1,4,2,24]{4,3,2,1,0:T(2,128)S(1)}, s32[1,1,4,2,24]{4,3,2,1,0:T(2,128)}, u32[]{:S(2)}) copy-start(s32[1,1,4,2,24]{4,3,2,1,0:T(2,128)} %param.8) | copy-start | bytes 2308
  6.0 0.7 %copy-start.2 = (s32[1,1,4,2,24]{4,3,2,1,0:T(2,128)S(1)}, s32[1,1,4,2,24]{4,3,2,1,0:T(2,128)}, u32[]{:S(2)}) copy-start(s32[1,1,4,2,24]{4,3,2,1,0:T(2,128)} %param.9) | copy-start | bytes 2308
  6.7 0.9 %copy-start = (f32[1,2,4,4096]{3,2,1,0:T(4,128)S(1)}, f32[1,2,4,4096]{3,2,1,0:T(4,128)}, u32[]{:S(2)}) copy-start(f32[1,2,4,4096]{3,2,1,0:T(4,128)} %param.6) | copy-start | bytes 393220
  7.7 9.8 %copy-start.4 = (f32[1,1,20,4096]{3,1,2,0:T(1,128)S(1)}, f32[1,1,20,4096]{3,1,2,0:T(1,128)}, u32[]{:S(2)}) copy-start(f32[1,1,20,4096]{3,1,2,0:T(1,128)} %param.7) | copy-start | bytes 983044
  8.2 7.9 %collective-permute-start.5 = (f32[264,128]{1,0:T(8,128)S(1)}, f32[264,128]{1,0:T(8,128)S(1)}, u32[]{:S(2)}, u32[]{:S(2)}) collective-permute-start(f32[264,128]{1,0:T(8,128)S(1)} %get-tuple-element.14), channel_id=1, source_target_pairs={{0,24},{1,25},{2,26},{3,27},{4,28},{5,29},{6,30},{7,31},{8,16},{9,... | collective-permute-start | bytes 405512 | tf_op jit(solution)/shard_map/ppermute | solution.py:297
  10.9 9.7 %collective-permute-start.4 = (f32[20,32,128]{2,1,0:T(8,128)S(1)}, f32[20,32,128]{2,1,0:T(8,128)S(1)}, u32[]{:S(2)}, u32[]{:S(2)}) collective-permute-start(f32[20,32,128]{2,1,0:T(8,128)S(1)} %collective-permute-done.3.right_z), channel_id=1, source_target_pairs={{0,4},{1,5},{2,6},{3,7},{4,0},{5,1},{6,2},{7,3},{8,12},{9,13},{10,... | collective-permute-start | bytes 983048 | tf_op jit(solution)/shard_map/ppermute | solution.py:297
  16.1 1.4 %collective-permute-start.6 = (f32[264,128]{1,0:T(8,128)S(1)}, f32[264,128]{1,0:T(8,128)S(1)}, u32[]{:S(2)}, u32[]{:S(2)}) collective-permute-start(f32[264,128]{1,0:T(8,128)S(1)} %collective-permute-done.5.panel_ref.left_a), channel_id=1, source_target_pairs={{0,1},{1,0},{2,3},{3,2},{4,5},{5,4},{6,7},{7,6},{8,9},{9,8},{10,11... | collective-permute-start | bytes 405512 | tf_op jit(solution)/shard_map/ppermute | solution.py:297
  16.1 8.0 %collective-permute-start.1 = (f32[256,128]{1,0:T(8,128)S(1)}, f32[256,128]{1,0:T(8,128)S(1)}, u32[]{:S(2)}, u32[]{:S(2)}) collective-permute-start(f32[256,128]{1,0:T(8,128)S(1)} %get-tuple-element.13.left_a), channel_id=1, source_target_pairs={{0,1},{1,0},{2,3},{3,2},{4,5},{5,4},{6,7},{7,6},{8,9},{9,8},{10,11... | collective-permute-start | bytes 393224 | tf_op jit(solution)/shard_map/ppermute | solution.py:297
  21.3 7.9 %collective-permute-start.7 = (f32[12,32,128]{2,1,0:T(8,128)S(1)}, f32[12,32,128]{2,1,0:T(8,128)S(1)}, u32[]{:S(2)}, u32[]{:S(2)}) collective-permute-start(f32[12,32,128]{2,1,0:T(8,128)S(1)} %far_last.1), channel_id=1, source_target_pairs={{0,24},{1,25},{2,26},{3,27},{4,28},{5,29},{6,30},{7,31},{8,16},{9,... | collective-permute-start | bytes 589832 | tf_op jit(solution)/shard_map/ppermute | solution.py:297
